TPU v7x, 256 devices: a whole 4x4x8 slice. The times are simulated.
256 devices in a mesh: batch: 16 (over x, z_lo), centre: 16 (over y, z_hi, core).
Axes of the slice: x: 4, y: 4, z: 8 (z_hi: 2, z_lo: 4; z = z_hi * 4 + z_lo), core: 2. Of those that a mesh axis runs over, the one named last changes fastest.
Arguments:
- batch_features: float32 [8192, 768], P(('batch', 'centre')), may hold values from -1 to 1
- centre_features: float32 [8192, 768], P(('centre', 'batch')), may hold values from -1 to 1
- targets: float32 [8192, 512], P(('batch', 'centre')), may hold values from -6 to 6
- weights: float32 [8192, 512], P(('centre', 'batch')), may hold values from -0.5 to 0.5
Outputs:
- residual: float32 [8192, 512], P(('batch', 'centre'))
- update: float32 [8192, 512], P(('centre', 'batch'))
All inputs are finite; a program needn't handle non-finite values.
Results may differ from a plain program's by a relative error of at most 0.000061.
Values sent between devices are 32-bit elements; how exact they have to be, the bound alone decides.
No kernel may reach another device: no remote copies, remote signals or barrier semaphores. Data moves between devices by JAX's collectives and lax.ppermute only.
A program may use at most 64 MiB of HBM per device.

v0:
```python
import math

import jax
import jax.numpy as jnp
from jax import lax
from jax.sharding import PartitionSpec as P

length_scale = 0.5
softening = 0.01


def spread(value, axis, source):
    kept = jnp.where(lax.axis_index(axis) == source, value, 0).astype(value.dtype)
    return lax.psum(kept, axis)


def kernel_matrix(left_rows, right_rows):
    left_norms = jnp.sum(left_rows * left_rows, axis=1)
    right_norms = jnp.sum(right_rows * right_rows, axis=1)
    inner = lax.dot_general(
        left_rows,
        right_rows,
        (((1,), (1,)), ((), ())),
        precision=lax.Precision.HIGHEST,
        preferred_element_type=jnp.float32,
    )
    squared = left_norms[:, None] + right_norms[None, :] - 2.0 * inner
    return jnp.exp(-jnp.sqrt(squared + softening) / length_scale)


def shards(batch_features, centre_features, targets, weights):
    batch_count = lax.axis_size("batch")
    centre_count = lax.axis_size("centre")
    batch_place = lax.axis_index("batch")
    own_rows = targets.shape[0]
    batch_rows = own_rows * centre_count
    centre_rows = centre_features.shape[0] * batch_count
    group_ratio = batch_count // centre_count
    source_index = batch_place // group_ratio
    batch_full = lax.all_gather(batch_features, "centre", axis=0, tiled=True)
    centre_full = lax.all_gather(centre_features, "batch", axis=0, tiled=True)
    weight_full = lax.all_gather(weights, "batch", axis=0, tiled=True)
    far_features = spread(centre_full, "centre", source_index)
    kernel_tile = kernel_matrix(batch_full, centre_full)
    partial_pred = jnp.dot(
        kernel_tile,
        weight_full,
        precision=lax.Precision.HIGHEST,
        preferred_element_type=jnp.float32,
    )
    pred_share = lax.psum_scatter(partial_pred, "centre", scatter_dimension=0, tiled=True)
    residual = pred_share - targets
    residual_full = lax.all_gather(residual, "centre", axis=0, tiled=True)
    partial_grad = lax.dot_general(
        kernel_tile,
        residual_full,
        (((0,), (0,)), ((), ())),
        precision=lax.Precision.HIGHEST,
        preferred_element_type=jnp.float32,
    )
    grad_share = lax.psum_scatter(partial_grad, "batch", scatter_dimension=0, tiled=True)
    grad_full = lax.all_gather(grad_share, "batch", axis=0, tiled=True)
    far_grads = spread(grad_full, "centre", source_index)
    centre_tile = kernel_matrix(centre_full, far_features)
    row_sums = lax.psum(jnp.sum(centre_tile, axis=1), "batch")
    largest = lax.pmax(jnp.max(row_sums), "centre")
    partial_product = jnp.dot(
        centre_tile, far_grads, precision=lax.Precision.HIGHEST, preferred_element_type=jnp.float32
    )
    product_share = lax.psum_scatter(partial_product, "batch", scatter_dimension=0, tiled=True)
    step_size = 1.0 / largest
    theta = 2.0 * step_size * grad_share - step_size * step_size * product_share
    output_scale = centre_rows * centre_count / math.sqrt(batch_rows * batch_count)
    return (residual, theta * output_scale)


def solution(mesh):
    in_specs = (
        P(("batch", "centre"), None),
        P(("centre", "batch"), None),
        P(("batch", "centre"), None),
        P(("centre", "batch"), None),
    )
    out_specs = (P(("batch", "centre"), None), P(("centre", "batch"), None))
    return jax.shard_map(shards, mesh=mesh, in_specs=in_specs, out_specs=out_specs, check_vma=False)
```

profile of v0, /device:TPU:1, one launch (start us, length us, event | category | flops | bytes accessed | tf_op | source)
XLA Modules:
  0.0 854.8 jit_solution(6126012840173237868)
XLA Ops:
  7.2 0.7 all-gather.6.cloned.1.call-update
  7.9 0.7 all-gather.8.cloned.1.call-update
  8.7 0.7 all-gather.10.cloned.1.call-update
  9.4 64.8 %all-gather.6.cloned.1.call-done = f32[512,768]{1,0:T(8,128)} async-done(((f32[32,768]{1,0:T(8,128)}), f32[512,768]{1,0:T(8,128)}) %all-gather.6.cloned.1.call-update) | async-done | bytes 1572880 | tf_op jit(solution)/shard_map/all_gather | solution.py:40
  74.2 1.6 multiply_reduce_fusion.2
  75.8 71.2 %all-gather.8.cloned.1.call-done = f32[512,768]{1,0:T(8,128)} async-done(((f32[32,768]{1,0:T(8,128)}), f32[512,768]{1,0:T(8,128)}) %all-gather.8.cloned.1.call-update) | async-done | bytes 1572880 | tf_op jit(solution)/shard_map/all_gather | solution.py:41
  147.1 2.9 broadcast_select_fusion
  149.9 3.1 fusion.7
  153.1 76.3 %all-gather.10.cloned.1.call-done = f32[512,512]{1,0:T(8,128)} async-done(((f32[32,512]{1,0:T(8,128)}), f32[512,512]{1,0:T(8,128)}) %all-gather.10.cloned.1.call-update) | async-done | bytes 1048592 | tf_op jit(solution)/shard_map/all_gather | solution.py:42
  229.3 4.0 fusion.14
  233.4 86.4 %reduce-scatter.4.cloned.1.call-done = f32[32,512]{1,0:T(8,128)} async-done(((f32[512,512]{1,0:T(8,128)}), f32[32,512]{1,0:T(8,128)}) %reduce-scatter.4.cloned.1.call-update) | async-done | bytes 65552 | tf_op jit(solution)/shard_map/reduce_scatter | solution.py:51
  319.9 1.5 sub.15
  321.4 56.2 %all-gather.12.cloned.1.call-done = f32[512,512]{1,0:T(8,128)} async-done(((f32[32,512]{1,0:T(8,128)}), f32[512,512]{1,0:T(8,128)}) %all-gather.12.cloned.1.call-update) | async-done | bytes 1048592 | tf_op jit(solution)/shard_map/all_gather | solution.py:53
  377.6 4.0 fusion.15
  381.7 71.6 %reduce-scatter.6.cloned.1.call-done = f32[32,512]{1,0:T(8,128)} async-done(((f32[512,512]{1,0:T(8,128)}), f32[32,512]{1,0:T(8,128)}) %reduce-scatter.6.cloned.1.call-update) | async-done | bytes 65552 | tf_op jit(solution)/shard_map/reduce_scatter | solution.py:61
  453.4 80.6 %all-gather.14.cloned.1.call-done = f32[512,512]{1,0:T(8,128)} async-done(((f32[32,512]{1,0:T(8,128)}), f32[512,512]{1,0:T(8,128)}) %all-gather.14.cloned.1.call-update) | async-done | bytes 1048592 | tf_op jit(solution)/shard_map/all_gather | solution.py:62
  533.9 1.1 broadcast_select_fusion.1
  535.3 217.9 %all-reduce.3.cloned.1.call-done = (f32[512,768]{1,0:T(8,128)}, f32[512,512]{1,0:T(8,128)}) async-done(((f32[512,768]{1,0:T(8,128)}, f32[512,512]{1,0:T(8,128)}), (f32[512,768]{1,0:T(8,128)}, f32[512,512]{1,0:T(8,128)})) %all-reduce.3.cloned.1.call-update) | async-done | bytes 2621456 | tf_op jit(solution)/shard_map/psum | solution.py:14
  753.2 1.7 multiply_reduce_fusion
  755.0 3.2 fusion.13
  758.3 2.8 fusion.16
  761.1 33.5 %psum.22 = f32[512]{0:T(512)S(1)} all-reduce(f32[512]{0:T(512)S(1)} %get-tuple-element.6), channel_id=1, replica_groups=mesh['batch'=16,'centre'=16] {'batch'}, use_global_device_ids=true, to_apply=%region_6.7 | all-reduce | flops 512 | bytes 4096 | tf_op jit(solution)/shard_map/psum | solution.py:65
  795.2 50.9 %pmax.7 = f32[]{:T(128)} all-reduce(f32[]{:T(128)} %reduce_max.9), channel_id=1, replica_groups=mesh['batch'=16,'centre'=16] {'centre'}, use_global_device_ids=true, to_apply=%region_8.9 | all-reduce | flops 1 | bytes 8 | tf_op jit(solution)/shard_map/pmax | solution.py:66
  846.8 1.5 subtract_multiply_fusion
  (29 shorter events, 1.5 us)
Async XLA Ops:
  7.2 67.1 %all-gather.6.cloned.1.call-start = ((), (), s32[]{:S(2)}) async-start(), calls=%async_computation.3 | async-start | bytes 1671168 | tf_op jit(solution)/shard_map/all_gather | solution.py:40
  7.9 139.1 %all-gather.8.cloned.1.call-start = ((), (), s32[]{:S(2)}) async-start(), calls=%async_computation.4 | async-start | bytes 1671168 | tf_op jit(solution)/shard_map/all_gather | solution.py:41
  8.6 220.7 %all-gather.10.cloned.1.call-start = ((), (), s32[]{:S(2)}) async-start(), calls=%async_computation.5 | async-start | bytes 1114112 | tf_op jit(solution)/shard_map/all_gather | solution.py:42
  9.4 310.5 %reduce-scatter.4.cloned.1.call-start = ((), (), s32[]{:S(2)}) async-start(), calls=%async_computation.6 | async-start | bytes 1114112 | tf_op jit(solution)/shard_map/reduce_scatter | solution.py:51
  147.0 2.9 copy-start
  147.0 2.9 copy-start.1
  153.0 166.8 %copy-start.5 = (f32[32,512]{1,0:T(8,128)S(1)}, f32[32,512]{1,0:T(8,128)}, u32[]{:S(2)}) copy-start(f32[32,512]{1,0:T(8,128)} %param.6) | copy-start | bytes 196612
  233.4 144.2 %all-gather.12.cloned.1.call-start = ((), (), s32[]{:S(2)}) async-start(), calls=%async_computation.7 | async-start | bytes 1114112 | tf_op jit(solution)/shard_map/all_gather | solution.py:53
  321.4 131.9 %reduce-scatter.6.cloned.1.call-start = ((), (), s32[]{:S(2)}) async-start(), calls=%async_computation.8 | async-start | bytes 1114112 | tf_op jit(solution)/shard_map/reduce_scatter | solution.py:61
  381.7 152.3 %all-gather.14.cloned.1.call-start = ((), (), s32[]{:S(2)}) async-start(), calls=%async_computation.9 | async-start | bytes 1114112 | tf_op jit(solution)/shard_map/all_gather | solution.py:62
  453.3 299.8 %all-reduce.3.cloned.1.call-start = ((), (), s32[]{:S(2)}) async-start(), calls=%async_computation.11 | async-start | bytes 5242880 | tf_op jit(solution)/shard_map/psum | solution.py:14
  535.0 311.8 %reduce-scatter.8.cloned.1.call-start = ((), (), s32[]{:S(2)}) async-start(), calls=%async_computation.10 | async-start | bytes 1114112 | tf_op jit(solution)/shard_map/reduce_scatter | solution.py:70
  753.2 1.9 copy-start.2
  755.0 3.2 copy-start.3
  758.3 88.5 %copy-start.4 = (f32[32,512]{1,0:T(8,128)S(1)}, f32[32,512]{1,0:T(8,128)}, u32[]{:S(2)}) copy-start(f32[32,512]{1,0:T(8,128)} %reduce-scatter.6.cloned.1.call-done) | copy-start | bytes 196612
Sparse Core Ops, SparseCore 0:
  10.7 63.5 all-gather.5
  76.0 70.9 all-gather.7
  148.8 80.4 all-gather.9
  233.5 86.3 reduce-scatter.3
  323.3 54.2 all-gather.11
  381.8 71.4 reduce-scatter.5
  455.1 78.7 all-gather.13
  536.6 216.4 all-reduce.2
  761.3 77.7 reduce-scatter.7
where the time goes:
time: 858 us; the launch traced here: 855 us
  waiting for transfers between devices  727 us (85%)
  blocking collectives  84.3 us (10%)
  matrix products  17.2 us (2%)
  between operations  14.6 us (2%)
  other arithmetic  10.8 us (1%)
    psum x1, waiting for transfers between devices, spread(): return lax.psum(kept, axis)  218 us
    reduce_scatter x1, waiting for transfers between devices, shards(): lax.psum_scatter(partial_pred, 'centre', scatter_dimension=0, tiled=True)  86.4 us
    all_gather x1, waiting for transfers between devices, shards(): grad_full = lax.all_gather(grad_share, 'batch', axis=0, tiled=True)  80.6 us
    all_gather x1, waiting for transfers between devices, shards(): weight_full = lax.all_gather(weights, 'batch', axis=0, tiled=True)  76.3 us
    reduce_scatter x1, waiting for transfers between devices, shards(): lax.psum_scatter(partial_grad, 'batch', scatter_dimension=0, tiled=True)  71.6 us
    all_gather x1, waiting for transfers between devices, shards(): centre_full = lax.all_gather(centre_features, 'batch', axis=0, tiled=True)  71.2 us
    all_gather x1, waiting for transfers between devices, shards(): batch_full = lax.all_gather(batch_features, 'centre', axis=0, tiled=True)  64.8 us
    all_gather x1, waiting for transfers between devices, shards(): residual_full = lax.all_gather(residual, 'centre', axis=0, tiled=True)  56.2 us
  transfers between devices with their start and end apart: 9, of which 8 were waited for; matrix products, arithmetic and copies ran while one was open for 1% of the time, Pallas kernels for 0%

commit v1 on v0

v1 whole, which is shorter than its diff:
```python
import math

import jax
import jax.numpy as jnp
from jax import lax
from jax.sharding import Mesh
from jax.sharding import PartitionSpec as P

length_scale = 0.5
softening = 0.01
plane = ("x", "y")
ring = ("z_hi", "z_lo")
swap = [(0, 1), (1, 0)]


def gather(value, axis):
    copies = jnp.broadcast_to(value[None], (lax.axis_size(axis),) + value.shape)
    return lax.all_to_all(copies, axis, 0, 0)


def exchange(parts, axis):
    return jnp.sum(lax.all_to_all(parts, axis, 0, 0), axis=0)


def both_cores(value):
    return jnp.stack([value, lax.ppermute(value, "core", swap)])


def to_columns(rows):
    core = lax.axis_index("core")
    half = rows.shape[1] // 2
    first, second = rows[:, :half], rows[:, half:]
    own = jnp.where(core == 0, first, second)
    other = jnp.where(core == 0, second, first)
    return jnp.stack([own, lax.ppermute(other, "core", swap)])


def to_rows(columns):
    core = lax.axis_index("core")
    own, other = columns[0], lax.ppermute(columns[1], "core", swap)
    first = jnp.where(core == 0, own, other)
    second = jnp.where(core == 0, other, own)
    return jnp.concatenate([first, second], axis=1)


def dot(left, right, contract, precision=lax.Precision.HIGHEST):
    return lax.dot_general(
        left, right, (contract, ((), ())), precision=precision, preferred_element_type=jnp.float32
    )


def kernel_matrix(left_rows, right_rows):
    left_norms = jnp.sum(left_rows * left_rows, axis=1)
    right_norms = jnp.sum(right_rows * right_rows, axis=1)
    inner = dot(left_rows, right_rows, ((1,), (1,)))
    squared = left_norms[:, None] + right_norms[None, :] - 2.0 * inner
    return jnp.exp(-jnp.sqrt(squared + softening) / length_scale)


def shards(batch_features, centre_features, targets, weights):
    n_plane, n_ring = lax.axis_size(plane), lax.axis_size(ring)
    own_rows, width = targets.shape
    depth = batch_features.shape[1]
    half = width // 2
    total_rows = own_rows * n_plane * n_ring * 2

    centre = both_cores(gather(centre_features, ring)).reshape(-1, depth)
    batch = both_cores(gather(batch_features, plane)).reshape(-1, depth)
    weight = gather(to_columns(weights), ring)
    weight = weight.transpose(1, 0, 2, 3).reshape(-1, half)
    target = to_columns(targets)
    far = both_cores(lax.all_gather(centre_features, plane, axis=0)).reshape(-1, depth)

    tile = kernel_matrix(batch, centre)
    partial_pred = dot(tile, weight, ((1,), (0,))).reshape(2, n_plane, own_rows, half)
    residual = exchange(partial_pred.transpose(1, 0, 2, 3), plane) - target
    residual_full = gather(residual, plane).transpose(1, 0, 2, 3).reshape(-1, half)
    partial_grad = dot(tile, residual_full, ((0,), (0,))).reshape(2, n_ring, own_rows, half)
    grad = exchange(partial_grad.transpose(1, 0, 2, 3), ring)
    grad_full = gather(grad, ring).transpose(1, 0, 2, 3).reshape(-1, half)

    far_tile = kernel_matrix(far, centre)
    partial_sums = jnp.sum(far_tile, axis=1).reshape(2, n_plane, own_rows)
    row_sums = exchange(partial_sums.transpose(1, 0, 2), plane)
    largest = jnp.max(row_sums).reshape(1, 1)
    largest = jnp.max(gather(largest, plane)).reshape(1, 1)
    largest = jnp.max(gather(largest, ring))

    partial_product = dot(far_tile, grad_full, ((1,), (0,))).reshape(2, n_plane, own_rows, half)
    product = exchange(partial_product.transpose(1, 0, 2, 3), plane)
    step_size = 1.0 / largest
    theta = 2.0 * step_size * grad - step_size * step_size * product
    output_scale = total_rows / math.sqrt(total_rows)
    return to_rows(residual), to_rows(theta * output_scale)


def solution(mesh):
    fine = Mesh(
        mesh.devices.reshape(4, 4, 4, 2, 2),
        ("x", "z_lo", "y", "z_hi", "core"),
    )
    by_batch = P(("x", "z_lo", "y", "z_hi", "core"), None)
    by_centre = P(("y", "z_hi", "core", "x", "z_lo"), None)
    return jax.shard_map(
        shards,
        mesh=fine,
        in_specs=(by_batch, by_centre, by_batch, by_centre),
        out_specs=(by_batch, by_centre),
        check_vma=False,
    )
```

time: 858 us -> 257 us (0.30)
  waiting for transfers between devices: 727 us -> 103 us
  starting transfers between devices: 0.54 us -> 85.1 us
  blocking collectives: 84.3 us -> 0 us
  local copies, waits for them, and re-layouts: 0.2 us -> 15.4 us
    all_gather x5 -> x1, waiting for transfers between devices: 349 us -> 0.01 us  [shards(): lax.all_gather(centre_features, plane, axis=0)]
    psum x1 -> x0, waiting for transfers between devices: 218 us -> none  [spread(): return lax.psum(kept, axis)]
    reduce_scatter x3 -> x0, waiting for transfers between devices: 158 us -> none  [the longest x1 86.4 us: shards(): lax.psum_scatter(partial_pred, 'centre', scatter_dimension=0, tiled=True)]
    all_to_all x0 -> x11, waiting for transfers between devices: none -> 98.1 us  [the longest x7 62.5 us: gather(): return lax.all_to_all(copies, axis, 0, 0)]
    all_to_all x0 -> x11, starting transfers between devices: none -> 53.8 us  [the longest x7 33.5 us: gather(): return lax.all_to_all(copies, axis, 0, 0)]
    pmax x1 -> x0, blocking collectives: 50.9 us -> none  [shards(): largest = lax.pmax(jnp.max(row_sums), 'centre')]
    psum x1 -> x0, blocking collectives: 33.5 us -> none  [shards(): row_sums = lax.psum(jnp.sum(centre_tile, axis=1), 'batch')]
    ppermute x0 -> x7, starting transfers between devices: none -> 31.3 us  [the longest x2 16.5 us: to_rows(): own, other = (columns[0], lax.ppermute(columns[1], 'core', swap))]
  transfers between devices with their start and end apart: 9 -> 19, of which waited for: 8 -> 13; matrix products, arithmetic and copies ran while one was open for 1% -> 18% of each run, Pallas kernels for 0% -> 0%
where the time goes in v1:
time: 257 us; the launch traced here: 256 us
  waiting for transfers between devices  103 us (40%)
  starting transfers between devices  85.1 us (33%)
  matrix products  23.4 us (9%)
  local copies, waits for them, and re-layouts  15.4 us (6%)
  between operations  15 us (6%)
  other arithmetic  14.2 us (6%)
    all_to_all x7, waiting for transfers between devices, gather(): return lax.all_to_all(copies, axis, 0, 0)  62.5 us
    all_to_all x4, waiting for transfers between devices, exchange(): return jnp.sum(lax.all_to_all(parts, axis, 0, 0), axis=0)  35.6 us
    all_to_all x7, starting transfers between devices, gather(): return lax.all_to_all(copies, axis, 0, 0)  33.5 us
    dot_general x5, matrix products, dot(): lax.dot_general(left, right, (contract, ((), ())), precision=precision, p...  23.4 us
    all_to_all x4, starting transfers between devices, exchange(): return jnp.sum(lax.all_to_all(parts, axis, 0, 0), axis=0)  20.2 us
    ppermute x2, starting transfers between devices, to_rows(): own, other = (columns[0], lax.ppermute(columns[1], 'core', swap))  16.5 us
    ppermute x3, starting transfers between devices, both_cores(): return jnp.stack([value, lax.ppermute(value, 'core', swap)])  14.3 us
    broadcast_in_dim x7, local copies, waits for them, and re-layouts, gather(): copies = jnp.broadcast_to(value[None], (lax.axis_size(axis),) + value.shape)  8.67 us
  transfers between devices with their start and end apart: 19, of which 13 were waited for; matrix products, arithmetic and copies ran while one was open for 18% of the time, Pallas kernels for 0%

profile of v1, /device:TPU:1, one launch (start us, length us, event | category | flops | bytes accessed | tf_op | source)
XLA Modules:
  0.0 255.8 jit_solution(2239489020283121836)
XLA Ops:
  9.4 7.7 %all-to-all-start = ((f32[16,32,768]{2,1,0:T(8,128)}), f32[16,32,768]{2,1,0:T(8,128)S(1)}, u32[]{:S(2)}, u32[]{:S(2)}) async-start(f32[16,32,768]{2,1,0:T(8,128)} %broadcast_in_dim.16), calls=%async_computation | async-start | bytes 3145728 | tf_op jit(solution)/shard_map/all_to_all | solution.py:18
  17.9 19.9 %all-to-all-done = f32[16,32,768]{2,1,0:T(8,128)S(1)} async-done(((f32[16,32,768]{2,1,0:T(8,128)}), f32[16,32,768]{2,1,0:T(8,128)S(1)}, u32[]{:S(2)}, u32[]{:S(2)}) %all-to-all-start) | async-done | bytes 1572896 | tf_op jit(solution)/shard_map/all_to_all | solution.py:18
  38.8 8.2 %all-to-all-start.1 = ((f32[8,32,768]{2,1,0:T(8,128)}), f32[8,32,768]{2,1,0:T(8,128)S(1)}, u32[]{:S(2)}, u32[]{:S(2)}) async-start(f32[8,32,768]{2,1,0:T(8,128)} %broadcast_in_dim.17), calls=%async_computation.1 | async-start | bytes 1572864 | tf_op jit(solution)/shard_map/all_to_all | solution.py:18
  47.0 4.4 %collective-permute-start = (f32[16,32,768]{2,1,0:T(8,128)S(1)}, f32[16,32,768]{2,1,0:T(8,128)}, u32[]{:S(2)}, u32[]{:S(2)}) collective-permute-start(f32[16,32,768]{2,1,0:T(8,128)S(1)} %all-to-all-done), channel_id=1, source_target_pairs={{0,1},{1,0},{2,3},{3,2},{4,5},{5,4},{6,7},{7,6},{8,9},{9,8},{10,11... | collective-permute-start | bytes 4718600 | tf_op jit(solution)/shard_map/ppermute | solution.py:26
  54.4 12.7 %all-to-all-done.1 = f32[8,32,768]{2,1,0:T(8,128)S(1)} async-done(((f32[8,32,768]{2,1,0:T(8,128)}), f32[8,32,768]{2,1,0:T(8,128)S(1)}, u32[]{:S(2)}, u32[]{:S(2)}) %all-to-all-start.1) | async-done | bytes 786464 | tf_op jit(solution)/shard_map/all_to_all | solution.py:18
  67.9 3.5 %all-to-all-start.2 = ((f32[8,2,32,256]{3,2,1,0:T(8,128)}), f32[8,2,32,256]{3,2,1,0:T(8,128)S(1)}, u32[]{:S(2)}, u32[]{:S(2)}) async-start(f32[8,2,32,256]{3,2,1,0:T(8,128)} %broadcast_in_dim.18), calls=%async_computation.2 | async-start | bytes 1048576 | tf_op jit(solution)/shard_map/all_to_all | solution.py:18
  71.4 4.2 %collective-permute-start.1 = (f32[8,32,768]{2,1,0:T(8,128)S(1)}, f32[8,32,768]{2,1,0:T(8,128)}, u32[]{:S(2)}, u32[]{:S(2)}) collective-permute-start(f32[8,32,768]{2,1,0:T(8,128)S(1)} %all-to-all-done.1), channel_id=1, source_target_pairs={{0,1},{1,0},{2,3},{3,2},{4,5},{5,4},{6,7},{7,6},{8,9},{9,8},{10,11... | collective-permute-start | bytes 2359304 | tf_op jit(solution)/shard_map/ppermute | solution.py:26
  75.6 8.7 %all-to-all-done.2 = f32[8,2,32,256]{3,2,1,0:T(8,128)S(1)} async-done(((f32[8,2,32,256]{3,2,1,0:T(8,128)}), f32[8,2,32,256]{3,2,1,0:T(8,128)S(1)}, u32[]{:S(2)}, u32[]{:S(2)}) %all-to-all-start.2) | async-done | bytes 524320 | tf_op jit(solution)/shard_map/all_to_all | solution.py:18
  87.7 5.7 %collective-permute-start.5 = (f32[16,32,768]{2,1,0:T(8,128)}, f32[16,32,768]{2,1,0:T(8,128)}, u32[]{:S(2)}, u32[]{:S(2)}) collective-permute-start(f32[16,32,768]{2,1,0:T(8,128)} %bitcast.97), channel_id=1, source_target_pairs={{0,1},{1,0},{2,3},{3,2},{4,5},{5,4},{6,7},{7,6},{8,9},{9,8},{10,11... | collective-permute-start | bytes 4718600 | tf_op jit(solution)/shard_map/ppermute | solution.py:26
  95.7 8.7 %multiply_exponential_fusion.1 = (f32[1024,512]{1,0:T(8,128)S(1)}, f32[1024,512]{1,0:T(8,128)}) fusion(f32[512]{0:T(512)S(1)} %add.48, f32[1024]{0:T(1024)S(1)} %add.46, f32[1024,768]{1,0:T(8,128)S(1)} %bitcast.82, f32[512,768]{1,0:T(8,128)} %bitcast.85), kind=kOutput, calls=%fused_computation.11 | convolution fusion | flops 4834983936 | bytes 8919040 | tf_op jit(solution)/shard_map/dot_general | solution.py:47
  107.3 6.7 %all-to-all-start.3 = ((f32[16,2,32,256]{3,2,1,0:T(8,128)}), f32[16,2,32,256]{3,2,1,0:T(8,128)S(1)}, u32[]{:S(2)}, u32[]{:S(2)}) async-start(f32[16,2,32,256]{3,2,1,0:T(8,128)} %copy.32), calls=%async_computation.3 | async-start | bytes 2097152 | tf_op jit(solution)/shard_map/all_to_all | solution.py:22
  114.4 16.6 %all-to-all-done.3 = f32[16,2,32,256]{3,2,1,0:T(8,128)S(1)} async-done(((f32[16,2,32,256]{3,2,1,0:T(8,128)}), f32[16,2,32,256]{3,2,1,0:T(8,128)S(1)}, u32[]{:S(2)}, u32[]{:S(2)}) %all-to-all-start.3) | async-done | bytes 1048608 | tf_op jit(solution)/shard_map/all_to_all | solution.py:22
  132.2 3.9 %all-to-all-start.7 = ((f32[16,2,32,256]{3,2,1,0:T(8,128)}), f32[16,2,32,256]{3,2,1,0:T(8,128)S(1)}, u32[]{:S(2)}, u32[]{:S(2)}) async-start(f32[16,2,32,256]{3,2,1,0:T(8,128)} %broadcast_in_dim.22), calls=%async_computation.7 | async-start | bytes 2097152 | tf_op jit(solution)/shard_map/all_to_all | solution.py:18
  140.4 3.8 %multiply_reduce_fusion = (f32[2,16,32]{2,1,0:T(8,128)S(1)}, f32[2,16,32,768]{3,2,1,0:T(8,128)}) fusion(f32[1,16,32,768]{3,2,1,0:T(8,128)} %bitcast.20, f32[1,16,32,768]{3,2,1,0:T(8,128)} %bitcast.98), kind=kLoop, calls=%fused_computation.2 | loop fusion | flops 2358272 | bytes 6295552 | tf_op jit(solution)/shard_map/reduce_sum | solution.py:53
  144.3 9.3 %fusion.9 = (f32[1024]{0:T(1024)S(1)}, f32[1024,512]{1,0:T(8,128)}) fusion(f32[1024,768]{1,0:T(8,128)} %bitcast.90, f32[512,768]{1,0:T(8,128)} %bitcast.86, f32[512]{0:T(512)S(1)} %add.48, f32[1024]{0:T(1024)S(1)} %add.52), kind=kOutput, calls=%fused_computation.34 | convolution fusion | flops 4835507200 | bytes 6825984 | tf_op jit(solution)/shard_map/dot_general | solution.py:47
  154.2 6.4 %all-to-all-start.4 = ((f32[16,2,32]{2,1,0:T(2,128)}), f32[16,2,32]{2,1,0:T(2,128)S(1)}, u32[]{:S(2)}, u32[]{:S(2)}) async-start(f32[16,2,32]{2,1,0:T(2,128)} %copy.33), calls=%async_computation.4 | async-start | bytes 32768 | tf_op jit(solution)/shard_map/all_to_all | solution.py:22
  163.4 3.7 %all-to-all-done.4 = f32[16,2,32]{2,1,0:T(2,128)S(1)} async-done(((f32[16,2,32]{2,1,0:T(2,128)}), f32[16,2,32]{2,1,0:T(2,128)S(1)}, u32[]{:S(2)}, u32[]{:S(2)}) %all-to-all-start.4) | async-done | bytes 4128 | tf_op jit(solution)/shard_map/all_to_all | solution.py:22
  167.1 3.5 %all-to-all-start.8 = ((f32[8,2,32,256]{3,2,1,0:T(8,128)}), f32[8,2,32,256]{3,2,1,0:T(8,128)S(1)}, u32[]{:S(2)}, u32[]{:S(2)}) async-start(f32[8,2,32,256]{3,2,1,0:T(8,128)} %copy.38), calls=%async_computation.8 | async-start | bytes 1048576 | tf_op jit(solution)/shard_map/all_to_all | solution.py:22
  171.2 13.5 %all-to-all-done.8 = f32[8,2,32,256]{3,2,1,0:T(8,128)S(1)} async-done(((f32[8,2,32,256]{3,2,1,0:T(8,128)}), f32[8,2,32,256]{3,2,1,0:T(8,128)S(1)}, u32[]{:S(2)}, u32[]{:S(2)}) %all-to-all-start.8) | async-done | bytes 524320 | tf_op jit(solution)/shard_map/all_to_all | solution.py:22
  189.5 6.2 %all-to-all-done.5 = f32[16,1,1]{2,1,0:T(1,128)S(1)} async-done(((f32[16,1,1]{2,1,0:T(1,128)}), f32[16,1,1]{2,1,0:T(1,128)S(1)}, u32[]{:S(2)}, u32[]{:S(2)}) %all-to-all-start.5) | async-done | bytes 96 | tf_op jit(solution)/shard_map/all_to_all | solution.py:18
  200.6 11.6 %all-to-all-done.9 = f32[8,2,32,256]{3,2,1,0:T(8,128)S(1)} async-done(((f32[8,2,32,256]{3,2,1,0:T(8,128)}), f32[8,2,32,256]{3,2,1,0:T(8,128)S(1)}, u32[]{:S(2)}, u32[]{:S(2)}) %all-to-all-start.9) | async-done | bytes 524320 | tf_op jit(solution)/shard_map/all_to_all | solution.py:18
  223.1 3.7 %all-to-all-start.10 = ((f32[16,2,32,256]{3,2,1,0:T(8,128)}), f32[16,2,32,256]{3,2,1,0:T(8,128)S(1)}, u32[]{:S(2)}, u32[]{:S(2)}) async-start(f32[16,2,32,256]{3,2,1,0:T(8,128)} %copy.40), calls=%async_computation.10 | async-start | bytes 2097152 | tf_op jit(solution)/shard_map/all_to_all | solution.py:22
  226.8 7.7 %collective-permute-start.4 = (f32[32,256]{1,0:T(8,128)S(1)}, f32[32,256]{1,0:T(8,128)S(1)}, u32[]{:S(2)}, u32[]{:S(2)}) collective-permute-start(f32[32,256]{1,0:T(8,128)S(1)} %slice_bitcast_fusion.2), channel_id=1, source_target_pairs={{0,1},{1,0},{2,3},{3,2},{4,5},{5,4},{6,7},{7,6},{8,9},{9,8},{10,11... | collective-permute-start | bytes 98312 | tf_op jit(solution)/shard_map/ppermute | solution.py:40
  238.6 8.8 %collective-permute-start.6 = (f32[32,256]{1,0:T(8,128)S(1)}, f32[32,256]{1,0:T(8,128)S(1)}, u32[]{:S(2)}, u32[]{:S(2)}) collective-permute-start(f32[32,256]{1,0:T(8,128)S(1)} %slice_bitcast_fusion), channel_id=1, source_target_pairs={{0,1},{1,0},{2,3},{3,2},{4,5},{5,4},{6,7},{7,6},{8,9},{9,8},{10,11... | collective-permute-start | bytes 98312 | tf_op jit(solution)/shard_map/ppermute | solution.py:40
  (75 shorter events, 52.0 us)
Async XLA Ops:
  7.2 30.6 %copy-start.4 = (f32[32,768]{1,0:T(8,128)S(1)}, f32[32,768]{1,0:T(8,128)}, u32[]{:S(2)}) copy-start(f32[32,768]{1,0:T(8,128)} %param.5) | copy-start | bytes 294916
  9.4 42.0 %copy-start.5 = (f32[32,512]{1,0:T(8,128)S(1)}, f32[32,512]{1,0:T(8,128)}, u32[]{:S(2)}) copy-start(f32[32,512]{1,0:T(8,128)} %param.7) | copy-start | bytes 196612
  9.4 28.3 %all-to-all-start = ((f32[16,32,768]{2,1,0:T(8,128)}), f32[16,32,768]{2,1,0:T(8,128)S(1)}, u32[]{:S(2)}, u32[]{:S(2)}) async-start(f32[16,32,768]{2,1,0:T(8,128)} %broadcast_in_dim.16), calls=%async_computation | async-start | bytes 3145728 | tf_op jit(solution)/shard_map/all_to_all | solution.py:18
  17.1 70.5 %all-gather.3.cloned.1.call-start = ((), (), s32[]{:S(2)}) async-start(), calls=%async_computation.11 | async-start | bytes 1671168 | tf_op jit(solution)/shard_map/all_gather | solution.py:72
  37.8 30.1 %copy-start.1 = (f32[16,32,768]{2,1,0:T(8,128)}, f32[16,32,768]{2,1,0:T(8,128)S(1)}, u32[]{:S(2)}) copy-start(f32[16,32,768]{2,1,0:T(8,128)S(1)} %all-to-all-done) | copy-start | bytes 4718596
  38.8 28.2 %all-to-all-start.1 = ((f32[8,32,768]{2,1,0:T(8,128)}), f32[8,32,768]{2,1,0:T(8,128)S(1)}, u32[]{:S(2)}, u32[]{:S(2)}) async-start(f32[8,32,768]{2,1,0:T(8,128)} %broadcast_in_dim.17), calls=%async_computation.1 | async-start | bytes 1572864 | tf_op jit(solution)/shard_map/all_to_all | solution.py:18
  47.0 46.3 %collective-permute-start = (f32[16,32,768]{2,1,0:T(8,128)S(1)}, f32[16,32,768]{2,1,0:T(8,128)}, u32[]{:S(2)}, u32[]{:S(2)}) collective-permute-start(f32[16,32,768]{2,1,0:T(8,128)S(1)} %all-to-all-done), channel_id=1, source_target_pairs={{0,1},{1,0},{2,3},{3,2},{4,5},{5,4},{6,7},{7,6},{8,9},{9,8},{10,11... | collective-permute-start | bytes 4718600 | tf_op jit(solution)/shard_map/ppermute | solution.py:26
  51.4 2.9 %collective-permute-start.2 = (f32[32,256]{1,0:T(8,128)S(1)}, f32[32,256]{1,0:T(8,128)S(1)}, u32[]{:S(2)}, u32[]{:S(2)}) collective-permute-start(f32[32,256]{1,0:T(8,128)S(1)} %get-tuple-element.15), channel_id=1, source_target_pairs={{0,1},{1,0},{2,3},{3,2},{4,5},{5,4},{6,7},{7,6},{8,9},{9,8},{10,11... | collective-permute-start | bytes 98312 | tf_op jit(solution)/shard_map/ppermute | solution.py:35
  67.9 16.4 %all-to-all-start.2 = ((f32[8,2,32,256]{3,2,1,0:T(8,128)}), f32[8,2,32,256]{3,2,1,0:T(8,128)S(1)}, u32[]{:S(2)}, u32[]{:S(2)}) async-start(f32[8,2,32,256]{3,2,1,0:T(8,128)} %broadcast_in_dim.18), calls=%async_computation.2 | async-start | bytes 1048576 | tf_op jit(solution)/shard_map/all_to_all | solution.py:18
  71.4 13.8 %collective-permute-start.1 = (f32[8,32,768]{2,1,0:T(8,128)S(1)}, f32[8,32,768]{2,1,0:T(8,128)}, u32[]{:S(2)}, u32[]{:S(2)}) collective-permute-start(f32[8,32,768]{2,1,0:T(8,128)S(1)} %all-to-all-done.1), channel_id=1, source_target_pairs={{0,1},{1,0},{2,3},{3,2},{4,5},{5,4},{6,7},{7,6},{8,9},{9,8},{10,11... | collective-permute-start | bytes 2359304 | tf_op jit(solution)/shard_map/ppermute | solution.py:26
  87.7 52.7 %collective-permute-start.5 = (f32[16,32,768]{2,1,0:T(8,128)}, f32[16,32,768]{2,1,0:T(8,128)}, u32[]{:S(2)}, u32[]{:S(2)}) collective-permute-start(f32[16,32,768]{2,1,0:T(8,128)} %bitcast.97), channel_id=1, source_target_pairs={{0,1},{1,0},{2,3},{3,2},{4,5},{5,4},{6,7},{7,6},{8,9},{9,8},{10,11... | collective-permute-start | bytes 4718600 | tf_op jit(solution)/shard_map/ppermute | solution.py:26
  107.3 23.6 %all-to-all-start.3 = ((f32[16,2,32,256]{3,2,1,0:T(8,128)}), f32[16,2,32,256]{3,2,1,0:T(8,128)S(1)}, u32[]{:S(2)}, u32[]{:S(2)}) async-start(f32[16,2,32,256]{3,2,1,0:T(8,128)} %copy.32), calls=%async_computation.3 | async-start | bytes 2097152 | tf_op jit(solution)/shard_map/all_to_all | solution.py:22
  114.0 22.1 %copy-start = (f32[1024,512]{1,0:T(8,128)S(1)}, f32[1024,512]{1,0:T(8,128)}, u32[]{:S(2)}) copy-start(f32[1024,512]{1,0:T(8,128)} %get-tuple-element.17) | copy-start | bytes 6291460
  114.0 17.0 %collective-permute-start.3 = (f32[32,256]{1,0:T(8,128)S(1)}, f32[32,256]{1,0:T(8,128)S(1)}, u32[]{:S(2)}, u32[]{:S(2)}) collective-permute-start(f32[32,256]{1,0:T(8,128)S(1)} %get-tuple-element.13), channel_id=1, source_target_pairs={{0,1},{1,0},{2,3},{3,2},{4,5},{5,4},{6,7},{7,6},{8,9},{9,8},{10,11... | collective-permute-start | bytes 98312 | tf_op jit(solution)/shard_map/ppermute | solution.py:35
  132.2 22.0 %all-to-all-start.7 = ((f32[16,2,32,256]{3,2,1,0:T(8,128)}), f32[16,2,32,256]{3,2,1,0:T(8,128)S(1)}, u32[]{:S(2)}, u32[]{:S(2)}) async-start(f32[16,2,32,256]{3,2,1,0:T(8,128)} %broadcast_in_dim.22), calls=%async_computation.7 | async-start | bytes 2097152 | tf_op jit(solution)/shard_map/all_to_all | solution.py:18
  154.2 12.9 %all-to-all-start.4 = ((f32[16,2,32]{2,1,0:T(2,128)}), f32[16,2,32]{2,1,0:T(2,128)S(1)}, u32[]{:S(2)}, u32[]{:S(2)}) async-start(f32[16,2,32]{2,1,0:T(2,128)} %copy.33), calls=%async_computation.4 | async-start | bytes 32768 | tf_op jit(solution)/shard_map/all_to_all | solution.py:22
  163.4 53.4 %copy-start.2 = (f32[1024,512]{1,0:T(8,128)S(1)}, f32[1024,512]{1,0:T(8,128)}, u32[]{:S(2)}) copy-start(f32[1024,512]{1,0:T(8,128)} %get-tuple-element.19) | copy-start | bytes 6291460
  167.1 17.6 %all-to-all-start.8 = ((f32[8,2,32,256]{3,2,1,0:T(8,128)}), f32[8,2,32,256]{3,2,1,0:T(8,128)S(1)}, u32[]{:S(2)}, u32[]{:S(2)}) async-start(f32[8,2,32,256]{3,2,1,0:T(8,128)} %copy.38), calls=%async_computation.8 | async-start | bytes 1048576 | tf_op jit(solution)/shard_map/all_to_all | solution.py:22
  185.9 9.8 %all-to-all-start.5 = ((f32[16,1,1]{2,1,0:T(1,128)}), f32[16,1,1]{2,1,0:T(1,128)S(1)}, u32[]{:S(2)}, u32[]{:S(2)}) async-start(f32[16,1,1]{2,1,0:T(1,128)} %broadcast_in_dim.20), calls=%async_computation.5 | async-start | bytes 16384 | tf_op jit(solution)/shard_map/all_to_all | solution.py:18
  196.5 15.7 %all-to-all-start.9 = ((f32[8,2,32,256]{3,2,1,0:T(8,128)}), f32[8,2,32,256]{3,2,1,0:T(8,128)S(1)}, u32[]{:S(2)}, u32[]{:S(2)}) async-start(f32[8,2,32,256]{3,2,1,0:T(8,128)} %broadcast_in_dim.23), calls=%async_computation.9 | async-start | bytes 1048576 | tf_op jit(solution)/shard_map/all_to_all | solution.py:18
  213.4 9.7 %all-to-all-start.6 = ((f32[8,1,1]{2,1,0:T(1,128)}), f32[8,1,1]{2,1,0:T(1,128)S(1)}, u32[]{:S(2)}, u32[]{:S(2)}) async-start(f32[8,1,1]{2,1,0:T(1,128)} %broadcast_in_dim.21), calls=%async_computation.6 | async-start | bytes 8192 | tf_op jit(solution)/shard_map/all_to_all | solution.py:18
  223.1 15.4 %all-to-all-start.10 = ((f32[16,2,32,256]{3,2,1,0:T(8,128)}), f32[16,2,32,256]{3,2,1,0:T(8,128)S(1)}, u32[]{:S(2)}, u32[]{:S(2)}) async-start(f32[16,2,32,256]{3,2,1,0:T(8,128)} %copy.40), calls=%async_computation.10 | async-start | bytes 2097152 | tf_op jit(solution)/shard_map/all_to_all | solution.py:22
  226.8 8.6 %collective-permute-start.4 = (f32[32,256]{1,0:T(8,128)S(1)}, f32[32,256]{1,0:T(8,128)S(1)}, u32[]{:S(2)}, u32[]{:S(2)}) collective-permute-start(f32[32,256]{1,0:T(8,128)S(1)} %slice_bitcast_fusion.2), channel_id=1, source_target_pairs={{0,1},{1,0},{2,3},{3,2},{4,5},{5,4},{6,7},{7,6},{8,9},{9,8},{10,11... | collective-permute-start | bytes 98312 | tf_op jit(solution)/shard_map/ppermute | solution.py:40
  238.6 9.7 %collective-permute-start.6 = (f32[32,256]{1,0:T(8,128)S(1)}, f32[32,256]{1,0:T(8,128)S(1)}, u32[]{:S(2)}, u32[]{:S(2)}) collective-permute-start(f32[32,256]{1,0:T(8,128)S(1)} %slice_bitcast_fusion), channel_id=1, source_target_pairs={{0,1},{1,0},{2,3},{3,2},{4,5},{5,4},{6,7},{7,6},{8,9},{9,8},{10,11... | collective-permute-start | bytes 98312 | tf_op jit(solution)/shard_map/ppermute | solution.py:40
  (2 other events, 16.5 us)
Sparse Core Ops, SparseCore 0:
  20.5 51.5 all-gather.2

commit v2 on v1

v2 whole, which is shorter than its diff:
```python
import math

import jax
import jax.numpy as jnp
from jax import lax
from jax.experimental import pallas as pl
from jax.experimental.pallas import tpu as pltpu
from jax.sharding import Mesh
from jax.sharding import PartitionSpec as P

length_scale = 0.5
softening = 0.01
plane = ("x", "y")
ring = ("z_hi", "z_lo")
swap = [(0, 1), (1, 0)]
rider = 8
vmem_bytes = 32 * 1024 * 1024


def whole(space=pltpu.VMEM):
    return pl.BlockSpec(memory_space=space)


def params():
    return pltpu.CompilerParams(vmem_limit_bytes=vmem_bytes)


def cost(flops, moved, transcendentals=0):
    return pl.CostEstimate(flops=flops, bytes_accessed=moved, transcendentals=transcendentals)


def dot(left, right, left_dim, right_dim):
    return lax.dot_general(
        left,
        right,
        (((left_dim,), (right_dim,)), ((), ())),
        precision=lax.Precision.HIGHEST,
        preferred_element_type=jnp.float32,
    )


def right_norms(rows):
    ones = jnp.ones((8, rows.shape[1]), jnp.float32)
    return dot(ones, rows * rows, 1, 1)


def kernel_block(left, right, norms):
    left_norms = jnp.sum(left * left, axis=1, keepdims=True)
    squared = left_norms + norms[:1] - 2.0 * dot(left, right, 1, 1)
    return jnp.exp(-jnp.sqrt(squared + softening) / length_scale)


def flat(value):
    return value.reshape(-1, value.shape[-1])


def predict_kernel(half, left_ref, own_ref, other_ref, mine_ref, *refs):
    tile_ref, pred_ref, norm_ref = refs[-3:]
    rows = own_ref.shape[0]

    @pl.when(pl.program_id(0) == 0)
    def _():
        norm_ref[:, :rows] = right_norms(own_ref[:, half:])
        norm_ref[:, rows:] = right_norms(other_ref[:, half:])

    left = flat(left_ref[...])
    own = kernel_block(left, own_ref[:, half:], norm_ref[:, :rows])
    other = kernel_block(left, other_ref[:, half:], norm_ref[:, rows:])
    tile_ref[:, :rows] = own
    tile_ref[:, rows:] = other
    pred = dot(own, mine_ref[...], 1, 0) + dot(other, other_ref[:, :half], 1, 0)
    pred_ref[...] = pred.reshape(pred_ref.shape)


def predict(left, own, other, mine, place, before=None):
    count, rows, depth = left.shape
    columns, half = 2 * own.shape[0], mine.shape[1]
    step = count // 2
    operands = [left, own, other, mine]
    in_specs = [
        pl.BlockSpec((step, rows, depth), lambda i: (i, 0, 0)),
        pl.BlockSpec(own.shape, lambda i: (0, 0)),
        pl.BlockSpec(other.shape, lambda i: (0, 0)),
        pl.BlockSpec(mine.shape, lambda i: (0, 0)),
    ]
    aliases = {}
    if before is not None:
        operands.append(before)
        in_specs.append(whole(pl.ANY))
        aliases = {4: 1}

    def body(*refs):
        predict_kernel(half, *refs)

    return pl.pallas_call(
        body,
        grid=(2,),
        in_specs=in_specs,
        out_specs=[
            pl.BlockSpec((step * rows, columns), lambda i: (i, 0)),
            pl.BlockSpec((step, 1, rows, half), lambda i: (i, place, 0, 0)),
        ],
        out_shape=[
            jax.ShapeDtypeStruct((count * rows, columns), jnp.float32),
            jax.ShapeDtypeStruct((count, 2, rows, half), jnp.float32),
        ],
        scratch_shapes=[pltpu.VMEM((8, columns), jnp.float32)],
        input_output_aliases=aliases,
        compiler_params=params(),
        cost_estimate=cost(12 * count * rows * columns * (depth + half), 6 * 1024 * 1024, 2 * count * rows * columns),
    )(*operands)


def far_kernel(half, shift_ref, left_ref, own_ref, other_ref, tile_ref, sums_ref, norm_ref, total_ref):
    rows = own_ref.shape[0]

    @pl.when(pl.program_id(0) == 0)
    def _():
        norm_ref[:, :rows] = right_norms(own_ref[:, half:])
        norm_ref[:, rows:] = right_norms(other_ref[:, half:])
        total_ref[...] = jnp.zeros_like(total_ref)

    left = flat(left_ref[...])
    for place, ref in ((0, own_ref), (1, other_ref)):
        columns = pl.ds(place * rows, rows)
        block = kernel_block(left, ref[:, half:], norm_ref[:, columns])
        tile_ref[:, columns] = block
        total_ref[place : place + 1] += jnp.sum(block, axis=0, keepdims=True)
    sums_ref[...] = pltpu.roll(total_ref[...], shift_ref[0], 1)


def far_tile(left, own, other, half, shift):
    count, rows, depth = left.shape
    columns = 2 * own.shape[0]
    step = count // 4

    def body(*refs):
        far_kernel(half, *refs)

    return pl.pallas_call(
        body,
        grid=(4,),
        in_specs=[
            whole(pltpu.SMEM),
            pl.BlockSpec((step, rows, depth), lambda i: (i, 0, 0)),
            pl.BlockSpec(own.shape, lambda i: (0, 0)),
            pl.BlockSpec(other.shape, lambda i: (0, 0)),
        ],
        out_specs=[
            pl.BlockSpec((step * rows, columns), lambda i: (i, 0)),
            pl.BlockSpec((rider, columns // 2), lambda i: (0, 0)),
        ],
        out_shape=[
            jax.ShapeDtypeStruct((count * rows, columns), jnp.float32),
            jax.ShapeDtypeStruct((rider, columns // 2), jnp.float32),
        ],
        scratch_shapes=[pltpu.VMEM((8, columns), jnp.float32), pltpu.VMEM((rider, columns // 2), jnp.float32)],
        compiler_params=params(),
        cost_estimate=cost(12 * count * rows * columns * depth, 7 * 1024 * 1024, 2 * count * rows * columns),
    )(shift, left, own, other)


def settle_kernel(parts_ref, target_ref, residual_ref, copies_ref):
    residual = jnp.sum(parts_ref[...], axis=0) - target_ref[...]
    residual_ref[...] = residual
    copies_ref[...] = jnp.broadcast_to(residual[None], copies_ref.shape)


def settle(parts, target):
    shape = jax.ShapeDtypeStruct
    return pl.pallas_call(
        settle_kernel,
        in_specs=[whole(), whole()],
        out_specs=[whole(), whole()],
        out_shape=[shape(target.shape, jnp.float32), shape(parts.shape, jnp.float32)],
        compiler_params=params(),
        cost_estimate=cost(2 * parts.size, 8 * parts.size),
    )(parts, target)


def gradient_kernel(rows, place_ref, first_ref, second_ref, residual_ref, sums_ref, out_ref):
    count = out_ref.shape[0]
    total = dot(first_ref[...], flat(residual_ref[:, :rows]), 0, 0)
    total += dot(second_ref[...], flat(residual_ref[:, rows:]), 0, 0)
    for step in range(count):
        place = lax.rem(place_ref[0] + step, count)
        out_ref[place, :rows] = total[step * rows : (step + 1) * rows]
        out_ref[place, rows : 2 * rows] = total[(count + step) * rows : (count + step + 1) * rows]
        out_ref[place, 2 * rows :] = sums_ref[...]


def gradient(place, first, second, residual, sums, rows):
    count = first.shape[1] // (2 * rows)
    half = residual.shape[-1]

    def body(*refs):
        gradient_kernel(rows, *refs)

    return pl.pallas_call(
        body,
        in_specs=[whole(pltpu.SMEM)] + [whole()] * 4,
        out_specs=whole(),
        out_shape=jax.ShapeDtypeStruct((count, 2 * rows + rider, half), jnp.float32),
        compiler_params=params(),
        cost_estimate=cost(24 * first.size * half, 4 * 1024 * 1024),
    )(place, first, second, residual, sums)


def collect_kernel(parts_ref, grad_ref, copies_ref, largest_ref):
    rows = grad_ref.shape[0]
    total = jnp.sum(parts_ref[...], axis=0)
    grad_ref[...] = total[:rows]
    copies_ref[...] = jnp.broadcast_to(total[None, :rows], copies_ref.shape)
    largest = jnp.max(jnp.max(total[rows:], axis=0, keepdims=True), axis=1, keepdims=True)
    largest_ref[...] = jnp.broadcast_to(largest, largest_ref.shape)


def collect(parts):
    count, packed, half = parts.shape
    rows = packed - rider
    shape = jax.ShapeDtypeStruct
    return pl.pallas_call(
        collect_kernel,
        in_specs=[whole()],
        out_specs=[whole()] * 3,
        out_shape=[
            shape((rows, half), jnp.float32),
            shape((count, rows, half), jnp.float32),
            shape((rider, half), jnp.float32),
        ],
        compiler_params=params(),
        cost_estimate=cost(2 * parts.size, 8 * parts.size),
    )(parts)


def product_kernel(rows, place_ref, tile_ref, grad_ref, largest_ref, out_ref):
    count = grad_ref.shape[0]
    places = [lax.rem(place_ref[0] + step, count) for step in range(count)]
    own = jnp.concatenate([grad_ref[place, :rows] for place in places], axis=0)
    other = jnp.concatenate([grad_ref[place, rows:] for place in places], axis=0)
    middle, rest = own.shape[0], out_ref.shape[0] * rows
    for core in range(2):
        tile = tile_ref[pl.ds(core * rest, rest), :]
        total = dot(tile[:, :middle], own, 1, 0) + dot(tile[:, middle:], other, 1, 0)
        out_ref[:, core * rows : (core + 1) * rows] = total.reshape(-1, rows, total.shape[-1])
    out_ref[:, 2 * rows :] = jnp.broadcast_to(largest_ref[...][None], (out_ref.shape[0], rider, out_ref.shape[2]))


def product(place, tile, grads, largest, rows):
    half = grads.shape[-1]
    count = tile.shape[0] // (2 * rows)

    def body(*refs):
        product_kernel(rows, *refs)

    return pl.pallas_call(
        body,
        in_specs=[whole(pltpu.SMEM)] + [whole()] * 3,
        out_specs=whole(),
        out_shape=jax.ShapeDtypeStruct((count, 2 * rows + rider, half), jnp.float32),
        compiler_params=params(),
        cost_estimate=cost(12 * tile.size * half, 4 * 1024 * 1024),
    )(place, tile, grads, largest)


def finish_kernel(scale, parts_ref, grad_ref, theta_ref):
    rows = grad_ref.shape[0]
    total = jnp.sum(parts_ref[:, :rows], axis=0)
    largest = jnp.max(parts_ref[:, rows:], axis=0)
    largest = jnp.max(jnp.max(largest, axis=0, keepdims=True), axis=1, keepdims=True)
    step_size = 1.0 / largest
    theta_ref[...] = (2.0 * step_size * grad_ref[...] - step_size * step_size * total) * scale


def finish(parts, grad, scale):
    def body(*refs):
        finish_kernel(scale, *refs)

    return pl.pallas_call(
        body,
        in_specs=[whole(), whole()],
        out_specs=whole(),
        out_shape=jax.ShapeDtypeStruct(grad.shape, jnp.float32),
        compiler_params=params(),
        cost_estimate=cost(2 * parts.size, 4 * parts.size),
    )(parts, grad)


def gather(value, axis):
    copies = jnp.broadcast_to(value[None], (lax.axis_size(axis),) + value.shape)
    return lax.all_to_all(copies, axis, 0, 0)


def ring_pieces(value):
    count, low = lax.axis_size(ring), lax.axis_size("z_lo")

    def slot(place):
        return place % low * (count // low) + place // low

    pieces = [value]
    for step in range(1, count):
        pairs = [(slot(place), slot((place - step) % count)) for place in range(count)]
        pieces.append(lax.ppermute(value, ("z_lo", "z_hi"), pairs))
    return pieces


def from_other(value):
    return lax.ppermute(value, "core", swap)


def halves(rows):
    core = lax.axis_index("core")
    half = rows.shape[1] // 2
    first, second = rows[:, :half], rows[:, half:]
    return jnp.where(core == 0, first, second), jnp.where(core == 0, second, first)


def to_rows(columns):
    core = lax.axis_index("core")
    rows = columns.shape[0] // 2
    own, other = columns[:rows], from_other(columns[rows:])
    first = jnp.where(core == 0, own, other)
    second = jnp.where(core == 0, other, own)
    return jnp.concatenate([first, second], axis=1)


def shards(batch_features, centre_features, targets, weights):
    rows, width = targets.shape
    half = width // 2
    total_rows = rows * lax.axis_size(plane) * lax.axis_size(ring) * 2
    place = lax.axis_index(ring)

    mine, theirs = halves(weights)
    pieces = ring_pieces(jnp.concatenate([theirs, centre_features, mine], axis=1))
    cut = half + centre_features.shape[1]
    batch = gather(batch_features, plane)
    own = jnp.concatenate([piece[:, :cut] for piece in pieces], axis=0)
    mine = jnp.concatenate([piece[:, cut:] for piece in pieces], axis=0)
    other = from_other(own)
    batch_other = from_other(batch)
    later, batch = lax.optimization_barrier((centre_features, batch))
    far = gather(later, plane)
    target_mine, target_theirs = halves(targets)
    target = jnp.concatenate([target_mine, from_other(target_theirs)], axis=0)

    first, pred = predict(batch, own, other, mine, 0)
    second, pred = predict(batch_other, own, other, mine, 1, pred)
    parts = lax.all_to_all(pred.reshape(-1, 2 * rows, half), plane, 0, 0)
    residual, copies = settle(parts, target)
    residual_full = lax.all_to_all(copies, plane, 0, 0)

    far, pred = lax.optimization_barrier((far, pred))
    far = jnp.concatenate([far, from_other(far)], axis=0)
    place_ref = place.reshape(1).astype(jnp.int32)
    tile, sums = far_tile(far, own, other, half, place_ref * rows)

    parts = lax.all_to_all(gradient(place_ref, first, second, residual_full, sums, rows), ring, 0, 0)
    grad, copies, largest = collect(parts)
    grad_full = lax.all_to_all(copies, ring, 0, 0)
    parts = lax.all_to_all(product(place_ref, tile, grad_full, largest, rows), plane, 0, 0)
    theta = finish(parts, grad, total_rows / math.sqrt(total_rows))
    return to_rows(residual), to_rows(theta)


def solution(mesh):
    fine = Mesh(
        mesh.devices.reshape(4, 4, 4, 2, 2),
        ("x", "z_lo", "y", "z_hi", "core"),
    )
    by_batch = P(("x", "z_lo", "y", "z_hi", "core"), None)
    by_centre = P(("y", "z_hi", "core", "x", "z_lo"), None)
    return jax.shard_map(
        shards,
        mesh=fine,
        in_specs=(by_batch, by_centre, by_batch, by_centre),
        out_specs=(by_batch, by_centre),
        check_vma=False,
    )
```

time: 257 us -> 194 us (0.75)
  waiting for transfers between devices: 103 us -> 40.5 us
  blocking collectives: 0 us -> 35.5 us
  Pallas kernels: 0 us -> 35.2 us
  starting transfers between devices: 85.1 us -> 60.3 us
  matrix products: 23.4 us -> 0 us
  between operations: 15 us -> 0.88 us
  other arithmetic: 14.2 us -> 5.87 us
    all_to_all x7 -> x2, waiting for transfers between devices: 62.5 us -> 1.16 us  [gather(): return lax.all_to_all(copies, axis, 0, 0)]
    all_to_all x0 -> x2, blocking collectives: none -> 35.5 us  [the longest x1 18.4 us: shards(): lax.all_to_all(gradient(place_ref, first, second, residual_full, sums, ro...]
    pallas_call x0 -> x8, Pallas kernels: none -> 35.2 us  [the longest x2 19 us: predict(): pl.pallas_call(body, grid=(2,), in_specs=in_specs, out_specs=[pl.BlockSpe...]
    dot_general x5 -> x0, matrix products: 23.4 us -> none  [dot(): lax.dot_general(left, right, (contract, ((), ())), precision=precision, p...]
    all_to_all x7 -> x2, starting transfers between devices: 33.5 us -> 12.1 us  [gather(): return lax.all_to_all(copies, axis, 0, 0)]
    all_to_all x4 -> x3, waiting for transfers between devices: 35.6 us -> 22.1 us  [the longest x1 14.7 us: shards(): parts = lax.all_to_all(pred.reshape(-1, 2 * rows, half), plane, 0, 0)]
    ppermute x7 -> x13, waiting for transfers between devices: 3.92 us -> 17.2 us  [the longest x7 15.3 us: ring_pieces(): pieces.append(lax.ppermute(value, ('z_lo', 'z_hi'), pairs))]
    unnamed x14 -> x32, local copies, waits for them, and re-layouts: 0.03 us -> 9.98 us
  transfers between devices with their start and end apart: 19 -> 18, of which waited for: 13 -> 10; matrix products, arithmetic and copies ran while one was open for 18% -> 6% of each run, Pallas kernels for 0% -> 16%
where the time goes in v2:
time: 194 us; the launch traced here: 193 us
  starting transfers between devices  60.3 us (31%)
  waiting for transfers between devices  40.5 us (21%)
  blocking collectives  35.5 us (18%)
  Pallas kernels  35.2 us (18%)
  local copies, waits for them, and re-layouts  14.3 us (7%)
  other arithmetic  5.87 us (3%)
    pallas_call x2, Pallas kernels, predict(): pl.pallas_call(body, grid=(2,), in_specs=in_specs, out_specs=[pl.BlockSpe...  19 us
    all_to_all x1, blocking collectives, shards(): lax.all_to_all(gradient(place_ref, first, second, residual_full, sums, ro...  18.4 us
    ppermute x6, starting transfers between devices, from_other(): return lax.ppermute(value, 'core', swap)  18.2 us
    all_to_all x1, blocking collectives, shards(): grad_full = lax.all_to_all(copies, ring, 0, 0)  17.1 us
    ppermute x7, starting transfers between devices, ring_pieces(): pieces.append(lax.ppermute(value, ('z_lo', 'z_hi'), pairs))  16.2 us
    ppermute x7, waiting for transfers between devices, ring_pieces(): pieces.append(lax.ppermute(value, ('z_lo', 'z_hi'), pairs))  15.3 us
    all_to_all x1, waiting for transfers between devices, shards(): parts = lax.all_to_all(pred.reshape(-1, 2 * rows, half), plane, 0, 0)  14.7 us
    all_to_all x2, starting transfers between devices, gather(): return lax.all_to_all(copies, axis, 0, 0)  12.1 us
  transfers between devices with their start and end apart: 18, of which 10 were waited for; matrix products, arithmetic and copies ran while one was open for 6% of the time, Pallas kernels for 16%

profile of v2, /device:TPU:1, one launch (start us, length us, event | category | flops | bytes accessed | tf_op | source)
XLA Modules:
  0.0 192.6 jit_solution(6379207374181108215)
XLA Ops:
  3.0 6.4 %collective-permute-start.1 = (f32[32,1280]{1,0:T(8,128)}, f32[32,1280]{1,0:T(8,128)}, u32[]{:S(2)}, u32[]{:S(2)}) collective-permute-start(f32[32,1280]{1,0:T(8,128)} %pad_maximum_fusion.1), channel_id=1, source_target_pairs={{0,50},{16,0},{32,16},{48,32},{2,48},{18,2},{34,18},{50,34},{1,51}... | collective-permute-start | bytes 491528 | tf_op jit(solution)/shard_map/ppermute | solution.py:303
  11.0 4.5 %collective-permute-start.4 = (f32[32,1280]{1,0:T(8,128)}, f32[32,1280]{1,0:T(8,128)S(1)}, u32[]{:S(2)}, u32[]{:S(2)}) collective-permute-start(f32[32,1280]{1,0:T(8,128)} %pad_maximum_fusion.1), channel_id=1, source_target_pairs={{0,2},{16,18},{32,34},{48,50},{2,0},{18,16},{34,32},{50,48},{1,3},... | collective-permute-start | bytes 491528 | tf_op jit(solution)/shard_map/ppermute | solution.py:303
  15.5 2.2 %broadcast_in_dim.4 = f32[16,32,768]{2,1,0:T(8,128)} broadcast(f32[32,768]{1,0:T(8,128)} %param.4), dimensions={1,2} | broadcast | bytes 1671168 | tf_op jit(solution)/shard_map/broadcast_in_dim | solution.py:290
  17.7 6.9 %all-to-all-start = ((f32[16,32,768]{2,1,0:T(8,128)}), f32[16,32,768]{2,1,0:T(8,128)S(1)}, u32[]{:S(2)}, u32[]{:S(2)}) async-start(f32[16,32,768]{2,1,0:T(8,128)} %broadcast_in_dim.4), calls=%async_computation | async-start | bytes 3145728 | tf_op jit(solution)/shard_map/all_to_all | solution.py:291
  24.7 2.1 %collective-permute-start.6 = (f32[32,1280]{1,0:T(8,128)}, f32[32,1280]{1,0:T(8,128)S(1)}, u32[]{:S(2)}, u32[]{:S(2)}) collective-permute-start(f32[32,1280]{1,0:T(8,128)} %pad_maximum_fusion.1), channel_id=1, source_target_pairs={{0,32},{16,48},{32,2},{48,18},{2,34},{18,50},{34,0},{50,16},{1,33}... | collective-permute-start | bytes 491528 | tf_op jit(solution)/shard_map/ppermute | solution.py:303
  29.3 7.7 %collective-permute-done.3 = f32[32,1280]{1,0:T(8,128)} collective-permute-done((f32[32,1280]{1,0:T(8,128)}, f32[32,1280]{1,0:T(8,128)}, u32[]{:S(2)}, u32[]{:S(2)}) %collective-permute-start.3) | collective-permute-done | bytes 163872 | tf_op jit(solution)/shard_map/ppermute | solution.py:303
  38.8 6.7 %collective-permute-done.7 = f32[32,1280]{1,0:T(8,128)S(1)} collective-permute-done((f32[32,1280]{1,0:T(8,128)}, f32[32,1280]{1,0:T(8,128)S(1)}, u32[]{:S(2)}, u32[]{:S(2)}) %collective-permute-start.7) | collective-permute-done | bytes 163872 | tf_op jit(solution)/shard_map/ppermute | solution.py:303
  47.1 2.1 %collective-permute-start = (f32[16,32,768]{2,1,0:T(8,128)S(1)}, f32[16,32,768]{2,1,0:T(8,128)}, u32[]{:S(2)}, u32[]{:S(2)}) collective-permute-start(f32[16,32,768]{2,1,0:T(8,128)S(1)} %all-to-all-done.refs_0_), channel_id=1, source_target_pairs={{0,1},{1,0},{2,3},{3,2},{4,5},{5,4},{6,7},{7,6},{8,9},{9,8},{10,11... | collective-permute-start | bytes 4718600 | tf_op jit(solution)/shard_map/ppermute | solution.py:308
  51.3 5.3 %all-to-all-start.2 = ((f32[16,32,768]{2,1,0:T(8,128)}), f32[16,32,768]{2,1,0:T(8,128)}, u32[]{:S(2)}, u32[]{:S(2)}) async-start(f32[16,32,768]{2,1,0:T(8,128)} %broadcast_in_dim.5), calls=%async_computation.2 | async-start | bytes 3145728 | tf_op jit(solution)/shard_map/all_to_all | solution.py:291
  58.1 9.4 %shard_map.59 = (f32[512,512]{1,0:T(8,128)S(1)}, f32[16,2,32,256]{3,2,1,0:T(8,128)}) custom-call(f32[16,32,768]{2,1,0:T(8,128)S(1)} %all-to-all-done.refs_0_, f32[256,1024]{1,0:T(8,128)S(1)} %slice_dynamic-update-slice_fusion.refs_1_.refs_2_, f32[256,1024]{1,0:T(8,128)} %collective-permute-done.8.refs_2_.refs_3_, ...), custom_call_target="tpu_custom_call" | custom-call | flops 3221225472 | bytes 6291456 | tf_op jit(solution)/shard_map/pallas_call | solution.py:95
  68.5 9.6 %shard_map.60 = (f32[512,512]{1,0:T(8,128)S(1)}, f32[16,2,32,256]{3,2,1,0:T(8,128)}) custom-call(f32[16,32,768]{2,1,0:T(8,128)} %collective-permute-done.refs_0_, f32[256,1024]{1,0:T(8,128)S(1)} %slice_dynamic-update-slice_fusion.refs_1_.refs_2_, f32[256,1024]{1,0:T(8,128)} %collective-permute-done.8.refs_2_.refs_3_, ...), custom_call_target="tpu_custom_call", output_to_operand_aliasing={{1}: (4, {})} | custom-call | flops 3221225472 | bytes 6291456 | tf_op jit(solution)/shard_map/pallas_call | solution.py:95
  82.2 4.1 %all-to-all-start.1 = ((f32[16,64,256]{2,1,0:T(8,128)}), f32[16,64,256]{2,1,0:T(8,128)S(1)}, u32[]{:S(2)}, u32[]{:S(2)}) async-start(f32[16,64,256]{2,1,0:T(8,128)} %bitcast), calls=%async_computation.1 | async-start | bytes 2097152 | tf_op jit(solution)/shard_map/all_to_all | solution.py:348
  87.7 14.7 %all-to-all-done.1.parts_ref = f32[16,64,256]{2,1,0:T(8,128)S(1)} async-done(((f32[16,64,256]{2,1,0:T(8,128)}), f32[16,64,256]{2,1,0:T(8,128)S(1)}, u32[]{:S(2)}, u32[]{:S(2)}) %all-to-all-start.1) | async-done | bytes 1048608 | tf_op jit(solution)/shard_map/all_to_all | solution.py:348
  103.6 4.4 %all-to-all-start.3 = ((f32[16,64,256]{2,1,0:T(8,128)}), f32[16,64,256]{2,1,0:T(8,128)S(1)}, u32[]{:S(2)}, u32[]{:S(2)}) async-start(f32[16,64,256]{2,1,0:T(8,128)} %get-tuple-element.25), calls=%async_computation.3 | async-start | bytes 2097152 | tf_op jit(solution)/shard_map/all_to_all | solution.py:350
  108.0 2.2 %pad_maximum_fusion.refs_1_ = f32[32,32,768]{2,1,0:T(8,128)S(1)} fusion(f32[16,32,768]{2,1,0:T(8,128)} %collective-permute-done.11, f32[16,32,768]{2,1,0:T(8,128)} %all-to-all-done.2), kind=kLoop, calls=%fused_computation | loop fusion | flops 786432 | bytes 6291456 | tf_op jit(solution)/shard_map/concatenate | solution.py:353
  110.2 9.8 %shard_map.62 = (f32[1024,512]{1,0:T(8,128)S(1)}, f32[8,256]{1,0:T(8,128)S(1)}) custom-call(s32[1]{0:T(128)S(6)} %mul.7.refs_0_, f32[32,32,768]{2,1,0:T(8,128)S(1)} %pad_maximum_fusion.refs_1_, f32[256,1024]{1,0:T(8,128)S(1)} %slice_dynamic-update-slice_fusion.refs_1_.refs_2_, f32[256,1024]{1,0:T(8,128)} %collective-permute-done.8.refs_2_.refs_3_), custom_call_target="tpu_custom_call" | custom-call | flops 4831838208 | bytes 7340032 | tf_op jit(solution)/shard_map/pallas_call | solution.py:140
  125.3 2.1 %shard_map.63 = f32[8,72,256]{2,1,0:T(8,128)S(1)} custom-call(s32[1]{0:T(128)} %bitcast.1.refs_0_, f32[512,512]{1,0:T(8,128)S(1)} %copy-done.3, f32[512,512]{1,0:T(8,128)S(1)} %copy-done.5, f32[16,64,256]{2,1,0:T(8,128)S(1)} %all-to-all-done.3.refs_3_, f32[8,256]{1,0:T(8,128)S(1)} %get-tuple-element.26.refs_4_), custom_call_target="tpu_custom_call" | custom-call | flops 1610612736 | bytes 4194304 | tf_op jit(solution)/shard_map/pallas_call | solution.py:199
  127.5 18.4 %all_to_all.35.parts_ref = f32[8,72,256]{2,1,0:T(8,128)S(1)} all-to-all(f32[8,72,256]{2,1,0:T(8,128)S(1)} %shard_map.63), channel_id=1, replica_groups=mesh['x'=4,'z_lo'=4,'y'=4,'z_hi'=2,'core'=2] {'z_hi','z_lo'}, dimensions={0} | all-to-all | bytes 1179648 | tf_op jit(solution)/shard_map/all_to_all | solution.py:357
  145.9 17.1 %all_to_all.36.refs_2_ = f32[8,64,256]{2,1,0:T(8,128)S(1)} all-to-all(f32[8,64,256]{2,1,0:T(8,128)S(1)} %get-tuple-element.27), channel_id=1, replica_groups=mesh['x'=4,'z_lo'=4,'y'=4,'z_hi'=2,'core'=2] {'z_hi','z_lo'}, dimensions={0} | all-to-all | bytes 1048576 | tf_op jit(solution)/shard_map/all_to_all | solution.py:359
  163.0 3.0 %shard_map.65 = f32[16,72,256]{2,1,0:T(8,128)} custom-call(s32[1]{0:T(128)} %bitcast.1.refs_0_, f32[1024,512]{1,0:T(8,128)S(1)} %copy-done.1, f32[8,64,256]{2,1,0:T(8,128)S(1)} %all_to_all.36.refs_2_, f32[8,256]{1,0:T(8,128)S(1)} %get-tuple-element.28.refs_3_), custom_call_target="tpu_custom_call" | custom-call | flops 1610612736 | bytes 4194304 | tf_op jit(solution)/shard_map/pallas_call | solution.py:256
  166.0 5.3 %all-to-all-start.6 = ((f32[16,72,256]{2,1,0:T(8,128)}), f32[16,72,256]{2,1,0:T(8,128)S(1)}, u32[]{:S(2)}, u32[]{:S(2)}) async-start(f32[16,72,256]{2,1,0:T(8,128)} %shard_map.65), calls=%async_computation.6 | async-start | bytes 2359296 | tf_op jit(solution)/shard_map/all_to_all | solution.py:360
  171.3 5.9 %collective-permute-start.10 = (f32[32,256]{1,0:T(8,128)S(1)}, f32[32,256]{1,0:T(8,128)S(1)}, u32[]{:S(2)}, u32[]{:S(2)}) collective-permute-start(f32[32,256]{1,0:T(8,128)S(1)} %slice.87), channel_id=1, source_target_pairs={{0,1},{1,0},{2,3},{3,2},{4,5},{5,4},{6,7},{7,6},{8,9},{9,8},{10,11... | collective-permute-start | bytes 98312 | tf_op jit(solution)/shard_map/ppermute | solution.py:308
  178.0 5.9 %all-to-all-done.6.refs_0_ = f32[16,72,256]{2,1,0:T(8,128)S(1)} async-done(((f32[16,72,256]{2,1,0:T(8,128)}), f32[16,72,256]{2,1,0:T(8,128)S(1)}, u32[]{:S(2)}, u32[]{:S(2)}) %all-to-all-start.6) | async-done | bytes 1179680 | tf_op jit(solution)/shard_map/all_to_all | solution.py:360
  184.0 7.1 %collective-permute-start.12 = (f32[32,256]{1,0:T(8,128)S(1)}, f32[32,256]{1,0:T(8,128)S(1)}, u32[]{:S(2)}, u32[]{:S(2)}) collective-permute-start(f32[32,256]{1,0:T(8,128)S(1)} %slice.105), channel_id=1, source_target_pairs={{0,1},{1,0},{2,3},{3,2},{4,5},{5,4},{6,7},{7,6},{8,9},{9,8},{10,11... | collective-permute-start | bytes 98312 | tf_op jit(solution)/shard_map/ppermute | solution.py:308
  (70 shorter events, 29.0 us)
Async XLA Ops:
  3.0 21.7 %collective-permute-start.1 = (f32[32,1280]{1,0:T(8,128)}, f32[32,1280]{1,0:T(8,128)}, u32[]{:S(2)}, u32[]{:S(2)}) collective-permute-start(f32[32,1280]{1,0:T(8,128)} %pad_maximum_fusion.1), channel_id=1, source_target_pairs={{0,50},{16,0},{32,16},{48,32},{2,48},{18,2},{34,18},{50,34},{1,51}... | collective-permute-start | bytes 491528 | tf_op jit(solution)/shard_map/ppermute | solution.py:303
  9.4 18.3 %collective-permute-start.2 = (f32[32,1280]{1,0:T(8,128)}, f32[32,1280]{1,0:T(8,128)S(1)}, u32[]{:S(2)}, u32[]{:S(2)}) collective-permute-start(f32[32,1280]{1,0:T(8,128)} %pad_maximum_fusion.1), channel_id=1, source_target_pairs={{0,34},{16,50},{32,0},{48,16},{2,32},{18,48},{34,2},{50,18},{1,35}... | collective-permute-start | bytes 491528 | tf_op jit(solution)/shard_map/ppermute | solution.py:303
  10.6 26.4 %collective-permute-start.3 = (f32[32,1280]{1,0:T(8,128)}, f32[32,1280]{1,0:T(8,128)}, u32[]{:S(2)}, u32[]{:S(2)}) collective-permute-start(f32[32,1280]{1,0:T(8,128)} %pad_maximum_fusion.1), channel_id=1, source_target_pairs={{0,18},{16,34},{32,50},{48,0},{2,16},{18,32},{34,48},{50,2},{1,19}... | collective-permute-start | bytes 491528 | tf_op jit(solution)/shard_map/ppermute | solution.py:303
  11.0 26.9 %collective-permute-start.4 = (f32[32,1280]{1,0:T(8,128)}, f32[32,1280]{1,0:T(8,128)S(1)}, u32[]{:S(2)}, u32[]{:S(2)}) collective-permute-start(f32[32,1280]{1,0:T(8,128)} %pad_maximum_fusion.1), channel_id=1, source_target_pairs={{0,2},{16,18},{32,34},{48,50},{2,0},{18,16},{34,32},{50,48},{1,3},... | collective-permute-start | bytes 491528 | tf_op jit(solution)/shard_map/ppermute | solution.py:303
  15.5 22.5 %collective-permute-start.5 = (f32[32,1280]{1,0:T(8,128)}, f32[32,1280]{1,0:T(8,128)S(1)}, u32[]{:S(2)}, u32[]{:S(2)}) collective-permute-start(f32[32,1280]{1,0:T(8,128)} %pad_maximum_fusion.1), channel_id=1, source_target_pairs={{0,48},{16,2},{32,18},{48,34},{2,50},{18,0},{34,16},{50,32},{1,49}... | collective-permute-start | bytes 491528 | tf_op jit(solution)/shard_map/ppermute | solution.py:303
  17.7 6.9 %copy-start.6 = (f32[32,768]{1,0:T(8,128)S(1)}, f32[32,768]{1,0:T(8,128)}, u32[]{:S(2)}) copy-start(f32[32,768]{1,0:T(8,128)} %param.5) | copy-start | bytes 294916
  17.7 29.4 %all-to-all-start = ((f32[16,32,768]{2,1,0:T(8,128)}), f32[16,32,768]{2,1,0:T(8,128)S(1)}, u32[]{:S(2)}, u32[]{:S(2)}) async-start(f32[16,32,768]{2,1,0:T(8,128)} %broadcast_in_dim.4), calls=%async_computation | async-start | bytes 3145728 | tf_op jit(solution)/shard_map/all_to_all | solution.py:291
  24.7 14.1 %collective-permute-start.6 = (f32[32,1280]{1,0:T(8,128)}, f32[32,1280]{1,0:T(8,128)S(1)}, u32[]{:S(2)}, u32[]{:S(2)}) collective-permute-start(f32[32,1280]{1,0:T(8,128)} %pad_maximum_fusion.1), channel_id=1, source_target_pairs={{0,32},{16,48},{32,2},{48,18},{2,34},{18,50},{34,0},{50,16},{1,33}... | collective-permute-start | bytes 491528 | tf_op jit(solution)/shard_map/ppermute | solution.py:303
  27.7 17.8 %collective-permute-start.7 = (f32[32,1280]{1,0:T(8,128)}, f32[32,1280]{1,0:T(8,128)S(1)}, u32[]{:S(2)}, u32[]{:S(2)}) collective-permute-start(f32[32,1280]{1,0:T(8,128)} %pad_maximum_fusion.1), channel_id=1, source_target_pairs={{0,16},{16,32},{32,48},{48,2},{2,18},{18,34},{34,50},{50,0},{1,17}... | collective-permute-start | bytes 491528 | tf_op jit(solution)/shard_map/ppermute | solution.py:303
  38.8 7.5 %copy-start.7 = (f32[32,1280]{1,0:T(8,128)}, f32[32,1280]{1,0:T(8,128)S(1)}, u32[]{:S(2)}) copy-start(f32[32,1280]{1,0:T(8,128)S(1)} %collective-permute-done.6) | copy-start | bytes 491524
  45.6 12.5 %collective-permute-start.8 = (f32[256,1024]{1,0:T(8,128)S(1)}, f32[256,1024]{1,0:T(8,128)}, u32[]{:S(2)}, u32[]{:S(2)}) collective-permute-start(f32[256,1024]{1,0:T(8,128)S(1)} %slice_dynamic-update-slice_fusion.refs_1_.refs_2_), channel_id=1, source_target_pairs={{0,1},{1,0},{2,3},{3,2},{4,5},{5,4},{6,7},{7,6},{8,9},{9,8},{10,11... | collective-permute-start | bytes 3145736 | tf_op jit(solution)/shard_map/ppermute | solution.py:308
  47.1 21.4 %collective-permute-start = (f32[16,32,768]{2,1,0:T(8,128)S(1)}, f32[16,32,768]{2,1,0:T(8,128)}, u32[]{:S(2)}, u32[]{:S(2)}) collective-permute-start(f32[16,32,768]{2,1,0:T(8,128)S(1)} %all-to-all-done.refs_0_), channel_id=1, source_target_pairs={{0,1},{1,0},{2,3},{3,2},{4,5},{5,4},{6,7},{7,6},{8,9},{9,8},{10,11... | collective-permute-start | bytes 4718600 | tf_op jit(solution)/shard_map/ppermute | solution.py:308
  51.3 29.0 %all-to-all-start.2 = ((f32[16,32,768]{2,1,0:T(8,128)}), f32[16,32,768]{2,1,0:T(8,128)}, u32[]{:S(2)}, u32[]{:S(2)}) async-start(f32[16,32,768]{2,1,0:T(8,128)} %broadcast_in_dim.5), calls=%async_computation.2 | async-start | bytes 3145728 | tf_op jit(solution)/shard_map/all_to_all | solution.py:291
  79.1 7.2 %copy-start.9 = (f32[32,512]{1,0:T(8,128)S(1)}, f32[32,512]{1,0:T(8,128)}, u32[]{:S(2)}) copy-start(f32[32,512]{1,0:T(8,128)} %param.6) | copy-start | bytes 196612
  80.3 27.7 %collective-permute-start.11 = (f32[16,32,768]{2,1,0:T(8,128)}, f32[16,32,768]{2,1,0:T(8,128)}, u32[]{:S(2)}, u32[]{:S(2)}) collective-permute-start(f32[16,32,768]{2,1,0:T(8,128)} %all-to-all-done.2), channel_id=1, source_target_pairs={{0,1},{1,0},{2,3},{3,2},{4,5},{5,4},{6,7},{7,6},{8,9},{9,8},{10,11... | collective-permute-start | bytes 4718600 | tf_op jit(solution)/shard_map/ppermute | solution.py:308
  82.2 20.2 %all-to-all-start.1 = ((f32[16,64,256]{2,1,0:T(8,128)}), f32[16,64,256]{2,1,0:T(8,128)S(1)}, u32[]{:S(2)}, u32[]{:S(2)}) async-start(f32[16,64,256]{2,1,0:T(8,128)} %bitcast), calls=%async_computation.1 | async-start | bytes 2097152 | tf_op jit(solution)/shard_map/all_to_all | solution.py:348
  86.4 1.4 collective-permute-start.9
  103.6 19.3 %all-to-all-start.3 = ((f32[16,64,256]{2,1,0:T(8,128)}), f32[16,64,256]{2,1,0:T(8,128)S(1)}, u32[]{:S(2)}, u32[]{:S(2)}) async-start(f32[16,64,256]{2,1,0:T(8,128)} %get-tuple-element.25), calls=%async_computation.3 | async-start | bytes 2097152 | tf_op jit(solution)/shard_map/all_to_all | solution.py:350
  119.9 1.4 copy-start
  122.9 1.2 copy-start.3
  127.4 35.6 %copy-start.1 = (f32[1024,512]{1,0:T(8,128)S(1)}, f32[1024,512]{1,0:T(8,128)}, u32[]{:S(2)}) copy-start(f32[1024,512]{1,0:T(8,128)} %copy-done) | copy-start | bytes 6291460
  166.0 17.9 %all-to-all-start.6 = ((f32[16,72,256]{2,1,0:T(8,128)}), f32[16,72,256]{2,1,0:T(8,128)S(1)}, u32[]{:S(2)}, u32[]{:S(2)}) async-start(f32[16,72,256]{2,1,0:T(8,128)} %shard_map.65), calls=%async_computation.6 | async-start | bytes 2359296 | tf_op jit(solution)/shard_map/all_to_all | solution.py:360
  171.3 6.7 %collective-permute-start.10 = (f32[32,256]{1,0:T(8,128)S(1)}, f32[32,256]{1,0:T(8,128)S(1)}, u32[]{:S(2)}, u32[]{:S(2)}) collective-permute-start(f32[32,256]{1,0:T(8,128)S(1)} %slice.87), channel_id=1, source_target_pairs={{0,1},{1,0},{2,3},{3,2},{4,5},{5,4},{6,7},{7,6},{8,9},{9,8},{10,11... | collective-permute-start | bytes 98312 | tf_op jit(solution)/shard_map/ppermute | solution.py:308
  184.0 7.9 %collective-permute-start.12 = (f32[32,256]{1,0:T(8,128)S(1)}, f32[32,256]{1,0:T(8,128)S(1)}, u32[]{:S(2)}, u32[]{:S(2)}) collective-permute-start(f32[32,256]{1,0:T(8,128)S(1)} %slice.105), channel_id=1, source_target_pairs={{0,1},{1,0},{2,3},{3,2},{4,5},{5,4},{6,7},{7,6},{8,9},{9,8},{10,11... | collective-permute-start | bytes 98312 | tf_op jit(solution)/shard_map/ppermute | solution.py:308
  (4 other events, 4.0 us)

commit v3 on v1

v3 whole, which is shorter than its diff:
```python
import functools
import math

import jax
import jax.numpy as jnp
from jax import lax
from jax.experimental import pallas as pl
from jax.experimental.pallas import tpu as pltpu
from jax.sharding import Mesh
from jax.sharding import PartitionSpec as P

length_scale = 0.5
softening = 0.01
plane = ("x", "y")
ring = ("z_hi", "z_lo")
swap = [(0, 1), (1, 0)]
rider = 8
vmem_bytes = 24 * 1024 * 1024
most_bytes = 60 * 1024 * 1024


def whole(space=pltpu.VMEM):
    return pl.BlockSpec(memory_space=space)


def params(size=vmem_bytes):
    return pltpu.CompilerParams(vmem_limit_bytes=size)


def shape(sizes, dtype=jnp.float32):
    return jax.ShapeDtypeStruct(sizes, dtype)


def cost(flops, moved, transcendentals=0):
    return pl.CostEstimate(flops=flops, bytes_accessed=moved, transcendentals=transcendentals)


def dot(left, right, left_dim, right_dim):
    return lax.dot_general(
        left,
        right,
        (((left_dim,), (right_dim,)), ((), ())),
        precision=lax.Precision.HIGHEST,
        preferred_element_type=jnp.float32,
    )


def flat(value):
    return value.reshape(-1, value.shape[-1])


def high(value):
    return value.astype(jnp.bfloat16)


def cut(value, count):
    terms = []
    for _ in range(count):
        terms.append(high(value))
        value = value - terms[-1].astype(jnp.float32)
    return terms


def mul(left, right, left_dim, right_dim):
    return lax.dot_general(
        left, right, (((left_dim,), (right_dim,)), ((), ())), preferred_element_type=jnp.float32
    )


def mul_terms(left, right, left_dim, right_dim):
    count = len(left)
    total = None
    for order in reversed(range(count)):
        for place in range(order + 1):
            term = mul(left[place], right[order - place], left_dim, right_dim)
            total = term if total is None else total + term
    return total


def tile_block(left, left_norms, right_refs, norm_ref, columns):
    inner = mul_terms(left, [ref[columns, :] for ref in right_refs], 1, 1)
    squared = left_norms + norm_ref[:1, columns] - 2.0 * inner
    return jnp.exp(-jnp.sqrt(squared + softening) / length_scale)


def square_sums(rows):
    return jnp.sum(rows * rows, axis=1, keepdims=True)


def tile_kernel(half, which, rows_ref, own_ref, other_ref, out_ref, *refs):
    left_ref, right_bufs, right_refs, norm_ref, tile_ref, come, leave = refs[0], refs[1:3], refs[3:6], *refs[6:]
    count, each, depth = left_ref.shape
    moves = []

    def start(source, target):
        moves.append(pltpu.make_async_copy(source, target, come.at[len(moves)]))
        moves[-1].start()

    columns = pl.ds(half, depth)
    start(own_ref.at[:, columns], right_bufs[0])
    middle = count // 2
    for part in (pl.ds(0, middle), pl.ds(middle, count - middle)):
        start(rows_ref.at[part, which], left_ref.at[part])
    start(other_ref.at[:, columns], right_bufs[1])
    gone = []
    for place, move in ((0, moves[0]), (1, moves[3])):
        centres = own_ref.shape[0]
        columns = pl.ds(place * centres, centres)
        move.wait()
        right = right_bufs[place][...]
        for term, ref in zip(cut(right, 3), right_refs):
            ref[columns, :] = term
        ones = jnp.ones((8, depth), jnp.float32)
        norm_ref[:, columns] = dot(ones, right * right, 1, 1)
        if place == 0:
            moves[1].wait()
            moves[2].wait()
            left = flat(left_ref[...])
            left_norms = square_sums(left)
            left = cut(left, 3)
        tile_ref[:, columns] = tile_block(left, left_norms, right_refs, norm_ref, columns)
        gone.append(pltpu.make_async_copy(tile_ref.at[:, columns], out_ref.at[:, columns], leave.at[place]))
        gone[-1].start()
    for move in gone:
        move.wait()


def tile_of(rows, which, own, other, half):
    count, _, each, depth = rows.shape
    columns = 2 * own.shape[0]
    return pl.pallas_call(
        functools.partial(tile_kernel, half, which),
        in_specs=[whole(pl.ANY)] * 3,
        out_specs=whole(pl.ANY),
        out_shape=shape((count * each, columns)),
        scratch_shapes=[pltpu.VMEM((count, each, depth), jnp.float32)]
        + [pltpu.VMEM((columns // 2, depth), jnp.float32)] * 2
        + [pltpu.VMEM((columns, depth), jnp.bfloat16)] * 3
        + [pltpu.VMEM((8, columns), jnp.float32), pltpu.VMEM((count * each, columns), jnp.float32)]
        + [pltpu.SemaphoreType.DMA((4,)), pltpu.SemaphoreType.DMA((2,))],
        compiler_params=params(most_bytes),
        cost_estimate=cost(12 * count * each * columns * depth, 8 * 1024 * 1024, 2 * count * each * columns),
    )(rows, own, other)


def swapped(rows):
    half = rows.shape[-1] // 2
    return jnp.concatenate([rows[:, half:], rows[:, :half]], axis=1)


def predict_kernel(core, tile_ref, mine_ref, held_ref, *refs):
    pred_ref, tile_buf, mine_buf, theirs_buf, pred_buf, come, leave = refs[-7:]
    count, each, half = pred_buf.shape
    pairs = [
        (mine_ref, mine_buf),
        (held_ref.at[:, pl.ds(0, half)], theirs_buf),
        (tile_ref, tile_buf),
    ]
    moves = [pltpu.make_async_copy(*pair, come.at[place]) for place, pair in enumerate(pairs)]
    for move in moves:
        move.start()
    moves[0].wait()
    moves[1].wait()
    weights = [mine_buf[...], theirs_buf[...]]
    if core:
        weights = weights[::-1]
    weights = cut(jnp.concatenate(weights, axis=0), 2)
    moves[2].wait()
    pred_buf[...] = mul_terms(cut(tile_buf[...], 2), weights, 1, 0).reshape(pred_buf.shape)
    move = pltpu.make_async_copy(pred_buf, pred_ref.at[:, pl.ds(core * each, each)], leave)
    move.start()
    move.wait()


def predict(core, tile, mine, held, count, before=()):
    each, half = tile.shape[0] // count, mine.shape[1]
    return pl.pallas_call(
        functools.partial(predict_kernel, core),
        in_specs=[whole(pl.ANY)] * (3 + len(before)),
        out_specs=whole(pl.ANY),
        out_shape=shape((count, 2 * each, half)),
        scratch_shapes=[
            pltpu.VMEM(tile.shape, jnp.float32),
            pltpu.VMEM(mine.shape, jnp.float32),
            pltpu.VMEM(mine.shape, jnp.float32),
            pltpu.VMEM((count, each, half), jnp.float32),
            pltpu.SemaphoreType.DMA((3,)),
            pltpu.SemaphoreType.DMA,
        ],
        input_output_aliases={3: 0} if before else {},
        compiler_params=params(most_bytes),
        cost_estimate=cost(6 * tile.size * half, 3 * 1024 * 1024),
    )(tile, mine, held, *before)


def settle_kernel(parts_ref, target_ref, copies_ref):
    residual = jnp.sum(parts_ref[...], axis=0) - target_ref[...]
    copies_ref[...] = jnp.broadcast_to(residual[None], copies_ref.shape)


def settle(parts, target):
    return pl.pallas_call(
        settle_kernel,
        in_specs=[whole(), whole()],
        out_specs=whole(),
        out_shape=shape(parts.shape),
        compiler_params=params(),
        cost_estimate=cost(2 * parts.size, 8 * parts.size),
    )(parts, target)


def far_terms_kernel(place_ref, own_ref, other_ref, high_ref, low_ref, sums_ref):
    count, columns = own_ref.shape
    total = None
    for core, ref in enumerate((own_ref, other_ref)):
        tile = swapped(ref[...]) if core else ref[...]
        for term, out in zip(cut(tile, 2), (high_ref, low_ref)):
            out[core * count : (core + 1) * count, :] = term
        part = jnp.sum(tile, axis=0, keepdims=True)
        total = part if total is None else total + part
    middle = columns // 2
    sums = [total[:, :middle], total[:, middle:], jnp.zeros((rider - 2, middle), jnp.float32)]
    sums_ref[...] = pltpu.roll(jnp.concatenate(sums, axis=0), place_ref[0], 1)


def far_terms(shift, own, other):
    count, columns = own.shape
    return pl.pallas_call(
        far_terms_kernel,
        in_specs=[whole(pltpu.SMEM), whole(), whole()],
        out_specs=[whole()] * 3,
        out_shape=[shape((2 * count, columns), jnp.bfloat16)] * 2 + [shape((rider, columns // 2))],
        compiler_params=params(),
        cost_estimate=cost(8 * own.size, 16 * own.size),
    )(shift, own, other)


def gradient_kernel(place_ref, own_ref, other_ref, residual_ref, sums_ref, out_ref):
    count = out_ref.shape[0]
    rows = residual_ref.shape[1] // 2
    own = mul_terms(cut(own_ref[...], 2), cut(flat(residual_ref[:, :rows]), 2), 0, 0)
    other = mul_terms(cut(other_ref[...], 2), cut(flat(residual_ref[:, rows:]), 2), 0, 0)
    middle = count * rows
    total = own + jnp.concatenate([other[middle:], other[:middle]], axis=0)
    for step in range(count):
        place = lax.rem(place_ref[0] + step, count)
        out_ref[place, :rows] = total[step * rows : (step + 1) * rows]
        out_ref[place, rows : 2 * rows] = total[middle + step * rows : middle + (step + 1) * rows]
        out_ref[place, 2 * rows :] = sums_ref[...]


def gradient(place, tiles, residual, sums):
    _, rows, half = residual.shape
    count = tiles[0].shape[1] // rows
    return pl.pallas_call(
        gradient_kernel,
        in_specs=[whole(pltpu.SMEM)] + [whole()] * 4,
        out_specs=whole(),
        out_shape=shape((count, rows + rider, half)),
        compiler_params=params(),
        cost_estimate=cost(12 * tiles[0].size * half, 4 * 1024 * 1024),
    )(place, *tiles, residual, sums)


def collect_kernel(parts_ref, grad_ref, copies_ref, largest_ref):
    rows = grad_ref.shape[0]
    total = jnp.sum(parts_ref[...], axis=0)
    grad_ref[...] = total[:rows]
    copies_ref[...] = jnp.broadcast_to(total[None, :rows], copies_ref.shape)
    largest = jnp.max(jnp.max(total[rows:], axis=0, keepdims=True), axis=1, keepdims=True)
    largest_ref[...] = jnp.broadcast_to(largest, largest_ref.shape)


def collect(parts):
    count, packed, half = parts.shape
    rows = packed - rider
    return pl.pallas_call(
        collect_kernel,
        in_specs=[whole()],
        out_specs=[whole()] * 3,
        out_shape=[
            shape((rows, half), jnp.float32),
            shape((count, rows, half), jnp.float32),
            shape((rider, half), jnp.float32),
        ],
        compiler_params=params(),
        cost_estimate=cost(2 * parts.size, 8 * parts.size),
    )(parts)


def product_kernel(place_ref, high_ref, low_ref, grad_ref, largest_ref, out_ref):
    count, rows, half = grad_ref.shape
    rows = rows // 2
    places = [lax.rem(place_ref[0] + step, count) for step in range(count)]
    grads = [grad_ref[place, :rows] for place in places] + [grad_ref[place, rows:] for place in places]
    total = mul_terms([high_ref[...], low_ref[...]], cut(jnp.concatenate(grads, axis=0), 2), 1, 0)
    middle = total.shape[0] // 2
    for core in range(2):
        part = total[core * middle : (core + 1) * middle]
        out_ref[:, core * rows : (core + 1) * rows] = part.reshape(-1, rows, half)
    out_ref[:, 2 * rows :] = jnp.broadcast_to(largest_ref[...][None], (out_ref.shape[0], rider, half))


def product(place, terms, grads, largest):
    _, rows, half = grads.shape
    count = terms[0].shape[0] // rows
    return pl.pallas_call(
        product_kernel,
        in_specs=[whole(pltpu.SMEM)] + [whole()] * 4,
        out_specs=whole(),
        out_shape=shape((count, rows + rider, half)),
        compiler_params=params(),
        cost_estimate=cost(6 * terms[0].size * half, 4 * 1024 * 1024),
    )(place, *terms, grads, largest)


def finish_kernel(scale, parts_ref, grad_ref, theta_ref):
    rows = grad_ref.shape[0]
    total = jnp.sum(parts_ref[:, :rows], axis=0)
    largest = jnp.max(parts_ref[:, rows:], axis=0)
    largest = jnp.max(jnp.max(largest, axis=0, keepdims=True), axis=1, keepdims=True)
    step_size = 1.0 / largest
    theta_ref[...] = (2.0 * step_size * grad_ref[...] - step_size * step_size * total) * scale


def finish(parts, grad, scale):
    def body(*refs):
        finish_kernel(scale, *refs)

    return pl.pallas_call(
        body,
        in_specs=[whole(), whole()],
        out_specs=whole(),
        out_shape=shape(grad.shape),
        compiler_params=params(),
        cost_estimate=cost(2 * parts.size, 4 * parts.size),
    )(parts, grad)


def assemble_kernel(count, *refs):
    own_ref, mine_ref = refs[count:]
    for place, ref in enumerate(refs[:count]):
        rows = ref.shape[0]
        edge = own_ref.shape[1]
        own_ref[place * rows : (place + 1) * rows, :] = ref[:, :edge]
        mine_ref[place * rows : (place + 1) * rows, :] = ref[:, edge:]


def assemble(pieces, edge):
    count = len(pieces)
    rows, width = pieces[0].shape

    def body(*refs):
        assemble_kernel(count, *refs)

    return pl.pallas_call(
        body,
        in_specs=[whole()] * count,
        out_specs=[whole()] * 2,
        out_shape=[
            shape((count * rows, edge)),
            shape((count * rows, width - edge)),
        ],
        compiler_params=params(),
        cost_estimate=cost(0, 8 * count * rows * width),
    )(*pieces)


def gather(value, axis):
    copies = jnp.broadcast_to(value[None], (lax.axis_size(axis),) + value.shape)
    return lax.all_to_all(copies, axis, 0, 0)


def ring_pieces(value):
    count, low = lax.axis_size(ring), lax.axis_size("z_lo")

    def slot(place):
        return place % low * (count // low) + place // low

    def hop(held, step):
        pairs = [(slot(place), slot((place + step) % count)) for place in range(count)]
        return lax.ppermute(held, ("z_lo", "z_hi"), pairs)

    ahead, behind = [value], [value]
    for step in range(1, count):
        if step % 2:
            behind.append(hop(behind[-1], 1))
        else:
            ahead.append(hop(ahead[-1], -1))
    return ahead + behind[:0:-1]


def from_other(value):
    return lax.ppermute(value, "core", swap)


def halves(rows):
    core = lax.axis_index("core")
    half = rows.shape[1] // 2
    first, second = rows[:, :half], rows[:, half:]
    return jnp.where(core == 0, first, second), jnp.where(core == 0, second, first)


def to_rows(*columns):
    core = lax.axis_index("core")
    rows = columns[0].shape[0] // 2
    own = jnp.concatenate([value[:rows] for value in columns], axis=0)
    other = from_other(jnp.concatenate([value[rows:] for value in columns], axis=0))
    first = jnp.where(core == 0, own, other)
    second = jnp.where(core == 0, other, own)
    both = jnp.concatenate([first, second], axis=1)
    return tuple(both[place * rows : (place + 1) * rows] for place in range(len(columns)))


def shards(batch_features, centre_features, targets, weights):
    rows, width = targets.shape
    half = width // 2
    total_rows = rows * lax.axis_size(plane) * lax.axis_size(ring) * 2
    place = lax.axis_index(ring)

    count = lax.axis_size(plane)
    place = place.reshape(1).astype(jnp.int32)

    mine, theirs = halves(weights)
    pieces = ring_pieces(jnp.concatenate([theirs, centre_features, mine], axis=1))
    features = jnp.stack([batch_features, centre_features])
    features = jnp.broadcast_to(features[None], (count,) + features.shape)
    features = lax.all_to_all(features, plane, 0, 0)
    target_mine, target_theirs = halves(targets)
    target = jnp.concatenate([target_mine, from_other(target_theirs)], axis=0)
    own, mine = assemble(pieces, half + centre_features.shape[1])
    other = from_other(own)

    tile = tile_of(features, 0, own, other, half)
    tiles = tile, from_other(tile)
    pred = predict(0, tiles[0], mine, other, count)
    pred = predict(1, tiles[1], mine, other, count, (pred,))
    far = tile_of(features, 1, own, other, half)
    *fars, sums = far_terms(place * rows, far, from_other(far))
    parts = lax.all_to_all(pred, plane, 0, 0)
    residuals = settle(parts, target)
    residual_full = lax.all_to_all(residuals, plane, 0, 0)
    parts = lax.all_to_all(gradient(place, tiles, residual_full, sums), ring, 0, 0)
    grad, copies, largest = collect(parts)
    grad_full = lax.all_to_all(copies, ring, 0, 0)
    parts = lax.all_to_all(product(place, fars, grad_full, largest), plane, 0, 0)
    theta = finish(parts, grad, total_rows / math.sqrt(total_rows))
    return to_rows(residuals[0], theta)


def solution(mesh):
    fine = Mesh(
        mesh.devices.reshape(4, 4, 4, 2, 2),
        ("x", "z_lo", "y", "z_hi", "core"),
    )
    by_batch = P(("x", "z_lo", "y", "z_hi", "core"), None)
    by_centre = P(("y", "z_hi", "core", "x", "z_lo"), None)
    return jax.shard_map(
        shards,
        mesh=fine,
        in_specs=(by_batch, by_centre, by_batch, by_centre),
        out_specs=(by_batch, by_centre),
        check_vma=False,
    )
```

time: 257 us -> 186 us (0.72)
  waiting for transfers between devices: 103 us -> 55.1 us
  blocking collectives: 0 us -> 39.2 us
  starting transfers between devices: 85.1 us -> 50.5 us
  Pallas kernels: 0 us -> 30 us
  matrix products: 23.4 us -> 0 us
  between operations: 15 us -> 0.9 us
  other arithmetic: 14.2 us -> 1.67 us
  local copies, waits for them, and re-layouts: 15.4 us -> 7.77 us
    all_to_all x11 -> x4, waiting for transfers between devices: 98.1 us -> 36.3 us  [the longest x1 12.2 us: shards(): lax.all_to_all(product(place, fars, grad_full, largest), plane, 0, 0)]
    all_to_all x0 -> x2, blocking collectives: none -> 39.2 us  [the longest x1 22.1 us: shards(): lax.all_to_all(gradient(place, tiles, residual_full, sums), ring, 0, 0)]
    pallas_call x0 -> x11, Pallas kernels: none -> 30 us  [the longest x2 17.9 us: tile_of(): pl.pallas_call(functools.partial(tile_kernel, half, which), in_specs=[who...]
    all_to_all x11 -> x4, starting transfers between devices: 53.8 us -> 25 us  [the longest x1 7.76 us: shards(): features = lax.all_to_all(features, plane, 0, 0)]
    dot_general x5 -> x0, matrix products: 23.4 us -> none  [dot(): lax.dot_general(left, right, (contract, ((), ())), precision=precision, p...]
    ppermute x7 -> x12, waiting for transfers between devices: 3.92 us -> 18.8 us  [the longest x7 15.6 us: hop(): return lax.ppermute(held, ('z_lo', 'z_hi'), pairs)]
    reduce_sum x7 -> x0, other arithmetic: 8.68 us -> none  [the longest x2 6.06 us: kernel_matrix(): left_norms = jnp.sum(left_rows * left_rows, axis=1)]
    broadcast_in_dim x7 -> x1, local copies, waits for them, and re-layouts: 8.67 us -> 2.04 us  [shards(): features = jnp.broadcast_to(features[None], (count,) + features.shape)]
  transfers between devices with their start and end apart: 19 -> 16, of which waited for: 13 -> 10; matrix products, arithmetic and copies ran while one was open for 18% -> 0% of each run, Pallas kernels for 0% -> 8%
where the time goes in v3:
time: 186 us; the launch traced here: 185 us
  waiting for transfers between devices  55.1 us (30%)
  starting transfers between devices  50.5 us (27%)
  blocking collectives  39.2 us (21%)
  Pallas kernels  30 us (16%)
  local copies, waits for them, and re-layouts  7.77 us (4%)
    all_to_all x1, blocking collectives, shards(): lax.all_to_all(gradient(place, tiles, residual_full, sums), ring, 0, 0)  22.1 us
    pallas_call x2, Pallas kernels, tile_of(): pl.pallas_call(functools.partial(tile_kernel, half, which), in_specs=[who...  17.9 us
    all_to_all x1, blocking collectives, shards(): grad_full = lax.all_to_all(copies, ring, 0, 0)  17.1 us
    ppermute x7, waiting for transfers between devices, hop(): return lax.ppermute(held, ('z_lo', 'z_hi'), pairs)  15.6 us
    ppermute x5, starting transfers between devices, from_other(): return lax.ppermute(value, 'core', swap)  14.4 us
    all_to_all x1, waiting for transfers between devices, shards(): lax.all_to_all(product(place, fars, grad_full, largest), plane, 0, 0)  12.2 us
    ppermute x7, starting transfers between devices, hop(): return lax.ppermute(held, ('z_lo', 'z_hi'), pairs)  11.1 us
    all_to_all x1, waiting for transfers between devices, shards(): residual_full = lax.all_to_all(residuals, plane, 0, 0)  9.93 us
  transfers between devices with their start and end apart: 16, of which 10 were waited for; matrix products, arithmetic and copies ran while one was open for 0% of the time, Pallas kernels for 8%

profile of v3, /device:TPU:1, one launch (start us, length us, event | category | flops | bytes accessed | tf_op | source)
XLA Modules:
  0.0 185.1 jit_solution(5134708921957687131)
XLA Ops:
  3.6 7.8 %all-to-all-start = ((f32[16,2,32,768]{3,2,1,0:T(8,128)}), f32[16,2,32,768]{3,2,1,0:T(8,128)}, u32[]{:S(2)}, u32[]{:S(2)}) async-start(f32[16,2,32,768]{3,2,1,0:T(8,128)} %broadcast_in_dim.2), calls=%async_computation | async-start | bytes 6291456 | tf_op jit(solution)/shard_map/all_to_all | solution.py:428
  13.2 4.0 %collective-permute-start = (f32[32,1280]{1,0:T(8,128)S(1)}, f32[32,1280]{1,0:T(8,128)S(1)}, u32[]{:S(2)}, u32[]{:S(2)}) collective-permute-start(f32[32,1280]{1,0:T(8,128)S(1)} %pad_maximum_fusion.1.refs_0_), channel_id=1, source_target_pairs={{0,50},{16,0},{32,16},{48,32},{2,48},{18,2},{34,18},{50,34},{1,51}... | collective-permute-start | bytes 491528 | tf_op jit(solution)/shard_map/ppermute | solution.py:382
  17.2 3.6 %collective-permute-done.3.refs_7_ = f32[32,1280]{1,0:T(8,128)S(1)} collective-permute-done((f32[32,1280]{1,0:T(8,128)S(1)}, f32[32,1280]{1,0:T(8,128)S(1)}, u32[]{:S(2)}, u32[]{:S(2)}) %collective-permute-start.3) | collective-permute-done | bytes 163872 | tf_op jit(solution)/shard_map/ppermute | solution.py:382
  20.8 2.7 %collective-permute-start.1 = (f32[32,1280]{1,0:T(8,128)S(1)}, f32[32,1280]{1,0:T(8,128)S(1)}, u32[]{:S(2)}, u32[]{:S(2)}) collective-permute-start(f32[32,1280]{1,0:T(8,128)S(1)} %collective-permute-done.refs_1_), channel_id=1, source_target_pairs={{0,50},{16,0},{32,16},{48,32},{2,48},{18,2},{34,18},{50,34},{1,51}... | collective-permute-start | bytes 491528 | tf_op jit(solution)/shard_map/ppermute | solution.py:382
  23.5 3.1 %collective-permute-done.4.refs_6_ = f32[32,1280]{1,0:T(8,128)S(1)} collective-permute-done((f32[32,1280]{1,0:T(8,128)S(1)}, f32[32,1280]{1,0:T(8,128)S(1)}, u32[]{:S(2)}, u32[]{:S(2)}) %collective-permute-start.4) | collective-permute-done | bytes 163872 | tf_op jit(solution)/shard_map/ppermute | solution.py:382
  26.6 2.7 %collective-permute-start.2 = (f32[32,1280]{1,0:T(8,128)S(1)}, f32[32,1280]{1,0:T(8,128)S(1)}, u32[]{:S(2)}, u32[]{:S(2)}) collective-permute-start(f32[32,1280]{1,0:T(8,128)S(1)} %collective-permute-done.1.refs_2_), channel_id=1, source_target_pairs={{0,50},{16,0},{32,16},{48,32},{2,48},{18,2},{34,18},{50,34},{1,51}... | collective-permute-start | bytes 491528 | tf_op jit(solution)/shard_map/ppermute | solution.py:382
  29.3 3.1 %collective-permute-done.5.refs_5_ = f32[32,1280]{1,0:T(8,128)S(1)} collective-permute-done((f32[32,1280]{1,0:T(8,128)S(1)}, f32[32,1280]{1,0:T(8,128)S(1)}, u32[]{:S(2)}, u32[]{:S(2)}) %collective-permute-start.5) | collective-permute-done | bytes 163872 | tf_op jit(solution)/shard_map/ppermute | solution.py:382
  32.4 5.8 %collective-permute-done.6.refs_4_ = f32[32,1280]{1,0:T(8,128)S(1)} collective-permute-done((f32[32,1280]{1,0:T(8,128)S(1)}, f32[32,1280]{1,0:T(8,128)S(1)}, u32[]{:S(2)}, u32[]{:S(2)}) %collective-permute-start.6) | collective-permute-done | bytes 163872 | tf_op jit(solution)/shard_map/ppermute | solution.py:382
  39.0 3.7 %collective-permute-start.7 = (f32[256,1024]{1,0:T(8,128)S(1)}, f32[256,1024]{1,0:T(8,128)S(1)}, u32[]{:S(2)}, u32[]{:S(2)}) collective-permute-start(f32[256,1024]{1,0:T(8,128)S(1)} %get-tuple-element.10.own_ref), channel_id=1, source_target_pairs={{0,1},{1,0},{2,3},{3,2},{4,5},{5,4},{6,7},{7,6},{8,9},{9,8},{10,11... | collective-permute-start | bytes 3145736 | tf_op jit(solution)/shard_map/ppermute | solution.py:394
  44.9 6.8 %all-to-all-done.rows_ref = f32[16,2,32,768]{3,2,1,0:T(8,128)} async-done(((f32[16,2,32,768]{3,2,1,0:T(8,128)}), f32[16,2,32,768]{3,2,1,0:T(8,128)}, u32[]{:S(2)}, u32[]{:S(2)}) %all-to-all-start) | async-done | bytes 3145760 | tf_op jit(solution)/shard_map/all_to_all | solution.py:428
  51.8 8.9 %shard_map.60.tile_ref.own_ref = f32[512,512]{1,0:T(8,128)} custom-call(f32[16,2,32,768]{3,2,1,0:T(8,128)} %all-to-all-done.rows_ref, f32[256,1024]{1,0:T(8,128)} %copy-done.9, f32[256,1024]{1,0:T(8,128)} %copy-done.10), custom_call_target="tpu_custom_call" | custom-call | flops 2415919104 | bytes 8388608 | tf_op jit(solution)/shard_map/pallas_call | solution.py:131
  60.7 3.4 %collective-permute-start.8 = (f32[512,512]{1,0:T(8,128)}, f32[512,512]{1,0:T(8,128)S(1)}, u32[]{:S(2)}, u32[]{:S(2)}) collective-permute-start(f32[512,512]{1,0:T(8,128)} %shard_map.60.tile_ref.own_ref), channel_id=1, source_target_pairs={{0,1},{1,0},{2,3},{3,2},{4,5},{5,4},{6,7},{7,6},{8,9},{9,8},{10,11... | collective-permute-start | bytes 3145736 | tf_op jit(solution)/shard_map/ppermute | solution.py:394
  64.1 2.8 %shard_map.61.refs_0_ = f32[16,64,256]{2,1,0:T(8,128)} custom-call(f32[512,512]{1,0:T(8,128)} %shard_map.60.tile_ref.own_ref, f32[256,256]{1,0:T(8,128)} %copy-done.8, f32[256,1024]{1,0:T(8,128)} %copy-done.10), custom_call_target="tpu_custom_call" | custom-call | flops 402653184 | bytes 3145728 | tf_op jit(solution)/shard_map/pallas_call | solution.py:177
  68.0 2.8 %shard_map.62 = f32[16,64,256]{2,1,0:T(8,128)} custom-call(f32[512,512]{1,0:T(8,128)} %copy-done, f32[256,256]{1,0:T(8,128)} %copy-done.8, f32[256,1024]{1,0:T(8,128)} %copy-done.10, f32[16,64,256]{2,1,0:T(8,128)} %shard_map.61.refs_0_), custom_call_target="tpu_custom_call", output_to_operand_aliasing={{}: (3, {})} | custom-call | flops 402653184 | bytes 3145728 | tf_op jit(solution)/shard_map/pallas_call | solution.py:177
  70.8 7.6 %all-to-all-start.1 = ((f32[16,64,256]{2,1,0:T(8,128)}), f32[16,64,256]{2,1,0:T(8,128)S(1)}, u32[]{:S(2)}, u32[]{:S(2)}) async-start(f32[16,64,256]{2,1,0:T(8,128)} %shard_map.62), calls=%async_computation.1 | async-start | bytes 2097152 | tf_op jit(solution)/shard_map/all_to_all | solution.py:440
  78.8 8.9 %shard_map.64.own_ref = f32[512,512]{1,0:T(8,128)} custom-call(f32[16,2,32,768]{3,2,1,0:T(8,128)} %all-to-all-done.rows_ref, f32[256,1024]{1,0:T(8,128)} %copy-done.9, f32[256,1024]{1,0:T(8,128)} %copy-done.10), custom_call_target="tpu_custom_call" | custom-call | flops 2415919104 | bytes 8388608 | tf_op jit(solution)/shard_map/pallas_call | solution.py:131
  88.1 7.3 %all-to-all-done.1.parts_ref = f32[16,64,256]{2,1,0:T(8,128)S(1)} async-done(((f32[16,64,256]{2,1,0:T(8,128)}), f32[16,64,256]{2,1,0:T(8,128)S(1)}, u32[]{:S(2)}, u32[]{:S(2)}) %all-to-all-start.1) | async-done | bytes 1048608 | tf_op jit(solution)/shard_map/all_to_all | solution.py:440
  96.6 3.7 %all-to-all-start.2 = ((f32[16,64,256]{2,1,0:T(8,128)}), f32[16,64,256]{2,1,0:T(8,128)S(1)}, u32[]{:S(2)}, u32[]{:S(2)}) async-start(f32[16,64,256]{2,1,0:T(8,128)} %shard_map.63), calls=%async_computation.2 | async-start | bytes 2097152 | tf_op jit(solution)/shard_map/all_to_all | solution.py:442
  105.4 9.9 %all-to-all-done.2.residual_ref = f32[16,64,256]{2,1,0:T(8,128)S(1)} async-done(((f32[16,64,256]{2,1,0:T(8,128)}), f32[16,64,256]{2,1,0:T(8,128)S(1)}, u32[]{:S(2)}, u32[]{:S(2)}) %all-to-all-start.2) | async-done | bytes 1048608 | tf_op jit(solution)/shard_map/all_to_all | solution.py:442
  116.4 22.1 %all_to_all.30.parts_ref = f32[8,72,256]{2,1,0:T(8,128)S(1)} all-to-all(f32[8,72,256]{2,1,0:T(8,128)S(1)} %shard_map.66), channel_id=1, replica_groups=mesh['x'=4,'z_lo'=4,'y'=4,'z_hi'=2,'core'=2] {'z_hi','z_lo'}, dimensions={0} | all-to-all | bytes 1179648 | tf_op jit(solution)/shard_map/all_to_all | solution.py:443
  138.6 17.1 %all_to_all.31.grad_ref = f32[8,64,256]{2,1,0:T(8,128)S(1)} all-to-all(f32[8,64,256]{2,1,0:T(8,128)S(1)} %get-tuple-element.15), channel_id=1, replica_groups=mesh['x'=4,'z_lo'=4,'y'=4,'z_hi'=2,'core'=2] {'z_hi','z_lo'}, dimensions={0} | all-to-all | bytes 1048576 | tf_op jit(solution)/shard_map/all_to_all | solution.py:445
  157.8 6.0 %all-to-all-start.5 = ((f32[16,72,256]{2,1,0:T(8,128)}), f32[16,72,256]{2,1,0:T(8,128)S(1)}, u32[]{:S(2)}, u32[]{:S(2)}) async-start(f32[16,72,256]{2,1,0:T(8,128)} %shard_map.68), calls=%async_computation.5 | async-start | bytes 2359296 | tf_op jit(solution)/shard_map/all_to_all | solution.py:446
  164.5 12.2 %all-to-all-done.5.refs_0_ = f32[16,72,256]{2,1,0:T(8,128)S(1)} async-done(((f32[16,72,256]{2,1,0:T(8,128)}), f32[16,72,256]{2,1,0:T(8,128)S(1)}, u32[]{:S(2)}, u32[]{:S(2)}) %all-to-all-start.5) | async-done | bytes 1179680 | tf_op jit(solution)/shard_map/all_to_all | solution.py:446
  176.9 6.7 %collective-permute-start.11 = (f32[64,256]{1,0:T(8,128)S(1)}, f32[64,256]{1,0:T(8,128)S(1)}, u32[]{:S(2)}, u32[]{:S(2)}) collective-permute-start(f32[64,256]{1,0:T(8,128)S(1)} %pad_maximum_fusion.5), channel_id=1, source_target_pairs={{0,1},{1,0},{2,3},{3,2},{4,5},{5,4},{6,7},{7,6},{8,9},{9,8},{10,11... | collective-permute-start | bytes 196616 | tf_op jit(solution)/shard_map/ppermute | solution.py:394
  (60 shorter events, 21.5 us)
Async XLA Ops:
  3.6 7.8 %copy-start.12 = (f32[32,512]{1,0:T(8,128)S(1)}, f32[32,512]{1,0:T(8,128)}, u32[]{:S(2)}) copy-start(f32[32,512]{1,0:T(8,128)} %param.7) | copy-start | bytes 196612
  3.6 7.8 %copy-start.11 = (f32[32,768]{1,0:T(8,128)S(1)}, f32[32,768]{1,0:T(8,128)}, u32[]{:S(2)}) copy-start(f32[32,768]{1,0:T(8,128)} %param.5) | copy-start | bytes 294916
  3.6 48.1 %all-to-all-start = ((f32[16,2,32,768]{3,2,1,0:T(8,128)}), f32[16,2,32,768]{3,2,1,0:T(8,128)}, u32[]{:S(2)}, u32[]{:S(2)}) async-start(f32[16,2,32,768]{3,2,1,0:T(8,128)} %broadcast_in_dim.2), calls=%async_computation | async-start | bytes 6291456 | tf_op jit(solution)/shard_map/all_to_all | solution.py:428
  11.5 9.4 %collective-permute-start.3 = (f32[32,1280]{1,0:T(8,128)S(1)}, f32[32,1280]{1,0:T(8,128)S(1)}, u32[]{:S(2)}, u32[]{:S(2)}) collective-permute-start(f32[32,1280]{1,0:T(8,128)S(1)} %pad_maximum_fusion.1.refs_0_), channel_id=1, source_target_pairs={{0,16},{16,32},{32,48},{48,2},{2,18},{18,34},{34,50},{50,0},{1,17}... | collective-permute-start | bytes 491528 | tf_op jit(solution)/shard_map/ppermute | solution.py:382
  13.2 7.7 %collective-permute-start = (f32[32,1280]{1,0:T(8,128)S(1)}, f32[32,1280]{1,0:T(8,128)S(1)}, u32[]{:S(2)}, u32[]{:S(2)}) collective-permute-start(f32[32,1280]{1,0:T(8,128)S(1)} %pad_maximum_fusion.1.refs_0_), channel_id=1, source_target_pairs={{0,50},{16,0},{32,16},{48,32},{2,48},{18,2},{34,18},{50,34},{1,51}... | collective-permute-start | bytes 491528 | tf_op jit(solution)/shard_map/ppermute | solution.py:382
  20.8 5.8 %collective-permute-start.4 = (f32[32,1280]{1,0:T(8,128)S(1)}, f32[32,1280]{1,0:T(8,128)S(1)}, u32[]{:S(2)}, u32[]{:S(2)}) collective-permute-start(f32[32,1280]{1,0:T(8,128)S(1)} %collective-permute-done.3.refs_7_), channel_id=1, source_target_pairs={{0,16},{16,32},{32,48},{48,2},{2,18},{18,34},{34,50},{50,0},{1,17}... | collective-permute-start | bytes 491528 | tf_op jit(solution)/shard_map/ppermute | solution.py:382
  20.8 5.8 %collective-permute-start.1 = (f32[32,1280]{1,0:T(8,128)S(1)}, f32[32,1280]{1,0:T(8,128)S(1)}, u32[]{:S(2)}, u32[]{:S(2)}) collective-permute-start(f32[32,1280]{1,0:T(8,128)S(1)} %collective-permute-done.refs_1_), channel_id=1, source_target_pairs={{0,50},{16,0},{32,16},{48,32},{2,48},{18,2},{34,18},{50,34},{1,51}... | collective-permute-start | bytes 491528 | tf_op jit(solution)/shard_map/ppermute | solution.py:382
  26.6 5.8 %collective-permute-start.5 = (f32[32,1280]{1,0:T(8,128)S(1)}, f32[32,1280]{1,0:T(8,128)S(1)}, u32[]{:S(2)}, u32[]{:S(2)}) collective-permute-start(f32[32,1280]{1,0:T(8,128)S(1)} %collective-permute-done.4.refs_6_), channel_id=1, source_target_pairs={{0,16},{16,32},{32,48},{48,2},{2,18},{18,34},{34,50},{50,0},{1,17}... | collective-permute-start | bytes 491528 | tf_op jit(solution)/shard_map/ppermute | solution.py:382
  26.6 5.8 %collective-permute-start.2 = (f32[32,1280]{1,0:T(8,128)S(1)}, f32[32,1280]{1,0:T(8,128)S(1)}, u32[]{:S(2)}, u32[]{:S(2)}) collective-permute-start(f32[32,1280]{1,0:T(8,128)S(1)} %collective-permute-done.1.refs_2_), channel_id=1, source_target_pairs={{0,50},{16,0},{32,16},{48,32},{2,48},{18,2},{34,18},{50,34},{1,51}... | collective-permute-start | bytes 491528 | tf_op jit(solution)/shard_map/ppermute | solution.py:382
  32.4 5.8 %collective-permute-start.6 = (f32[32,1280]{1,0:T(8,128)S(1)}, f32[32,1280]{1,0:T(8,128)S(1)}, u32[]{:S(2)}, u32[]{:S(2)}) collective-permute-start(f32[32,1280]{1,0:T(8,128)S(1)} %collective-permute-done.5.refs_5_), channel_id=1, source_target_pairs={{0,16},{16,32},{32,48},{48,2},{2,18},{18,34},{34,50},{50,0},{1,17}... | collective-permute-start | bytes 491528 | tf_op jit(solution)/shard_map/ppermute | solution.py:382
  39.0 12.8 %copy-start.9 = (f32[256,1024]{1,0:T(8,128)}, f32[256,1024]{1,0:T(8,128)S(1)}, u32[]{:S(2)}) copy-start(f32[256,1024]{1,0:T(8,128)S(1)} %get-tuple-element.10.own_ref) | copy-start | bytes 3145732
  39.0 6.0 %collective-permute-start.7 = (f32[256,1024]{1,0:T(8,128)S(1)}, f32[256,1024]{1,0:T(8,128)S(1)}, u32[]{:S(2)}, u32[]{:S(2)}) collective-permute-start(f32[256,1024]{1,0:T(8,128)S(1)} %get-tuple-element.10.own_ref), channel_id=1, source_target_pairs={{0,1},{1,0},{2,3},{3,2},{4,5},{5,4},{6,7},{7,6},{8,9},{9,8},{10,11... | collective-permute-start | bytes 3145736 | tf_op jit(solution)/shard_map/ppermute | solution.py:394
  60.7 6.2 %collective-permute-start.8 = (f32[512,512]{1,0:T(8,128)}, f32[512,512]{1,0:T(8,128)S(1)}, u32[]{:S(2)}, u32[]{:S(2)}) collective-permute-start(f32[512,512]{1,0:T(8,128)} %shard_map.60.tile_ref.own_ref), channel_id=1, source_target_pairs={{0,1},{1,0},{2,3},{3,2},{4,5},{5,4},{6,7},{7,6},{8,9},{9,8},{10,11... | collective-permute-start | bytes 3145736 | tf_op jit(solution)/shard_map/ppermute | solution.py:394
  66.9 11.5 %copy-start.13 = (f32[32,512]{1,0:T(8,128)S(1)}, f32[32,512]{1,0:T(8,128)}, u32[]{:S(2)}) copy-start(f32[32,512]{1,0:T(8,128)} %param.6) | copy-start | bytes 196612
  70.8 24.6 %all-to-all-start.1 = ((f32[16,64,256]{2,1,0:T(8,128)}), f32[16,64,256]{2,1,0:T(8,128)S(1)}, u32[]{:S(2)}, u32[]{:S(2)}) async-start(f32[16,64,256]{2,1,0:T(8,128)} %shard_map.62), calls=%async_computation.1 | async-start | bytes 2097152 | tf_op jit(solution)/shard_map/all_to_all | solution.py:440
  78.5 9.6 %collective-permute-start.9 = (f32[32,256]{1,0:T(8,128)S(1)}, f32[32,256]{1,0:T(8,128)S(1)}, u32[]{:S(2)}, u32[]{:S(2)}) collective-permute-start(f32[32,256]{1,0:T(8,128)S(1)} %get-tuple-element.27), channel_id=1, source_target_pairs={{0,1},{1,0},{2,3},{3,2},{4,5},{5,4},{6,7},{7,6},{8,9},{9,8},{10,11... | collective-permute-start | bytes 98312 | tf_op jit(solution)/shard_map/ppermute | solution.py:394
  87.8 12.4 %collective-permute-start.10 = (f32[512,512]{1,0:T(8,128)}, f32[512,512]{1,0:T(8,128)}, u32[]{:S(2)}, u32[]{:S(2)}) collective-permute-start(f32[512,512]{1,0:T(8,128)} %shard_map.64.own_ref), channel_id=1, source_target_pairs={{0,1},{1,0},{2,3},{3,2},{4,5},{5,4},{6,7},{7,6},{8,9},{9,8},{10,11... | collective-permute-start | bytes 3145736 | tf_op jit(solution)/shard_map/ppermute | solution.py:394
  88.1 27.2 %copy-start.1 = (f32[512,512]{1,0:T(8,128)S(1)}, f32[512,512]{1,0:T(8,128)}, u32[]{:S(2)}) copy-start(f32[512,512]{1,0:T(8,128)} %copy-done) | copy-start | bytes 3145732
  88.1 27.2 %copy-start.2 = (f32[512,512]{1,0:T(8,128)S(1)}, f32[512,512]{1,0:T(8,128)}, u32[]{:S(2)}) copy-start(f32[512,512]{1,0:T(8,128)} %shard_map.60.tile_ref.own_ref) | copy-start | bytes 3145732
  96.6 18.7 %all-to-all-start.2 = ((f32[16,64,256]{2,1,0:T(8,128)}), f32[16,64,256]{2,1,0:T(8,128)S(1)}, u32[]{:S(2)}, u32[]{:S(2)}) async-start(f32[16,64,256]{2,1,0:T(8,128)} %shard_map.63), calls=%async_computation.2 | async-start | bytes 2097152 | tf_op jit(solution)/shard_map/all_to_all | solution.py:442
  115.3 40.4 %copy-start.5 = (bf16[1024,512]{1,0:T(8,128)(2,1)S(1)}, bf16[1024,512]{1,0:T(8,128)(2,1)}, u32[]{:S(2)}) copy-start(bf16[1024,512]{1,0:T(8,128)(2,1)} %copy-done.4) | copy-start | bytes 3145732
  115.3 40.4 %copy-start.7 = (bf16[1024,512]{1,0:T(8,128)(2,1)S(1)}, bf16[1024,512]{1,0:T(8,128)(2,1)}, u32[]{:S(2)}) copy-start(bf16[1024,512]{1,0:T(8,128)(2,1)} %copy-done.6) | copy-start | bytes 3145732
  157.8 18.9 %all-to-all-start.5 = ((f32[16,72,256]{2,1,0:T(8,128)}), f32[16,72,256]{2,1,0:T(8,128)S(1)}, u32[]{:S(2)}, u32[]{:S(2)}) async-start(f32[16,72,256]{2,1,0:T(8,128)} %shard_map.68), calls=%async_computation.5 | async-start | bytes 2359296 | tf_op jit(solution)/shard_map/all_to_all | solution.py:446
  176.9 7.6 %collective-permute-start.11 = (f32[64,256]{1,0:T(8,128)S(1)}, f32[64,256]{1,0:T(8,128)S(1)}, u32[]{:S(2)}, u32[]{:S(2)}) collective-permute-start(f32[64,256]{1,0:T(8,128)S(1)} %pad_maximum_fusion.5), channel_id=1, source_target_pairs={{0,1},{1,0},{2,3},{3,2},{4,5},{5,4},{6,7},{7,6},{8,9},{9,8},{10,11... | collective-permute-start | bytes 196616 | tf_op jit(solution)/shard_map/ppermute | solution.py:394
  (6 other events, 11.8 us)

commit v4 on v3

v4 whole, which is shorter than its diff:
```python
import functools
import math

import jax
import jax.numpy as jnp
from jax import lax
from jax.experimental import pallas as pl
from jax.experimental.pallas import tpu as pltpu
from jax.sharding import Mesh
from jax.sharding import PartitionSpec as P

length_scale = 0.5
softening = 0.01
plane = ("x", "y")
ring = ("z_hi", "z_lo")
swap = [(0, 1), (1, 0)]
rider = 8
vmem_bytes = 24 * 1024 * 1024
most_bytes = 60 * 1024 * 1024


def whole(space=pltpu.VMEM):
    return pl.BlockSpec(memory_space=space)


def params(size=vmem_bytes):
    return pltpu.CompilerParams(vmem_limit_bytes=size)


def shape(sizes, dtype=jnp.float32):
    return jax.ShapeDtypeStruct(sizes, dtype)


def cost(flops, moved, transcendentals=0):
    return pl.CostEstimate(flops=flops, bytes_accessed=moved, transcendentals=transcendentals)


def dot(left, right, left_dim, right_dim):
    return lax.dot_general(
        left,
        right,
        (((left_dim,), (right_dim,)), ((), ())),
        precision=lax.Precision.HIGHEST,
        preferred_element_type=jnp.float32,
    )


def flat(value):
    return value.reshape(-1, value.shape[-1])


def high(value):
    return value.astype(jnp.bfloat16)


def cut(value, count):
    terms = []
    for _ in range(count):
        terms.append(high(value))
        value = value - terms[-1].astype(jnp.float32)
    return terms


def mul(left, right, left_dim, right_dim):
    return lax.dot_general(
        left, right, (((left_dim,), (right_dim,)), ((), ())), preferred_element_type=jnp.float32
    )


def mul_terms(left, right, left_dim, right_dim):
    count = len(left)
    total = None
    for order in reversed(range(count)):
        for place in range(order + 1):
            term = mul(left[place], right[order - place], left_dim, right_dim)
            total = term if total is None else total + term
    return total


def tile_block(left, left_norms, right_refs, norm_ref, columns):
    inner = mul_terms(left, [ref[columns, :] for ref in right_refs], 1, 1)
    squared = left_norms + norm_ref[:1, columns] - 2.0 * inner
    return jnp.exp(-jnp.sqrt(squared + softening) / length_scale)


def square_sums(rows):
    return jnp.sum(rows * rows, axis=1, keepdims=True)


def tile_kernel(half, shared, own_ref, other_ref, packed_ref, *refs):
    outs, refs = refs[: 1 + shared], refs[1 + shared :]
    left_ref, right_refs, rights, norm_ref, tile_ref, come, leave = refs[0], refs[1:3], refs[3:6], *refs[6:10]
    count, each, width = packed_ref.shape
    rows, depth = own_ref.shape
    step = count // 2
    centre_ref = packed_ref.at[:, :, pl.ds(half, depth)]
    pairs = [
        (centre_ref.at[pl.ds(0, step)], right_refs[0]),
        (own_ref, left_ref.at[pl.ds(0, rows)]),
        (other_ref, left_ref.at[pl.ds(rows, rows)]),
        (centre_ref.at[pl.ds(step, step)], right_refs[1]),
    ]
    if shared:
        weight_refs, share_refs = refs[10:12], refs[12:14]
        for place, columns in enumerate((pl.ds(0, half), pl.ds(width - half, half))):
            pairs.append((packed_ref.at[:, :, columns], weight_refs[place]))
    moves = [pltpu.make_async_copy(*pair, come.at[place]) for place, pair in enumerate(pairs)]
    for move in moves:
        move.start()
    shares, gone = [None] * shared, []

    def send(source, target):
        gone.append(pltpu.make_async_copy(source, target, leave.at[len(gone)]))
        gone[-1].start()

    for place, move in ((0, moves[0]), (1, moves[3])):
        columns = pl.ds(place * step * each, step * each)
        move.wait()
        right = flat(right_refs[place][...])
        for term, ref in zip(cut(right, 3), rights):
            ref[columns, :] = term
        ones = jnp.ones((8, depth), jnp.float32)
        norm_ref[:, columns] = dot(ones, right * right, 1, 1)
        if place == 0:
            moves[1].wait()
            moves[2].wait()
            left = left_ref[...]
            left_norms = square_sums(left)
            left = cut(left, 3)
        block = tile_block(left, left_norms, rights, norm_ref, columns)
        tile_ref[:, columns] = block
        send(tile_ref.at[:, columns], outs[0].at[:, columns])
        if shared:
            if place == 0:
                moves[4].wait()
                moves[5].wait()
            terms = cut(block, 2)
            for part, ref in enumerate(weight_refs):
                weights = cut(flat(ref[place * step : (place + 1) * step]), 2)
                share = mul_terms(terms, weights, 1, 0)
                shares[part] = share if shares[part] is None else shares[part] + share
    for part in range(shared):
        share_refs[part][...] = shares[part]
        send(share_refs[part], outs[1 + part])
    for move in gone:
        move.wait()


def tile_of(own, other, packed, half, shared=0):
    count, each, _ = packed.shape
    rows, depth = own.shape
    rows, columns = 2 * rows, count * each
    scratch = [pltpu.VMEM((rows, depth), jnp.float32)]
    scratch += [pltpu.VMEM((count // 2, each, depth), jnp.float32)] * 2
    scratch += [pltpu.VMEM((columns, depth), jnp.bfloat16)] * 3
    scratch += [pltpu.VMEM((8, columns), jnp.float32), pltpu.VMEM((rows, columns), jnp.float32)]
    scratch += [pltpu.SemaphoreType.DMA((4 + shared,)), pltpu.SemaphoreType.DMA((2 + shared,))]
    scratch += [pltpu.VMEM((count, each, half), jnp.float32)] * shared
    scratch += [pltpu.VMEM((rows, half), jnp.float32)] * shared
    return pl.pallas_call(
        functools.partial(tile_kernel, half, shared),
        in_specs=[whole(pl.ANY)] * 3,
        out_specs=[whole(pl.ANY)] * (1 + shared),
        out_shape=[shape((rows, columns))] + [shape((rows, half))] * shared,
        scratch_shapes=scratch,
        compiler_params=params(most_bytes),
        cost_estimate=cost(12 * rows * columns * depth, 6 * 1024 * 1024, 2 * rows * columns),
    )(own, other, packed)


def swapped(rows):
    half = rows.shape[0] // 2
    return jnp.concatenate([rows[half:], rows[:half]], axis=0)


def ring_places(place_ref, count):
    return [lax.rem(place_ref[0] + step, count) for step in range(count)]


def from_ring(ref, places, rows):
    mine = [ref[place, :rows] for place in places]
    return jnp.concatenate(mine + [ref[place, rows : 2 * rows] for place in places], axis=0)


def to_ring(total, ref, places, rows):
    middle = total.shape[0] // 2
    for step, place in enumerate(places):
        ref[place, :rows] = total[step * rows : (step + 1) * rows]
        ref[place, rows : 2 * rows] = total[middle + step * rows : middle + (step + 1) * rows]


def join_kernel(place_ref, own_ref, other_ref, pred_ref):
    count, rows, _ = pred_ref.shape
    to_ring(own_ref[...] + swapped(other_ref[...]), pred_ref, ring_places(place_ref, count), rows // 2)


def join(place, own, other, rows):
    count, half = own.shape
    return pl.pallas_call(
        join_kernel,
        in_specs=[whole(pltpu.SMEM), whole(), whole()],
        out_specs=whole(),
        out_shape=shape((count // (2 * rows), 2 * rows, half)),
        compiler_params=params(),
        cost_estimate=cost(own.size, 12 * own.size),
    )(place, own, other)


def settle_kernel(parts_ref, target_ref, copies_ref):
    residual = jnp.sum(parts_ref[...], axis=0) - target_ref[...]
    copies_ref[...] = jnp.broadcast_to(residual[None], copies_ref.shape)


def settle(parts, target):
    return pl.pallas_call(
        settle_kernel,
        in_specs=[whole(), whole()],
        out_specs=whole(),
        out_shape=shape(parts.shape),
        compiler_params=params(),
        cost_estimate=cost(2 * parts.size, 8 * parts.size),
    )(parts, target)


def far_terms_kernel(own_ref, other_ref, high_ref, low_ref, sums_ref):
    columns, width = own_ref.shape[1], sums_ref.shape[1]
    lines = []
    for core, ref in enumerate((own_ref, other_ref)):
        tile = swapped(ref[...]) if core else ref[...]
        for term, out in zip(cut(tile, 2), (high_ref, low_ref)):
            out[:, core * columns : (core + 1) * columns] = term
        part = jnp.sum(tile, axis=0, keepdims=True)
        lines += [part[:, place : place + width] for place in range(0, columns, width)]
    lines.append(jnp.zeros((rider - len(lines), width), jnp.float32))
    sums_ref[...] = jnp.concatenate(lines, axis=0)


def far_terms(own, other, half):
    rows, columns = own.shape
    return pl.pallas_call(
        far_terms_kernel,
        in_specs=[whole(), whole()],
        out_specs=[whole()] * 3,
        out_shape=[shape((rows, 2 * columns), jnp.bfloat16)] * 2 + [shape((rider, half))],
        compiler_params=params(),
        cost_estimate=cost(8 * own.size, 16 * own.size),
    )(own, other)


def gradient_kernel(place_ref, own_ref, other_ref, residual_ref, sums_ref, out_ref):
    count, rows, half = residual_ref.shape
    rows = rows // 2
    residual = from_ring(residual_ref, ring_places(place_ref, count), rows)
    own = mul_terms(cut(own_ref[...], 2), cut(residual, 2), 0, 0)
    other = mul_terms(cut(other_ref[...], 2), cut(swapped(residual), 2), 0, 0)
    out_ref[:, :rows] = own.reshape(-1, rows, half)
    out_ref[:, rows : 2 * rows] = other.reshape(-1, rows, half)
    out_ref[:, 2 * rows :] = jnp.broadcast_to(sums_ref[...][None], (out_ref.shape[0], rider, half))


def gradient(place, tiles, residual, sums):
    _, rows, half = residual.shape
    count = 2 * tiles[0].shape[1] // rows
    return pl.pallas_call(
        gradient_kernel,
        in_specs=[whole(pltpu.SMEM)] + [whole()] * 4,
        out_specs=whole(),
        out_shape=shape((count, rows + rider, half)),
        compiler_params=params(),
        cost_estimate=cost(12 * tiles[0].size * half, 4 * 1024 * 1024),
    )(place, *tiles, residual, sums)


def collect_kernel(parts_ref, grad_ref, copies_ref, largest_ref):
    rows = grad_ref.shape[0]
    total = jnp.sum(parts_ref[...], axis=0)
    grad_ref[...] = total[:rows]
    copies_ref[...] = jnp.broadcast_to(total[None, :rows], copies_ref.shape)
    largest = jnp.max(jnp.max(total[rows:], axis=0, keepdims=True), axis=1, keepdims=True)
    largest_ref[...] = jnp.broadcast_to(largest, largest_ref.shape)


def collect(parts):
    count, packed, half = parts.shape
    rows = packed - rider
    return pl.pallas_call(
        collect_kernel,
        in_specs=[whole()],
        out_specs=[whole()] * 3,
        out_shape=[
            shape((rows, half), jnp.float32),
            shape((count, rows, half), jnp.float32),
            shape((rider, half), jnp.float32),
        ],
        compiler_params=params(),
        cost_estimate=cost(2 * parts.size, 8 * parts.size),
    )(parts)


def product_kernel(place_ref, high_ref, low_ref, grad_ref, largest_ref, out_ref):
    rows = grad_ref.shape[1] // 2
    count, _, half = out_ref.shape
    grads = jnp.concatenate([flat(grad_ref[:, :rows]), flat(grad_ref[:, rows:])], axis=0)
    total = mul_terms([high_ref[...], low_ref[...]], cut(grads, 2), 1, 0)
    to_ring(total, out_ref, ring_places(place_ref, count), rows)
    out_ref[:, 2 * rows :] = jnp.broadcast_to(largest_ref[...][None], (count, rider, half))


def product(place, terms, grads, largest):
    _, rows, half = grads.shape
    count = terms[0].shape[0] // rows
    return pl.pallas_call(
        product_kernel,
        in_specs=[whole(pltpu.SMEM)] + [whole()] * 4,
        out_specs=whole(),
        out_shape=shape((count, rows + rider, half)),
        compiler_params=params(),
        cost_estimate=cost(6 * terms[0].size * half, 4 * 1024 * 1024),
    )(place, *terms, grads, largest)


def finish_kernel(scale, parts_ref, grad_ref, theta_ref):
    rows = grad_ref.shape[0]
    total = jnp.sum(parts_ref[:, :rows], axis=0)
    largest = jnp.max(parts_ref[:, rows:], axis=0)
    largest = jnp.max(jnp.max(largest, axis=0, keepdims=True), axis=1, keepdims=True)
    step_size = 1.0 / largest
    theta_ref[...] = (2.0 * step_size * grad_ref[...] - step_size * step_size * total) * scale


def finish(parts, grad, scale):
    def body(*refs):
        finish_kernel(scale, *refs)

    return pl.pallas_call(
        body,
        in_specs=[whole(), whole()],
        out_specs=whole(),
        out_shape=shape(grad.shape),
        compiler_params=params(),
        cost_estimate=cost(2 * parts.size, 4 * parts.size),
    )(parts, grad)


def spread_kernel(core_ref, weight_ref, centre_ref, out_ref, packed_ref, semaphores):
    half, width = weight_ref.shape[1] // 2, packed_ref.shape[1]
    packed_ref[:, half : width - half] = centre_ref[...]
    first, second = weight_ref[:, :half], weight_ref[:, half:]
    low = core_ref[0] == 0
    packed_ref[:, :half] = jnp.where(low, second, first)
    packed_ref[:, width - half :] = jnp.where(low, first, second)
    moves = [
        pltpu.make_async_copy(packed_ref, out_ref.at[place], semaphores.at[place]) for place in range(out_ref.shape[0])
    ]
    for move in moves:
        move.start()
    for move in moves:
        move.wait()


def spread(weights, centres, count):
    rows, width = weights.shape[0], weights.shape[1] + centres.shape[1]
    return pl.pallas_call(
        spread_kernel,
        in_specs=[whole(pltpu.SMEM), whole(), whole()],
        out_specs=whole(pl.ANY),
        out_shape=shape((count, rows, width)),
        scratch_shapes=[pltpu.VMEM((rows, width), jnp.float32), pltpu.SemaphoreType.DMA((count,))],
        compiler_params=params(most_bytes),
        cost_estimate=cost(0, 4 * count * rows * width),
    )(lax.axis_index("core").reshape(1).astype(jnp.int32), weights, centres)


def assemble_kernel(count, *refs):
    for place, ref in enumerate(refs[:count]):
        rows = ref.shape[0] // 2
        for part, out_ref in enumerate(refs[count:]):
            out_ref[place * rows : (place + 1) * rows, :] = ref[part * rows : (part + 1) * rows, :]


def assemble(pieces):
    count = len(pieces)
    rows, width = pieces[0].shape
    return pl.pallas_call(
        functools.partial(assemble_kernel, count),
        in_specs=[whole()] * count,
        out_specs=[whole()] * 2,
        out_shape=[shape((count * rows // 2, width))] * 2,
        compiler_params=params(),
        cost_estimate=cost(0, 8 * count * rows * width),
    )(*pieces)


def gather(value, axis):
    copies = jnp.broadcast_to(value[None], (lax.axis_size(axis),) + value.shape)
    return lax.all_to_all(copies, axis, 0, 0)


def ring_pieces(value):
    count, low = lax.axis_size(ring), lax.axis_size("z_lo")

    def slot(place):
        return place % low * (count // low) + place // low

    def hop(held, step):
        pairs = [(slot(place), slot((place + step) % count)) for place in range(count)]
        return lax.ppermute(held, ("z_lo", "z_hi"), pairs)

    ahead, behind = [value], [value]
    for step in range(1, count):
        if step % 2:
            behind.append(hop(behind[-1], 1))
        else:
            ahead.append(hop(ahead[-1], -1))
    return ahead + behind[:0:-1]


def from_other(value):
    return lax.ppermute(value, "core", swap)


def halves(rows):
    core = lax.axis_index("core")
    half = rows.shape[1] // 2
    first, second = rows[:, :half], rows[:, half:]
    return jnp.where(core == 0, first, second), jnp.where(core == 0, second, first)


def to_rows(*columns):
    core = lax.axis_index("core")
    rows = columns[0].shape[0] // 2
    own = jnp.concatenate([value[:rows] for value in columns], axis=0)
    other = from_other(jnp.concatenate([value[rows:] for value in columns], axis=0))
    first = jnp.where(core == 0, own, other)
    second = jnp.where(core == 0, other, own)
    both = jnp.concatenate([first, second], axis=1)
    return tuple(both[place * rows : (place + 1) * rows] for place in range(len(columns)))


def shards(batch_features, centre_features, targets, weights):
    rows, width = targets.shape
    half = width // 2
    total_rows = rows * lax.axis_size(plane) * lax.axis_size(ring) * 2
    place = lax.axis_index(ring)

    place = place.reshape(1).astype(jnp.int32)

    centres = spread(weights, centre_features, lax.axis_size(plane))
    centres = lax.all_to_all(centres, plane, 0, 0)
    pieces = ring_pieces(jnp.concatenate([batch_features, centre_features], axis=0))
    batch, far = assemble(pieces)
    batch_other = from_other(batch)
    far_other = from_other(far)
    tile, theirs, mine = tile_of(batch, batch_other, centres, half, 2)
    pred = join(place, mine, from_other(theirs), rows)
    tiles = tile, from_other(tile)
    target_mine, target_theirs = halves(targets)
    target = jnp.concatenate([target_mine, from_other(target_theirs)], axis=0)
    parts = lax.all_to_all(pred, ring, 0, 0)
    residuals = settle(parts, target)
    residual_full = lax.all_to_all(residuals, ring, 0, 0)

    (far_tile,) = tile_of(far, far_other, centres, half)
    *fars, sums = far_terms(far_tile, from_other(far_tile), half)
    parts = lax.all_to_all(gradient(place, tiles, residual_full, sums), plane, 0, 0)
    grad, copies, largest = collect(parts)
    grad_full = lax.all_to_all(copies, plane, 0, 0)
    parts = lax.all_to_all(product(place, fars, grad_full, largest), ring, 0, 0)
    theta = finish(parts, grad, total_rows / math.sqrt(total_rows))
    return to_rows(residuals[0], theta)


def solution(mesh):
    fine = Mesh(
        mesh.devices.reshape(4, 4, 4, 2, 2),
        ("x", "z_lo", "y", "z_hi", "core"),
    )
    by_batch = P(("x", "z_lo", "y", "z_hi", "core"), None)
    by_centre = P(("y", "z_hi", "core", "x", "z_lo"), None)
    return jax.shard_map(
        shards,
        mesh=fine,
        in_specs=(by_batch, by_centre, by_batch, by_centre),
        out_specs=(by_batch, by_centre),
        check_vma=False,
    )
```

time: 186 us -> 183 us (0.984)
  waiting for transfers between devices: 55.1 us -> 59.9 us
  starting transfers between devices: 50.5 us -> 46 us
    ppermute x5 -> x7, starting transfers between devices: 14.4 us -> 11.9 us  [from_other(): return lax.ppermute(value, 'core', swap)]
    pallas_call x6, Pallas kernels: 25.5 us -> 23.3 us  [the longest x2 19.3 us: tile_of(): pl.pallas_call(functools.partial(tile_kernel, half, shared), in_specs=[wh...]
    broadcast_in_dim x1 -> x0, local copies, waits for them, and re-layouts: 2.04 us -> none  [shards(): features = jnp.broadcast_to(features[None], (count,) + features.shape)]
    all_to_all x4, starting transfers between devices: 25 us -> 23 us  [the longest x1 8.19 us: shards(): parts = lax.all_to_all(pred, ring, 0, 0)]
    ppermute x7, waiting for transfers between devices: 15.6 us -> 17.5 us  [hop(): return lax.ppermute(held, ('z_lo', 'z_hi'), pairs)]
    ppermute x5 -> x7, waiting for transfers between devices: 3.2 us -> 4.46 us  [from_other(): return lax.ppermute(value, 'core', swap)]
    unnamed x28 -> x29, local copies, waits for them, and re-layouts: 4.94 us -> 5.67 us
  transfers between devices with their start and end apart: 16 -> 18, of which waited for: 10 -> 11; matrix products, arithmetic and copies ran while one was open for 0% -> 0% of each run, Pallas kernels for 8% -> 6%
where the time goes in v4:
time: 183 us; the launch traced here: 182 us
  waiting for transfers between devices  59.9 us (33%)
  starting transfers between devices  46 us (25%)
  blocking collectives  39.7 us (22%)
  Pallas kernels  28.5 us (16%)
  local copies, waits for them, and re-layouts  6.47 us (4%)
    all_to_all x1, blocking collectives, shards(): lax.all_to_all(gradient(place, tiles, residual_full, sums), plane, 0, 0)  21.4 us
    pallas_call x2, Pallas kernels, tile_of(): pl.pallas_call(functools.partial(tile_kernel, half, shared), in_specs=[wh...  19.3 us
    all_to_all x1, blocking collectives, shards(): grad_full = lax.all_to_all(copies, plane, 0, 0)  18.3 us
    ppermute x7, waiting for transfers between devices, hop(): return lax.ppermute(held, ('z_lo', 'z_hi'), pairs)  17.5 us
    all_to_all x1, waiting for transfers between devices, shards(): residual_full = lax.all_to_all(residuals, ring, 0, 0)  15.5 us
    all_to_all x1, waiting for transfers between devices, shards(): parts = lax.all_to_all(product(place, fars, grad_full, largest), ring, 0, 0)  15.3 us
    ppermute x7, starting transfers between devices, from_other(): return lax.ppermute(value, 'core', swap)  11.9 us
    ppermute x7, starting transfers between devices, hop(): return lax.ppermute(held, ('z_lo', 'z_hi'), pairs)  11.1 us
  transfers between devices with their start and end apart: 18, of which 11 were waited for; matrix products, arithmetic and copies ran while one was open for 0% of the time, Pallas kernels for 6%

profile of v4, /device:TPU:1, one launch (start us, length us, event | category | flops | bytes accessed | tf_op | source)
XLA Modules:
  0.0 182.2 jit_solution(8673419555979528062)
XLA Ops:
  0.6 2.6 %shard_map.60 = f32[16,32,1280]{2,1,0:T(8,128)} custom-call(s32[1]{0:T(128)} %bitcast.1.core_ref, f32[32,512]{1,0:T(8,128)} %weight_ref.1, f32[32,768]{1,0:T(8,128)} %centre_ref.1), custom_call_target="tpu_custom_call" | custom-call | bytes 2621440 | tf_op jit(solution)/shard_map/pallas_call | solution.py:363
  3.3 7.8 %all-to-all-start = ((f32[16,32,1280]{2,1,0:T(8,128)}), f32[16,32,1280]{2,1,0:T(8,128)}, u32[]{:S(2)}, u32[]{:S(2)}) async-start(f32[16,32,1280]{2,1,0:T(8,128)} %shard_map.60), calls=%async_computation | async-start | bytes 5242880 | tf_op jit(solution)/shard_map/all_to_all | solution.py:449
  12.8 4.0 %collective-permute-start = (f32[64,768]{1,0:T(8,128)S(1)}, f32[64,768]{1,0:T(8,128)S(1)}, u32[]{:S(2)}, u32[]{:S(2)}) collective-permute-start(f32[64,768]{1,0:T(8,128)S(1)} %constant_dynamic-update-slice_fusion.refs_0_), channel_id=1, source_target_pairs={{0,50},{16,0},{32,16},{48,32},{2,48},{18,2},{34,18},{50,34},{1,51}... | collective-permute-start | bytes 589832 | tf_op jit(solution)/shard_map/ppermute | solution.py:407
  16.8 4.3 %collective-permute-done.3.refs_7_ = f32[64,768]{1,0:T(8,128)S(1)} collective-permute-done((f32[64,768]{1,0:T(8,128)S(1)}, f32[64,768]{1,0:T(8,128)S(1)}, u32[]{:S(2)}, u32[]{:S(2)}) %collective-permute-start.3) | collective-permute-done | bytes 196640 | tf_op jit(solution)/shard_map/ppermute | solution.py:407
  21.2 2.7 %collective-permute-start.1 = (f32[64,768]{1,0:T(8,128)S(1)}, f32[64,768]{1,0:T(8,128)S(1)}, u32[]{:S(2)}, u32[]{:S(2)}) collective-permute-start(f32[64,768]{1,0:T(8,128)S(1)} %collective-permute-done.refs_1_), channel_id=1, source_target_pairs={{0,50},{16,0},{32,16},{48,32},{2,48},{18,2},{34,18},{50,34},{1,51}... | collective-permute-start | bytes 589832 | tf_op jit(solution)/shard_map/ppermute | solution.py:407
  23.8 3.6 %collective-permute-done.4.refs_6_ = f32[64,768]{1,0:T(8,128)S(1)} collective-permute-done((f32[64,768]{1,0:T(8,128)S(1)}, f32[64,768]{1,0:T(8,128)S(1)}, u32[]{:S(2)}, u32[]{:S(2)}) %collective-permute-start.4) | collective-permute-done | bytes 196640 | tf_op jit(solution)/shard_map/ppermute | solution.py:407
  27.4 2.7 %collective-permute-start.2 = (f32[64,768]{1,0:T(8,128)S(1)}, f32[64,768]{1,0:T(8,128)S(1)}, u32[]{:S(2)}, u32[]{:S(2)}) collective-permute-start(f32[64,768]{1,0:T(8,128)S(1)} %collective-permute-done.1.refs_2_), channel_id=1, source_target_pairs={{0,50},{16,0},{32,16},{48,32},{2,48},{18,2},{34,18},{50,34},{1,51}... | collective-permute-start | bytes 589832 | tf_op jit(solution)/shard_map/ppermute | solution.py:407
  30.1 3.5 %collective-permute-done.5.refs_5_ = f32[64,768]{1,0:T(8,128)S(1)} collective-permute-done((f32[64,768]{1,0:T(8,128)S(1)}, f32[64,768]{1,0:T(8,128)S(1)}, u32[]{:S(2)}, u32[]{:S(2)}) %collective-permute-start.5) | collective-permute-done | bytes 196640 | tf_op jit(solution)/shard_map/ppermute | solution.py:407
  33.6 6.1 %collective-permute-done.6.refs_4_ = f32[64,768]{1,0:T(8,128)S(1)} collective-permute-done((f32[64,768]{1,0:T(8,128)S(1)}, f32[64,768]{1,0:T(8,128)S(1)}, u32[]{:S(2)}, u32[]{:S(2)}) %collective-permute-start.6) | collective-permute-done | bytes 196640 | tf_op jit(solution)/shard_map/ppermute | solution.py:407
  39.8 3.8 %collective-permute-start.7 = (f32[256,768]{1,0:T(8,128)S(1)}, f32[256,768]{1,0:T(8,128)S(1)}, u32[]{:S(2)}, u32[]{:S(2)}) collective-permute-start(f32[256,768]{1,0:T(8,128)S(1)} %get-tuple-element.13.own_ref), channel_id=1, source_target_pairs={{0,1},{1,0},{2,3},{3,2},{4,5},{5,4},{6,7},{7,6},{8,9},{9,8},{10,11... | collective-permute-start | bytes 2359304 | tf_op jit(solution)/shard_map/ppermute | solution.py:419
  43.7 1.9 %collective-permute-done.7.other_ref = f32[256,768]{1,0:T(8,128)S(1)} collective-permute-done((f32[256,768]{1,0:T(8,128)S(1)}, f32[256,768]{1,0:T(8,128)S(1)}, u32[]{:S(2)}, u32[]{:S(2)}) %collective-permute-start.7) | collective-permute-done | bytes 786464 | tf_op jit(solution)/shard_map/ppermute | solution.py:419
  46.5 10.3 %shard_map.61 = (f32[512,512]{1,0:T(8,128)}, f32[512,256]{1,0:T(8,128)}, f32[512,256]{1,0:T(8,128)}) custom-call(f32[256,768]{1,0:T(8,128)} %copy-done.8, f32[256,768]{1,0:T(8,128)} %copy-done.13, f32[16,32,1280]{2,1,0:T(8,128)} %all-to-all-done.packed_ref), custom_call_target="tpu_custom_call" | custom-call | flops 2415919104 | bytes 6291456 | tf_op jit(solution)/shard_map/pallas_call | solution.py:160
  56.8 2.9 %collective-permute-start.8 = (f32[512,256]{1,0:T(8,128)}, f32[512,256]{1,0:T(8,128)S(1)}, u32[]{:S(2)}, u32[]{:S(2)}) collective-permute-start(f32[512,256]{1,0:T(8,128)} %get-tuple-element.15), channel_id=1, source_target_pairs={{0,1},{1,0},{2,3},{3,2},{4,5},{5,4},{6,7},{7,6},{8,9},{9,8},{10,11... | collective-permute-start | bytes 1572872 | tf_op jit(solution)/shard_map/ppermute | solution.py:419
  63.5 8.2 %all-to-all-start.1 = ((f32[8,64,256]{2,1,0:T(8,128)}), f32[8,64,256]{2,1,0:T(8,128)S(1)}, u32[]{:S(2)}, u32[]{:S(2)}) async-start(f32[8,64,256]{2,1,0:T(8,128)} %shard_map.62), calls=%async_computation.1 | async-start | bytes 1048576 | tf_op jit(solution)/shard_map/all_to_all | solution.py:459
  73.3 9.0 %shard_map.64.own_ref = f32[512,512]{1,0:T(8,128)} custom-call(f32[256,768]{1,0:T(8,128)} %copy-done.7, f32[256,768]{1,0:T(8,128)} %copy-done.12, f32[16,32,1280]{2,1,0:T(8,128)} %all-to-all-done.packed_ref), custom_call_target="tpu_custom_call" | custom-call | flops 2415919104 | bytes 6291456 | tf_op jit(solution)/shard_map/pallas_call | solution.py:160
  82.9 6.7 %all-to-all-done.1.parts_ref = f32[8,64,256]{2,1,0:T(8,128)S(1)} async-done(((f32[8,64,256]{2,1,0:T(8,128)}), f32[8,64,256]{2,1,0:T(8,128)S(1)}, u32[]{:S(2)}, u32[]{:S(2)}) %all-to-all-start.1) | async-done | bytes 524320 | tf_op jit(solution)/shard_map/all_to_all | solution.py:459
  90.5 3.5 %all-to-all-start.2 = ((f32[8,64,256]{2,1,0:T(8,128)}), f32[8,64,256]{2,1,0:T(8,128)S(1)}, u32[]{:S(2)}, u32[]{:S(2)}) async-start(f32[8,64,256]{2,1,0:T(8,128)} %shard_map.63), calls=%async_computation.2 | async-start | bytes 1048576 | tf_op jit(solution)/shard_map/all_to_all | solution.py:461
  96.3 15.5 %all-to-all-done.2.residual_ref = f32[8,64,256]{2,1,0:T(8,128)S(1)} async-done(((f32[8,64,256]{2,1,0:T(8,128)}), f32[8,64,256]{2,1,0:T(8,128)S(1)}, u32[]{:S(2)}, u32[]{:S(2)}) %all-to-all-start.2) | async-done | bytes 524320 | tf_op jit(solution)/shard_map/all_to_all | solution.py:461
  113.1 2.3 %shard_map.66 = f32[16,72,256]{2,1,0:T(8,128)S(1)} custom-call(s32[1]{0:T(128)} %bitcast.place_ref, f32[512,512]{1,0:T(8,128)S(1)} %copy-done.1, f32[512,512]{1,0:T(8,128)} %collective-permute-done.12.other_ref, f32[8,64,256]{2,1,0:T(8,128)S(1)} %all-to-all-done.2.residual_ref, f32[8,256]{1,0:T(8,128)S(1)} %get-tuple-element.20.sums_ref), custom_call_target="tpu_custom_call" | custom-call | flops 805306368 | bytes 4194304 | tf_op jit(solution)/shard_map/pallas_call | solution.py:264
  115.4 21.4 %all_to_all.30.parts_ref = f32[16,72,256]{2,1,0:T(8,128)S(1)} all-to-all(f32[16,72,256]{2,1,0:T(8,128)S(1)} %shard_map.66), channel_id=1, replica_groups=mesh['x'=4,'z_lo'=4,'y'=4,'z_hi'=2,'core'=2] {'x','y'}, dimensions={0} | all-to-all | bytes 2359296 | tf_op jit(solution)/shard_map/all_to_all | solution.py:465
  136.9 18.3 %all_to_all.31.grad_ref = f32[16,64,256]{2,1,0:T(8,128)S(1)} all-to-all(f32[16,64,256]{2,1,0:T(8,128)S(1)} %get-tuple-element.21), channel_id=1, replica_groups=mesh['x'=4,'z_lo'=4,'y'=4,'z_hi'=2,'core'=2] {'x','y'}, dimensions={0} | all-to-all | bytes 2097152 | tf_op jit(solution)/shard_map/all_to_all | solution.py:467
  157.1 3.5 %all-to-all-start.5 = ((f32[8,72,256]{2,1,0:T(8,128)}), f32[8,72,256]{2,1,0:T(8,128)S(1)}, u32[]{:S(2)}, u32[]{:S(2)}) async-start(f32[8,72,256]{2,1,0:T(8,128)} %shard_map.68), calls=%async_computation.5 | async-start | bytes 1179648 | tf_op jit(solution)/shard_map/all_to_all | solution.py:468
  161.4 15.3 %all-to-all-done.5.refs_0_ = f32[8,72,256]{2,1,0:T(8,128)S(1)} async-done(((f32[8,72,256]{2,1,0:T(8,128)}), f32[8,72,256]{2,1,0:T(8,128)S(1)}, u32[]{:S(2)}, u32[]{:S(2)}) %all-to-all-start.5) | async-done | bytes 589856 | tf_op jit(solution)/shard_map/all_to_all | solution.py:468
  176.9 3.7 %collective-permute-start.13 = (f32[64,256]{1,0:T(8,128)S(1)}, f32[64,256]{1,0:T(8,128)S(1)}, u32[]{:S(2)}, u32[]{:S(2)}) collective-permute-start(f32[64,256]{1,0:T(8,128)S(1)} %pad_maximum_fusion.3), channel_id=1, source_target_pairs={{0,1},{1,0},{2,3},{3,2},{4,5},{5,4},{6,7},{7,6},{8,9},{9,8},{10,11... | collective-permute-start | bytes 196616 | tf_op jit(solution)/shard_map/ppermute | solution.py:419
  (62 shorter events, 17.5 us)
Async XLA Ops:
  3.2 7.8 %copy-start.9 = (f32[32,768]{1,0:T(8,128)S(1)}, f32[32,768]{1,0:T(8,128)}, u32[]{:S(2)}) copy-start(f32[32,768]{1,0:T(8,128)} %centre_ref.1) | copy-start | bytes 294916
  3.3 42.7 %all-to-all-start = ((f32[16,32,1280]{2,1,0:T(8,128)}), f32[16,32,1280]{2,1,0:T(8,128)}, u32[]{:S(2)}, u32[]{:S(2)}) async-start(f32[16,32,1280]{2,1,0:T(8,128)} %shard_map.60), calls=%async_computation | async-start | bytes 5242880 | tf_op jit(solution)/shard_map/all_to_all | solution.py:449
  11.1 10.1 %collective-permute-start.3 = (f32[64,768]{1,0:T(8,128)S(1)}, f32[64,768]{1,0:T(8,128)S(1)}, u32[]{:S(2)}, u32[]{:S(2)}) collective-permute-start(f32[64,768]{1,0:T(8,128)S(1)} %constant_dynamic-update-slice_fusion.refs_0_), channel_id=1, source_target_pairs={{0,16},{16,32},{32,48},{48,2},{2,18},{18,34},{34,50},{50,0},{1,17}... | collective-permute-start | bytes 589832 | tf_op jit(solution)/shard_map/ppermute | solution.py:407
  12.8 8.4 %collective-permute-start = (f32[64,768]{1,0:T(8,128)S(1)}, f32[64,768]{1,0:T(8,128)S(1)}, u32[]{:S(2)}, u32[]{:S(2)}) collective-permute-start(f32[64,768]{1,0:T(8,128)S(1)} %constant_dynamic-update-slice_fusion.refs_0_), channel_id=1, source_target_pairs={{0,50},{16,0},{32,16},{48,32},{2,48},{18,2},{34,18},{50,34},{1,51}... | collective-permute-start | bytes 589832 | tf_op jit(solution)/shard_map/ppermute | solution.py:407
  21.2 6.3 %collective-permute-start.4 = (f32[64,768]{1,0:T(8,128)S(1)}, f32[64,768]{1,0:T(8,128)S(1)}, u32[]{:S(2)}, u32[]{:S(2)}) collective-permute-start(f32[64,768]{1,0:T(8,128)S(1)} %collective-permute-done.3.refs_7_), channel_id=1, source_target_pairs={{0,16},{16,32},{32,48},{48,2},{2,18},{18,34},{34,50},{50,0},{1,17}... | collective-permute-start | bytes 589832 | tf_op jit(solution)/shard_map/ppermute | solution.py:407
  21.2 6.3 %collective-permute-start.1 = (f32[64,768]{1,0:T(8,128)S(1)}, f32[64,768]{1,0:T(8,128)S(1)}, u32[]{:S(2)}, u32[]{:S(2)}) collective-permute-start(f32[64,768]{1,0:T(8,128)S(1)} %collective-permute-done.refs_1_), channel_id=1, source_target_pairs={{0,50},{16,0},{32,16},{48,32},{2,48},{18,2},{34,18},{50,34},{1,51}... | collective-permute-start | bytes 589832 | tf_op jit(solution)/shard_map/ppermute | solution.py:407
  27.4 6.1 %collective-permute-start.5 = (f32[64,768]{1,0:T(8,128)S(1)}, f32[64,768]{1,0:T(8,128)S(1)}, u32[]{:S(2)}, u32[]{:S(2)}) collective-permute-start(f32[64,768]{1,0:T(8,128)S(1)} %collective-permute-done.4.refs_6_), channel_id=1, source_target_pairs={{0,16},{16,32},{32,48},{48,2},{2,18},{18,34},{34,50},{50,0},{1,17}... | collective-permute-start | bytes 589832 | tf_op jit(solution)/shard_map/ppermute | solution.py:407
  27.4 6.1 %collective-permute-start.2 = (f32[64,768]{1,0:T(8,128)S(1)}, f32[64,768]{1,0:T(8,128)S(1)}, u32[]{:S(2)}, u32[]{:S(2)}) collective-permute-start(f32[64,768]{1,0:T(8,128)S(1)} %collective-permute-done.1.refs_2_), channel_id=1, source_target_pairs={{0,50},{16,0},{32,16},{48,32},{2,48},{18,2},{34,18},{50,34},{1,51}... | collective-permute-start | bytes 589832 | tf_op jit(solution)/shard_map/ppermute | solution.py:407
  33.6 6.1 %collective-permute-start.6 = (f32[64,768]{1,0:T(8,128)S(1)}, f32[64,768]{1,0:T(8,128)S(1)}, u32[]{:S(2)}, u32[]{:S(2)}) collective-permute-start(f32[64,768]{1,0:T(8,128)S(1)} %collective-permute-done.5.refs_5_), channel_id=1, source_target_pairs={{0,16},{16,32},{32,48},{48,2},{2,18},{18,34},{34,50},{50,0},{1,17}... | collective-permute-start | bytes 589832 | tf_op jit(solution)/shard_map/ppermute | solution.py:407
  39.8 20.0 %copy-start.7 = (f32[256,768]{1,0:T(8,128)}, f32[256,768]{1,0:T(8,128)S(1)}, u32[]{:S(2)}) copy-start(f32[256,768]{1,0:T(8,128)S(1)} %get-tuple-element.16.own_ref) | copy-start | bytes 2359300
  39.8 5.8 %collective-permute-start.7 = (f32[256,768]{1,0:T(8,128)S(1)}, f32[256,768]{1,0:T(8,128)S(1)}, u32[]{:S(2)}, u32[]{:S(2)}) collective-permute-start(f32[256,768]{1,0:T(8,128)S(1)} %get-tuple-element.13.own_ref), channel_id=1, source_target_pairs={{0,1},{1,0},{2,3},{3,2},{4,5},{5,4},{6,7},{7,6},{8,9},{9,8},{10,11... | collective-permute-start | bytes 2359304 | tf_op jit(solution)/shard_map/ppermute | solution.py:419
  46.5 25.2 %copy-start.11 = (f32[32,512]{1,0:T(8,128)S(1)}, f32[32,512]{1,0:T(8,128)}, u32[]{:S(2)}) copy-start(f32[32,512]{1,0:T(8,128)} %param.6) | copy-start | bytes 196612
  56.8 4.7 %collective-permute-start.8 = (f32[512,256]{1,0:T(8,128)}, f32[512,256]{1,0:T(8,128)S(1)}, u32[]{:S(2)}, u32[]{:S(2)}) collective-permute-start(f32[512,256]{1,0:T(8,128)} %get-tuple-element.15), channel_id=1, source_target_pairs={{0,1},{1,0},{2,3},{3,2},{4,5},{5,4},{6,7},{7,6},{8,9},{9,8},{10,11... | collective-permute-start | bytes 1572872 | tf_op jit(solution)/shard_map/ppermute | solution.py:419
  59.8 12.6 %collective-permute-start.10 = (f32[256,768]{1,0:T(8,128)S(1)}, f32[256,768]{1,0:T(8,128)S(1)}, u32[]{:S(2)}, u32[]{:S(2)}) collective-permute-start(f32[256,768]{1,0:T(8,128)S(1)} %get-tuple-element.16.own_ref), channel_id=1, source_target_pairs={{0,1},{1,0},{2,3},{3,2},{4,5},{5,4},{6,7},{7,6},{8,9},{9,8},{10,11... | collective-permute-start | bytes 2359304 | tf_op jit(solution)/shard_map/ppermute | solution.py:419
  63.5 26.1 %all-to-all-start.1 = ((f32[8,64,256]{2,1,0:T(8,128)}), f32[8,64,256]{2,1,0:T(8,128)S(1)}, u32[]{:S(2)}, u32[]{:S(2)}) async-start(f32[8,64,256]{2,1,0:T(8,128)} %shard_map.62), calls=%async_computation.1 | async-start | bytes 1048576 | tf_op jit(solution)/shard_map/all_to_all | solution.py:459
  71.7 11.2 %collective-permute-start.9 = (f32[32,256]{1,0:T(8,128)S(1)}, f32[32,256]{1,0:T(8,128)S(1)}, u32[]{:S(2)}, u32[]{:S(2)}) collective-permute-start(f32[32,256]{1,0:T(8,128)S(1)} %get-tuple-element.33), channel_id=1, source_target_pairs={{0,1},{1,0},{2,3},{3,2},{4,5},{5,4},{6,7},{7,6},{8,9},{9,8},{10,11... | collective-permute-start | bytes 98312 | tf_op jit(solution)/shard_map/ppermute | solution.py:419
  82.3 11.7 %copy-start = (f32[512,512]{1,0:T(8,128)S(1)}, f32[512,512]{1,0:T(8,128)}, u32[]{:S(2)}) copy-start(f32[512,512]{1,0:T(8,128)} %shard_map.64.own_ref) | copy-start | bytes 3145732
  82.3 11.7 %collective-permute-start.11 = (f32[512,512]{1,0:T(8,128)}, f32[512,512]{1,0:T(8,128)S(1)}, u32[]{:S(2)}, u32[]{:S(2)}) collective-permute-start(f32[512,512]{1,0:T(8,128)} %shard_map.64.own_ref), channel_id=1, source_target_pairs={{0,1},{1,0},{2,3},{3,2},{4,5},{5,4},{6,7},{7,6},{8,9},{9,8},{10,11... | collective-permute-start | bytes 3145736 | tf_op jit(solution)/shard_map/ppermute | solution.py:419
  82.4 13.9 %collective-permute-start.12 = (f32[512,512]{1,0:T(8,128)}, f32[512,512]{1,0:T(8,128)}, u32[]{:S(2)}, u32[]{:S(2)}) collective-permute-start(f32[512,512]{1,0:T(8,128)} %get-tuple-element.19.own_ref), channel_id=1, source_target_pairs={{0,1},{1,0},{2,3},{3,2},{4,5},{5,4},{6,7},{7,6},{8,9},{9,8},{10,11... | collective-permute-start | bytes 3145736 | tf_op jit(solution)/shard_map/ppermute | solution.py:419
  90.5 21.4 %all-to-all-start.2 = ((f32[8,64,256]{2,1,0:T(8,128)}), f32[8,64,256]{2,1,0:T(8,128)S(1)}, u32[]{:S(2)}, u32[]{:S(2)}) async-start(f32[8,64,256]{2,1,0:T(8,128)} %shard_map.63), calls=%async_computation.2 | async-start | bytes 1048576 | tf_op jit(solution)/shard_map/all_to_all | solution.py:461
  115.4 39.9 %copy-start.3 = (bf16[512,1024]{1,0:T(8,128)(2,1)S(1)}, bf16[512,1024]{1,0:T(8,128)(2,1)}, u32[]{:S(2)}) copy-start(bf16[512,1024]{1,0:T(8,128)(2,1)} %copy-done.2) | copy-start | bytes 3145732
  115.4 39.9 %copy-start.5 = (bf16[512,1024]{1,0:T(8,128)(2,1)S(1)}, bf16[512,1024]{1,0:T(8,128)(2,1)}, u32[]{:S(2)}) copy-start(bf16[512,1024]{1,0:T(8,128)(2,1)} %copy-done.4) | copy-start | bytes 3145732
  157.1 19.7 %all-to-all-start.5 = ((f32[8,72,256]{2,1,0:T(8,128)}), f32[8,72,256]{2,1,0:T(8,128)S(1)}, u32[]{:S(2)}, u32[]{:S(2)}) async-start(f32[8,72,256]{2,1,0:T(8,128)} %shard_map.68), calls=%async_computation.5 | async-start | bytes 1179648 | tf_op jit(solution)/shard_map/all_to_all | solution.py:468
  176.9 4.6 %collective-permute-start.13 = (f32[64,256]{1,0:T(8,128)S(1)}, f32[64,256]{1,0:T(8,128)S(1)}, u32[]{:S(2)}, u32[]{:S(2)}) collective-permute-start(f32[64,256]{1,0:T(8,128)S(1)} %pad_maximum_fusion.3), channel_id=1, source_target_pairs={{0,1},{1,0},{2,3},{3,2},{4,5},{5,4},{6,7},{7,6},{8,9},{9,8},{10,11... | collective-permute-start | bytes 196616 | tf_op jit(solution)/shard_map/ppermute | solution.py:419
  (8 other events, 20.0 us)

commit v5 on v4

--- a/solution.py
+++ b/solution.py
@@ -250,12 +250,16 @@
 def gradient_kernel(place_ref, own_ref, other_ref, residual_ref, sums_ref, out_ref):
     count, rows, half = residual_ref.shape
     rows = rows // 2
-    residual = from_ring(residual_ref, ring_places(place_ref, count), rows)
+    places = [count - 1 - place for place in ring_places(place_ref, count)]
+    residual = from_ring(residual_ref, places, rows)
     own = mul_terms(cut(own_ref[...], 2), cut(residual, 2), 0, 0)
     other = mul_terms(cut(other_ref[...], 2), cut(swapped(residual), 2), 0, 0)
-    out_ref[:, :rows] = own.reshape(-1, rows, half)
-    out_ref[:, rows : 2 * rows] = other.reshape(-1, rows, half)
-    out_ref[:, 2 * rows :] = jnp.broadcast_to(sums_ref[...][None], (out_ref.shape[0], rider, half))
+    last = out_ref.shape[0] - 1
+    for step in range(last + 1):
+        block = slice(step * rows, (step + 1) * rows)
+        out_ref[last - step, :rows] = own[block]
+        out_ref[last - step, rows : 2 * rows] = other[block]
+    out_ref[:, 2 * rows :] = jnp.broadcast_to(sums_ref[...][None], (last + 1, rider, half))
 
 
 def gradient(place, tiles, residual, sums):
@@ -391,6 +395,11 @@
     )(*pieces)
 
 
+def backward(copies, axis):
+    order = [list(range(lax.axis_size(axis)))[::-1]]
+    return lax.all_to_all(copies, axis, 0, 0, axis_index_groups=order)
+
+
 def gather(value, axis):
     copies = jnp.broadcast_to(value[None], (lax.axis_size(axis),) + value.shape)
     return lax.all_to_all(copies, axis, 0, 0)
@@ -446,7 +455,7 @@
     place = place.reshape(1).astype(jnp.int32)
 
     centres = spread(weights, centre_features, lax.axis_size(plane))
-    centres = lax.all_to_all(centres, plane, 0, 0)
+    centres = backward(centres, plane)
     pieces = ring_pieces(jnp.concatenate([batch_features, centre_features], axis=0))
     batch, far = assemble(pieces)
     batch_other = from_other(batch)
@@ -458,13 +467,13 @@
     target = jnp.concatenate([target_mine, from_other(target_theirs)], axis=0)
     parts = lax.all_to_all(pred, ring, 0, 0)
     residuals = settle(parts, target)
-    residual_full = lax.all_to_all(residuals, ring, 0, 0)
+    residual_full = backward(residuals, ring)
 
     (far_tile,) = tile_of(far, far_other, centres, half)
     *fars, sums = far_terms(far_tile, from_other(far_tile), half)
     parts = lax.all_to_all(gradient(place, tiles, residual_full, sums), plane, 0, 0)
     grad, copies, largest = collect(parts)
-    grad_full = lax.all_to_all(copies, plane, 0, 0)
+    grad_full = backward(copies, plane)
     parts = lax.all_to_all(product(place, fars, grad_full, largest), ring, 0, 0)
     theta = finish(parts, grad, total_rows / math.sqrt(total_rows))
     return to_rows(residuals[0], theta)

time: 183 us -> 179 us (0.978)
  starting transfers between devices: 46 us -> 57.3 us
  waiting for transfers between devices: 59.9 us -> 51.4 us
  blocking collectives: 39.7 us -> 33.1 us
    all_to_all x1, starting transfers between devices: 3.54 us -> 15.6 us  [shards(): parts = lax.all_to_all(product(place, fars, grad_full, largest), ring, 0, 0)]
    all_to_all x2, waiting for transfers between devices: 15.9 us -> 7.4 us  [backward(): return lax.all_to_all(copies, axis, 0, 0, axis_index_groups=order)]
    all_to_all x1, blocking collectives: 18.3 us -> 14.1 us  [backward(): return lax.all_to_all(copies, axis, 0, 0, axis_index_groups=order)]
    all_to_all x2, starting transfers between devices: 11.3 us -> 14.1 us  [backward(): return lax.all_to_all(copies, axis, 0, 0, axis_index_groups=order)]
    all_to_all x1, blocking collectives: 21.4 us -> 19 us  [shards(): lax.all_to_all(gradient(place, tiles, residual_full, sums), plane, 0, 0)]
    ppermute x7, starting transfers between devices: 11.9 us -> 9.75 us  [from_other(): return lax.ppermute(value, 'core', swap)]
  transfers between devices with their start and end apart: 18 -> 18, of which waited for: 11 -> 10; matrix products, arithmetic and copies ran while one was open for 0% -> 0% of each run, Pallas kernels for 6% -> 6%
where the time goes in v5:
time: 179 us
  starting transfers between devices  57.3 us (32%)
  waiting for transfers between devices  51.4 us (29%)
  blocking collectives  33.1 us (18%)
  Pallas kernels  28.5 us (16%)
  local copies, waits for them, and re-layouts  6.84 us (4%)
    pallas_call x2, Pallas kernels, tile_of(): pl.pallas_call(functools.partial(tile_kernel, half, shared), in_specs=[wh...  19.3 us
    all_to_all x1, blocking collectives, shards(): lax.all_to_all(gradient(place, tiles, residual_full, sums), plane, 0, 0)  19 us
    ppermute x7, waiting for transfers between devices, hop(): return lax.ppermute(held, ('z_lo', 'z_hi'), pairs)  17.5 us
    all_to_all x1, starting transfers between devices, shards(): parts = lax.all_to_all(product(place, fars, grad_full, largest), ring, 0, 0)  15.6 us
    all_to_all x1, waiting for transfers between devices, shards(): parts = lax.all_to_all(product(place, fars, grad_full, largest), ring, 0, 0)  15.4 us
    all_to_all x2, starting transfers between devices, backward(): return lax.all_to_all(copies, axis, 0, 0, axis_index_groups=order)  14.1 us
    all_to_all x1, blocking collectives, backward(): return lax.all_to_all(copies, axis, 0, 0, axis_index_groups=order)  14.1 us
    ppermute x7, starting transfers between devices, hop(): return lax.ppermute(held, ('z_lo', 'z_hi'), pairs)  11.1 us
  transfers between devices with their start and end apart: 18, of which 10 were waited for; matrix products, arithmetic and copies ran while one was open for 0% of the time, Pallas kernels for 6%

profile of v5, /device:TPU:1, one launch (start us, length us, event | category | flops | bytes accessed | tf_op | source)
XLA Modules:
  0.0 178.7 jit_solution(7590704679201112216)
XLA Ops:
  0.6 2.6 %shard_map.60 = f32[16,32,1280]{2,1,0:T(8,128)} custom-call(s32[1]{0:T(128)} %bitcast.1.core_ref, f32[32,512]{1,0:T(8,128)} %weight_ref.1, f32[32,768]{1,0:T(8,128)} %centre_ref.1), custom_call_target="tpu_custom_call" | custom-call | bytes 2621440 | tf_op jit(solution)/shard_map/pallas_call | solution.py:367
  3.3 10.2 %all-to-all-start = ((f32[16,32,1280]{2,1,0:T(8,128)}), f32[16,32,1280]{2,1,0:T(8,128)}, u32[]{:S(2)}, u32[]{:S(2)}) async-start(f32[16,32,1280]{2,1,0:T(8,128)} %shard_map.60), calls=%async_computation | async-start | bytes 5242880 | tf_op jit(solution)/shard_map/all_to_all | solution.py:400
  15.2 4.0 %collective-permute-start = (f32[64,768]{1,0:T(8,128)S(1)}, f32[64,768]{1,0:T(8,128)S(1)}, u32[]{:S(2)}, u32[]{:S(2)}) collective-permute-start(f32[64,768]{1,0:T(8,128)S(1)} %constant_dynamic-update-slice_fusion.refs_0_), channel_id=1, source_target_pairs={{0,50},{16,0},{32,16},{48,32},{2,48},{18,2},{34,18},{50,34},{1,51}... | collective-permute-start | bytes 589832 | tf_op jit(solution)/shard_map/ppermute | solution.py:416
  19.2 4.3 %collective-permute-done.3.refs_7_ = f32[64,768]{1,0:T(8,128)S(1)} collective-permute-done((f32[64,768]{1,0:T(8,128)S(1)}, f32[64,768]{1,0:T(8,128)S(1)}, u32[]{:S(2)}, u32[]{:S(2)}) %collective-permute-start.3) | collective-permute-done | bytes 196640 | tf_op jit(solution)/shard_map/ppermute | solution.py:416
  23.6 2.7 %collective-permute-start.1 = (f32[64,768]{1,0:T(8,128)S(1)}, f32[64,768]{1,0:T(8,128)S(1)}, u32[]{:S(2)}, u32[]{:S(2)}) collective-permute-start(f32[64,768]{1,0:T(8,128)S(1)} %collective-permute-done.refs_1_), channel_id=1, source_target_pairs={{0,50},{16,0},{32,16},{48,32},{2,48},{18,2},{34,18},{50,34},{1,51}... | collective-permute-start | bytes 589832 | tf_op jit(solution)/shard_map/ppermute | solution.py:416
  26.3 3.6 %collective-permute-done.4.refs_6_ = f32[64,768]{1,0:T(8,128)S(1)} collective-permute-done((f32[64,768]{1,0:T(8,128)S(1)}, f32[64,768]{1,0:T(8,128)S(1)}, u32[]{:S(2)}, u32[]{:S(2)}) %collective-permute-start.4) | collective-permute-done | bytes 196640 | tf_op jit(solution)/shard_map/ppermute | solution.py:416
  29.8 2.7 %collective-permute-start.2 = (f32[64,768]{1,0:T(8,128)S(1)}, f32[64,768]{1,0:T(8,128)S(1)}, u32[]{:S(2)}, u32[]{:S(2)}) collective-permute-start(f32[64,768]{1,0:T(8,128)S(1)} %collective-permute-done.1.refs_2_), channel_id=1, source_target_pairs={{0,50},{16,0},{32,16},{48,32},{2,48},{18,2},{34,18},{50,34},{1,51}... | collective-permute-start | bytes 589832 | tf_op jit(solution)/shard_map/ppermute | solution.py:416
  32.5 3.5 %collective-permute-done.5.refs_5_ = f32[64,768]{1,0:T(8,128)S(1)} collective-permute-done((f32[64,768]{1,0:T(8,128)S(1)}, f32[64,768]{1,0:T(8,128)S(1)}, u32[]{:S(2)}, u32[]{:S(2)}) %collective-permute-start.5) | collective-permute-done | bytes 196640 | tf_op jit(solution)/shard_map/ppermute | solution.py:416
  36.0 6.1 %collective-permute-done.6.refs_4_ = f32[64,768]{1,0:T(8,128)S(1)} collective-permute-done((f32[64,768]{1,0:T(8,128)S(1)}, f32[64,768]{1,0:T(8,128)S(1)}, u32[]{:S(2)}, u32[]{:S(2)}) %collective-permute-start.6) | collective-permute-done | bytes 196640 | tf_op jit(solution)/shard_map/ppermute | solution.py:416
  42.2 3.8 %collective-permute-start.7 = (f32[256,768]{1,0:T(8,128)S(1)}, f32[256,768]{1,0:T(8,128)S(1)}, u32[]{:S(2)}, u32[]{:S(2)}) collective-permute-start(f32[256,768]{1,0:T(8,128)S(1)} %get-tuple-element.13.own_ref), channel_id=1, source_target_pairs={{0,1},{1,0},{2,3},{3,2},{4,5},{5,4},{6,7},{7,6},{8,9},{9,8},{10,11... | collective-permute-start | bytes 2359304 | tf_op jit(solution)/shard_map/ppermute | solution.py:428
  46.1 1.9 %collective-permute-done.7.other_ref = f32[256,768]{1,0:T(8,128)S(1)} collective-permute-done((f32[256,768]{1,0:T(8,128)S(1)}, f32[256,768]{1,0:T(8,128)S(1)}, u32[]{:S(2)}, u32[]{:S(2)}) %collective-permute-start.7) | collective-permute-done | bytes 786464 | tf_op jit(solution)/shard_map/ppermute | solution.py:428
  48.9 10.3 %shard_map.61 = (f32[512,512]{1,0:T(8,128)}, f32[512,256]{1,0:T(8,128)}, f32[512,256]{1,0:T(8,128)}) custom-call(f32[256,768]{1,0:T(8,128)} %copy-done.8, f32[256,768]{1,0:T(8,128)} %copy-done.13, f32[16,32,1280]{2,1,0:T(8,128)} %all-to-all-done.packed_ref), custom_call_target="tpu_custom_call" | custom-call | flops 2415919104 | bytes 6291456 | tf_op jit(solution)/shard_map/pallas_call | solution.py:160
  63.6 6.7 %all-to-all-start.1 = ((f32[8,64,256]{2,1,0:T(8,128)}), f32[8,64,256]{2,1,0:T(8,128)S(1)}, u32[]{:S(2)}, u32[]{:S(2)}) async-start(f32[8,64,256]{2,1,0:T(8,128)} %shard_map.62), calls=%async_computation.1 | async-start | bytes 1048576 | tf_op jit(solution)/shard_map/all_to_all | solution.py:468
  72.0 9.0 %shard_map.64.own_ref = f32[512,512]{1,0:T(8,128)} custom-call(f32[256,768]{1,0:T(8,128)} %copy-done.7, f32[256,768]{1,0:T(8,128)} %copy-done.12, f32[16,32,1280]{2,1,0:T(8,128)} %all-to-all-done.packed_ref), custom_call_target="tpu_custom_call" | custom-call | flops 2415919104 | bytes 6291456 | tf_op jit(solution)/shard_map/pallas_call | solution.py:160
  81.6 6.7 %all-to-all-done.1.parts_ref = f32[8,64,256]{2,1,0:T(8,128)S(1)} async-done(((f32[8,64,256]{2,1,0:T(8,128)}), f32[8,64,256]{2,1,0:T(8,128)S(1)}, u32[]{:S(2)}, u32[]{:S(2)}) %all-to-all-start.1) | async-done | bytes 524320 | tf_op jit(solution)/shard_map/all_to_all | solution.py:468
  89.1 4.0 %all-to-all-start.2 = ((f32[8,64,256]{2,1,0:T(8,128)}), f32[8,64,256]{2,1,0:T(8,128)S(1)}, u32[]{:S(2)}, u32[]{:S(2)}) async-start(f32[8,64,256]{2,1,0:T(8,128)} %shard_map.63), calls=%async_computation.2 | async-start | bytes 1048576 | tf_op jit(solution)/shard_map/all_to_all | solution.py:400
  95.4 7.4 %all-to-all-done.2.residual_ref = f32[8,64,256]{2,1,0:T(8,128)S(1)} async-done(((f32[8,64,256]{2,1,0:T(8,128)}), f32[8,64,256]{2,1,0:T(8,128)S(1)}, u32[]{:S(2)}, u32[]{:S(2)}) %all-to-all-start.2) | async-done | bytes 524320 | tf_op jit(solution)/shard_map/all_to_all | solution.py:400
  104.0 2.3 %shard_map.66 = f32[16,72,256]{2,1,0:T(8,128)S(1)} custom-call(s32[1]{0:T(128)} %bitcast.place_ref, f32[512,512]{1,0:T(8,128)S(1)} %copy-done.1, f32[512,512]{1,0:T(8,128)} %collective-permute-done.12.other_ref, f32[8,64,256]{2,1,0:T(8,128)S(1)} %all-to-all-done.2.residual_ref, f32[8,256]{1,0:T(8,128)S(1)} %get-tuple-element.20.sums_ref), custom_call_target="tpu_custom_call" | custom-call | flops 805306368 | bytes 4194304 | tf_op jit(solution)/shard_map/pallas_call | solution.py:268
  106.4 19.0 %all_to_all.30.parts_ref = f32[16,72,256]{2,1,0:T(8,128)S(1)} all-to-all(f32[16,72,256]{2,1,0:T(8,128)S(1)} %shard_map.66), channel_id=1, replica_groups=mesh['x'=4,'z_lo'=4,'y'=4,'z_hi'=2,'core'=2] {'x','y'}, dimensions={0} | all-to-all | bytes 2359296 | tf_op jit(solution)/shard_map/all_to_all | solution.py:474
  125.5 14.1 %all_to_all.31.grad_ref = f32[16,64,256]{2,1,0:T(8,128)S(1)} all-to-all(f32[16,64,256]{2,1,0:T(8,128)S(1)} %get-tuple-element.21), channel_id=1, replica_groups={{204,200,196,192,140,136,132,128,76,72,68,64,12,8,4,0},{205,201,197,193..., dimensions={0} | all-to-all | bytes 2097152 | tf_op jit(solution)/shard_map/all_to_all | solution.py:400
  139.6 1.8 %shard_map.68 = f32[8,72,256]{2,1,0:T(8,128)} custom-call(s32[1]{0:T(128)} %bitcast.place_ref, bf16[512,1024]{1,0:T(8,128)(2,1)S(1)} %copy-done.3, bf16[512,1024]{1,0:T(8,128)(2,1)S(1)} %copy-done.5, f32[16,64,256]{2,1,0:T(8,128)S(1)} %all_to_all.31.grad_ref, f32[8,256]{1,0:T(8,128)S(1)} %get-tuple-element.22.largest_ref), custom_call_target="tpu_custom_call" | custom-call | flops 805306368 | bytes 4194304 | tf_op jit(solution)/shard_map/pallas_call | solution.py:316
  141.4 15.6 %all-to-all-start.5 = ((f32[8,72,256]{2,1,0:T(8,128)}), f32[8,72,256]{2,1,0:T(8,128)S(1)}, u32[]{:S(2)}, u32[]{:S(2)}) async-start(f32[8,72,256]{2,1,0:T(8,128)} %shard_map.68), calls=%async_computation.5 | async-start | bytes 1179648 | tf_op jit(solution)/shard_map/all_to_all | solution.py:477
  157.8 15.4 %all-to-all-done.5.refs_0_ = f32[8,72,256]{2,1,0:T(8,128)S(1)} async-done(((f32[8,72,256]{2,1,0:T(8,128)}), f32[8,72,256]{2,1,0:T(8,128)S(1)}, u32[]{:S(2)}, u32[]{:S(2)}) %all-to-all-start.5) | async-done | bytes 589856 | tf_op jit(solution)/shard_map/all_to_all | solution.py:477
  173.3 3.8 %collective-permute-start.13 = (f32[64,256]{1,0:T(8,128)S(1)}, f32[64,256]{1,0:T(8,128)S(1)}, u32[]{:S(2)}, u32[]{:S(2)}) collective-permute-start(f32[64,256]{1,0:T(8,128)S(1)} %pad_maximum_fusion.3), channel_id=1, source_target_pairs={{0,1},{1,0},{2,3},{3,2},{4,5},{5,4},{6,7},{7,6},{8,9},{9,8},{10,11... | collective-permute-start | bytes 196616 | tf_op jit(solution)/shard_map/ppermute | solution.py:428
  (62 shorter events, 16.4 us)
Async XLA Ops:
  3.2 10.2 %copy-start.9 = (f32[32,768]{1,0:T(8,128)S(1)}, f32[32,768]{1,0:T(8,128)}, u32[]{:S(2)}) copy-start(f32[32,768]{1,0:T(8,128)} %centre_ref.1) | copy-start | bytes 294916
  3.3 44.7 %all-to-all-start = ((f32[16,32,1280]{2,1,0:T(8,128)}), f32[16,32,1280]{2,1,0:T(8,128)}, u32[]{:S(2)}, u32[]{:S(2)}) async-start(f32[16,32,1280]{2,1,0:T(8,128)} %shard_map.60), calls=%async_computation | async-start | bytes 5242880 | tf_op jit(solution)/shard_map/all_to_all | solution.py:400
  13.5 10.1 %collective-permute-start.3 = (f32[64,768]{1,0:T(8,128)S(1)}, f32[64,768]{1,0:T(8,128)S(1)}, u32[]{:S(2)}, u32[]{:S(2)}) collective-permute-start(f32[64,768]{1,0:T(8,128)S(1)} %constant_dynamic-update-slice_fusion.refs_0_), channel_id=1, source_target_pairs={{0,16},{16,32},{32,48},{48,2},{2,18},{18,34},{34,50},{50,0},{1,17}... | collective-permute-start | bytes 589832 | tf_op jit(solution)/shard_map/ppermute | solution.py:416
  15.2 8.4 %collective-permute-start = (f32[64,768]{1,0:T(8,128)S(1)}, f32[64,768]{1,0:T(8,128)S(1)}, u32[]{:S(2)}, u32[]{:S(2)}) collective-permute-start(f32[64,768]{1,0:T(8,128)S(1)} %constant_dynamic-update-slice_fusion.refs_0_), channel_id=1, source_target_pairs={{0,50},{16,0},{32,16},{48,32},{2,48},{18,2},{34,18},{50,34},{1,51}... | collective-permute-start | bytes 589832 | tf_op jit(solution)/shard_map/ppermute | solution.py:416
  23.6 6.3 %collective-permute-start.4 = (f32[64,768]{1,0:T(8,128)S(1)}, f32[64,768]{1,0:T(8,128)S(1)}, u32[]{:S(2)}, u32[]{:S(2)}) collective-permute-start(f32[64,768]{1,0:T(8,128)S(1)} %collective-permute-done.3.refs_7_), channel_id=1, source_target_pairs={{0,16},{16,32},{32,48},{48,2},{2,18},{18,34},{34,50},{50,0},{1,17}... | collective-permute-start | bytes 589832 | tf_op jit(solution)/shard_map/ppermute | solution.py:416
  23.6 6.3 %collective-permute-start.1 = (f32[64,768]{1,0:T(8,128)S(1)}, f32[64,768]{1,0:T(8,128)S(1)}, u32[]{:S(2)}, u32[]{:S(2)}) collective-permute-start(f32[64,768]{1,0:T(8,128)S(1)} %collective-permute-done.refs_1_), channel_id=1, source_target_pairs={{0,50},{16,0},{32,16},{48,32},{2,48},{18,2},{34,18},{50,34},{1,51}... | collective-permute-start | bytes 589832 | tf_op jit(solution)/shard_map/ppermute | solution.py:416
  29.8 6.1 %collective-permute-start.5 = (f32[64,768]{1,0:T(8,128)S(1)}, f32[64,768]{1,0:T(8,128)S(1)}, u32[]{:S(2)}, u32[]{:S(2)}) collective-permute-start(f32[64,768]{1,0:T(8,128)S(1)} %collective-permute-done.4.refs_6_), channel_id=1, source_target_pairs={{0,16},{16,32},{32,48},{48,2},{2,18},{18,34},{34,50},{50,0},{1,17}... | collective-permute-start | bytes 589832 | tf_op jit(solution)/shard_map/ppermute | solution.py:416
  29.8 6.1 %collective-permute-start.2 = (f32[64,768]{1,0:T(8,128)S(1)}, f32[64,768]{1,0:T(8,128)S(1)}, u32[]{:S(2)}, u32[]{:S(2)}) collective-permute-start(f32[64,768]{1,0:T(8,128)S(1)} %collective-permute-done.1.refs_2_), channel_id=1, source_target_pairs={{0,50},{16,0},{32,16},{48,32},{2,48},{18,2},{34,18},{50,34},{1,51}... | collective-permute-start | bytes 589832 | tf_op jit(solution)/shard_map/ppermute | solution.py:416
  36.0 6.1 %collective-permute-start.6 = (f32[64,768]{1,0:T(8,128)S(1)}, f32[64,768]{1,0:T(8,128)S(1)}, u32[]{:S(2)}, u32[]{:S(2)}) collective-permute-start(f32[64,768]{1,0:T(8,128)S(1)} %collective-permute-done.5.refs_5_), channel_id=1, source_target_pairs={{0,16},{16,32},{32,48},{48,2},{2,18},{18,34},{34,50},{50,0},{1,17}... | collective-permute-start | bytes 589832 | tf_op jit(solution)/shard_map/ppermute | solution.py:416
  42.2 17.7 %copy-start.7 = (f32[256,768]{1,0:T(8,128)}, f32[256,768]{1,0:T(8,128)S(1)}, u32[]{:S(2)}) copy-start(f32[256,768]{1,0:T(8,128)S(1)} %get-tuple-element.16.own_ref) | copy-start | bytes 2359300
  42.2 5.8 %collective-permute-start.7 = (f32[256,768]{1,0:T(8,128)S(1)}, f32[256,768]{1,0:T(8,128)S(1)}, u32[]{:S(2)}, u32[]{:S(2)}) collective-permute-start(f32[256,768]{1,0:T(8,128)S(1)} %get-tuple-element.13.own_ref), channel_id=1, source_target_pairs={{0,1},{1,0},{2,3},{3,2},{4,5},{5,4},{6,7},{7,6},{8,9},{9,8},{10,11... | collective-permute-start | bytes 2359304 | tf_op jit(solution)/shard_map/ppermute | solution.py:428
  48.9 21.4 %copy-start.11 = (f32[32,512]{1,0:T(8,128)S(1)}, f32[32,512]{1,0:T(8,128)}, u32[]{:S(2)}) copy-start(f32[32,512]{1,0:T(8,128)} %param.6) | copy-start | bytes 196612
  59.2 2.4 %collective-permute-start.8 = (f32[512,256]{1,0:T(8,128)}, f32[512,256]{1,0:T(8,128)S(1)}, u32[]{:S(2)}, u32[]{:S(2)}) collective-permute-start(f32[512,256]{1,0:T(8,128)} %get-tuple-element.15), channel_id=1, source_target_pairs={{0,1},{1,0},{2,3},{3,2},{4,5},{5,4},{6,7},{7,6},{8,9},{9,8},{10,11... | collective-permute-start | bytes 1572872 | tf_op jit(solution)/shard_map/ppermute | solution.py:428
  59.9 11.2 %collective-permute-start.10 = (f32[256,768]{1,0:T(8,128)S(1)}, f32[256,768]{1,0:T(8,128)S(1)}, u32[]{:S(2)}, u32[]{:S(2)}) collective-permute-start(f32[256,768]{1,0:T(8,128)S(1)} %get-tuple-element.16.own_ref), channel_id=1, source_target_pairs={{0,1},{1,0},{2,3},{3,2},{4,5},{5,4},{6,7},{7,6},{8,9},{9,8},{10,11... | collective-permute-start | bytes 2359304 | tf_op jit(solution)/shard_map/ppermute | solution.py:428
  63.6 24.7 %all-to-all-start.1 = ((f32[8,64,256]{2,1,0:T(8,128)}), f32[8,64,256]{2,1,0:T(8,128)S(1)}, u32[]{:S(2)}, u32[]{:S(2)}) async-start(f32[8,64,256]{2,1,0:T(8,128)} %shard_map.62), calls=%async_computation.1 | async-start | bytes 1048576 | tf_op jit(solution)/shard_map/all_to_all | solution.py:468
  70.3 11.2 %collective-permute-start.9 = (f32[32,256]{1,0:T(8,128)S(1)}, f32[32,256]{1,0:T(8,128)S(1)}, u32[]{:S(2)}, u32[]{:S(2)}) collective-permute-start(f32[32,256]{1,0:T(8,128)S(1)} %get-tuple-element.33), channel_id=1, source_target_pairs={{0,1},{1,0},{2,3},{3,2},{4,5},{5,4},{6,7},{7,6},{8,9},{9,8},{10,11... | collective-permute-start | bytes 98312 | tf_op jit(solution)/shard_map/ppermute | solution.py:428
  81.0 12.1 %copy-start = (f32[512,512]{1,0:T(8,128)S(1)}, f32[512,512]{1,0:T(8,128)}, u32[]{:S(2)}) copy-start(f32[512,512]{1,0:T(8,128)} %shard_map.64.own_ref) | copy-start | bytes 3145732
  81.0 12.1 %collective-permute-start.11 = (f32[512,512]{1,0:T(8,128)}, f32[512,512]{1,0:T(8,128)S(1)}, u32[]{:S(2)}, u32[]{:S(2)}) collective-permute-start(f32[512,512]{1,0:T(8,128)} %shard_map.64.own_ref), channel_id=1, source_target_pairs={{0,1},{1,0},{2,3},{3,2},{4,5},{5,4},{6,7},{7,6},{8,9},{9,8},{10,11... | collective-permute-start | bytes 3145736 | tf_op jit(solution)/shard_map/ppermute | solution.py:428
  81.1 14.3 %collective-permute-start.12 = (f32[512,512]{1,0:T(8,128)}, f32[512,512]{1,0:T(8,128)}, u32[]{:S(2)}, u32[]{:S(2)}) collective-permute-start(f32[512,512]{1,0:T(8,128)} %get-tuple-element.19.own_ref), channel_id=1, source_target_pairs={{0,1},{1,0},{2,3},{3,2},{4,5},{5,4},{6,7},{7,6},{8,9},{9,8},{10,11... | collective-permute-start | bytes 3145736 | tf_op jit(solution)/shard_map/ppermute | solution.py:428
  89.1 13.7 %all-to-all-start.2 = ((f32[8,64,256]{2,1,0:T(8,128)}), f32[8,64,256]{2,1,0:T(8,128)S(1)}, u32[]{:S(2)}, u32[]{:S(2)}) async-start(f32[8,64,256]{2,1,0:T(8,128)} %shard_map.63), calls=%async_computation.2 | async-start | bytes 1048576 | tf_op jit(solution)/shard_map/all_to_all | solution.py:400
  106.3 33.2 %copy-start.3 = (bf16[512,1024]{1,0:T(8,128)(2,1)S(1)}, bf16[512,1024]{1,0:T(8,128)(2,1)}, u32[]{:S(2)}) copy-start(bf16[512,1024]{1,0:T(8,128)(2,1)} %copy-done.2) | copy-start | bytes 3145732
  106.3 33.2 %copy-start.5 = (bf16[512,1024]{1,0:T(8,128)(2,1)S(1)}, bf16[512,1024]{1,0:T(8,128)(2,1)}, u32[]{:S(2)}) copy-start(bf16[512,1024]{1,0:T(8,128)(2,1)} %copy-done.4) | copy-start | bytes 3145732
  141.4 31.7 %all-to-all-start.5 = ((f32[8,72,256]{2,1,0:T(8,128)}), f32[8,72,256]{2,1,0:T(8,128)S(1)}, u32[]{:S(2)}, u32[]{:S(2)}) async-start(f32[8,72,256]{2,1,0:T(8,128)} %shard_map.68), calls=%async_computation.5 | async-start | bytes 1179648 | tf_op jit(solution)/shard_map/all_to_all | solution.py:477
  173.3 4.7 %collective-permute-start.13 = (f32[64,256]{1,0:T(8,128)S(1)}, f32[64,256]{1,0:T(8,128)S(1)}, u32[]{:S(2)}, u32[]{:S(2)}) collective-permute-start(f32[64,256]{1,0:T(8,128)S(1)} %pad_maximum_fusion.3), channel_id=1, source_target_pairs={{0,1},{1,0},{2,3},{3,2},{4,5},{5,4},{6,7},{7,6},{8,9},{9,8},{10,11... | collective-permute-start | bytes 196616 | tf_op jit(solution)/shard_map/ppermute | solution.py:428
  (8 other events, 22.0 us)

commit v6 on v5

--- a/solution.py
+++ b/solution.py
@@ -14,6 +14,8 @@
 plane = ("x", "y")
 ring = ("z_hi", "z_lo")
 swap = [(0, 1), (1, 0)]
+ring_low = 4
+ring_order = ("z_lo", "z_hi")
 rider = 8
 vmem_bytes = 24 * 1024 * 1024
 most_bytes = 60 * 1024 * 1024
@@ -174,7 +176,8 @@
 
 
 def ring_places(place_ref, count):
-    return [lax.rem(place_ref[0] + step, count) for step in range(count)]
+    places = [lax.rem(place_ref[0] + step, count) for step in range(count)]
+    return [lax.rem(place, ring_low) * (count // ring_low) + lax.div(place, ring_low) for place in places]
 
 
 def from_ring(ref, places, rows):
@@ -306,7 +309,8 @@
     count, _, half = out_ref.shape
     grads = jnp.concatenate([flat(grad_ref[:, :rows]), flat(grad_ref[:, rows:])], axis=0)
     total = mul_terms([high_ref[...], low_ref[...]], cut(grads, 2), 1, 0)
-    to_ring(total, out_ref, ring_places(place_ref, count), rows)
+    places = [count - 1 - place for place in ring_places(place_ref, count)]
+    to_ring(total, out_ref, places, rows)
     out_ref[:, 2 * rows :] = jnp.broadcast_to(largest_ref[...][None], (count, rider, half))
 
 
@@ -465,16 +469,16 @@
     tiles = tile, from_other(tile)
     target_mine, target_theirs = halves(targets)
     target = jnp.concatenate([target_mine, from_other(target_theirs)], axis=0)
-    parts = lax.all_to_all(pred, ring, 0, 0)
+    parts = lax.all_to_all(pred, ring_order, 0, 0)
     residuals = settle(parts, target)
-    residual_full = backward(residuals, ring)
+    residual_full = backward(residuals, ring_order)
 
     (far_tile,) = tile_of(far, far_other, centres, half)
     *fars, sums = far_terms(far_tile, from_other(far_tile), half)
     parts = lax.all_to_all(gradient(place, tiles, residual_full, sums), plane, 0, 0)
     grad, copies, largest = collect(parts)
     grad_full = backward(copies, plane)
-    parts = lax.all_to_all(product(place, fars, grad_full, largest), ring, 0, 0)
+    parts = backward(product(place, fars, grad_full, largest), ring_order)
     theta = finish(parts, grad, total_rows / math.sqrt(total_rows))
     return to_rows(residuals[0], theta)
 

time: 179 us -> 174 us (0.972)
  waiting for transfers between devices: 51.4 us -> 41.1 us
  starting transfers between devices: 57.3 us -> 62.2 us
    all_to_all x2 -> x1, waiting for transfers between devices: 22 us -> 1.24 us  [shards(): parts = lax.all_to_all(pred, ring_order, 0, 0)]
    all_to_all x2 -> x3, starting transfers between devices: 14.1 us -> 33.6 us  [backward(): return lax.all_to_all(copies, axis, 0, 0, axis_index_groups=order)]
    all_to_all x2 -> x1, starting transfers between devices: 22.3 us -> 6.73 us  [shards(): parts = lax.all_to_all(pred, ring_order, 0, 0)]
    all_to_all x2 -> x3, waiting for transfers between devices: 7.4 us -> 17.9 us  [backward(): return lax.all_to_all(copies, axis, 0, 0, axis_index_groups=order)]
where the time goes in v6:
time: 174 us
  starting transfers between devices  62.2 us (36%)
  waiting for transfers between devices  41.1 us (24%)
  blocking collectives  33.5 us (19%)
  Pallas kernels  28.5 us (16%)
  local copies, waits for them, and re-layouts  6.84 us (4%)
    all_to_all x3, starting transfers between devices, backward(): return lax.all_to_all(copies, axis, 0, 0, axis_index_groups=order)  33.6 us
    pallas_call x2, Pallas kernels, tile_of(): pl.pallas_call(functools.partial(tile_kernel, half, shared), in_specs=[wh...  19.3 us
    all_to_all x1, blocking collectives, shards(): lax.all_to_all(gradient(place, tiles, residual_full, sums), plane, 0, 0)  19.3 us
    all_to_all x3, waiting for transfers between devices, backward(): return lax.all_to_all(copies, axis, 0, 0, axis_index_groups=order)  17.9 us
    ppermute x7, waiting for transfers between devices, hop(): return lax.ppermute(held, ('z_lo', 'z_hi'), pairs)  17.5 us
    all_to_all x1, blocking collectives, backward(): return lax.all_to_all(copies, axis, 0, 0, axis_index_groups=order)  14.2 us
    ppermute x7, starting transfers between devices, hop(): return lax.ppermute(held, ('z_lo', 'z_hi'), pairs)  11.1 us
    ppermute x7, starting transfers between devices, from_other(): return lax.ppermute(value, 'core', swap)  10.8 us
  transfers between devices with their start and end apart: 18, of which 10 were waited for; matrix products, arithmetic and copies ran while one was open for 0% of the time, Pallas kernels for 6%

profile of v6, /device:TPU:1, one launch (start us, length us, event | category | flops | bytes accessed | tf_op | source)
XLA Modules:
  0.0 173.6 jit_solution(12588129144601815354)
XLA Ops:
  0.6 2.6 %shard_map.60 = f32[16,32,1280]{2,1,0:T(8,128)} custom-call(s32[1]{0:T(128)} %bitcast.1.core_ref, f32[32,512]{1,0:T(8,128)} %weight_ref.1, f32[32,768]{1,0:T(8,128)} %centre_ref.1), custom_call_target="tpu_custom_call" | custom-call | bytes 2621440 | tf_op jit(solution)/shard_map/pallas_call | solution.py:371
  3.3 10.2 %all-to-all-start = ((f32[16,32,1280]{2,1,0:T(8,128)}), f32[16,32,1280]{2,1,0:T(8,128)}, u32[]{:S(2)}, u32[]{:S(2)}) async-start(f32[16,32,1280]{2,1,0:T(8,128)} %shard_map.60), calls=%async_computation | async-start | bytes 5242880 | tf_op jit(solution)/shard_map/all_to_all | solution.py:404
  13.5 1.7 collective-permute-start.3
  15.2 4.0 %collective-permute-start = (f32[64,768]{1,0:T(8,128)S(1)}, f32[64,768]{1,0:T(8,128)S(1)}, u32[]{:S(2)}, u32[]{:S(2)}) collective-permute-start(f32[64,768]{1,0:T(8,128)S(1)} %constant_dynamic-update-slice_fusion.refs_0_), channel_id=1, source_target_pairs={{0,50},{16,0},{32,16},{48,32},{2,48},{18,2},{34,18},{50,34},{1,51}... | collective-permute-start | bytes 589832 | tf_op jit(solution)/shard_map/ppermute | solution.py:420
  19.2 4.3 %collective-permute-done.3.refs_7_ = f32[64,768]{1,0:T(8,128)S(1)} collective-permute-done((f32[64,768]{1,0:T(8,128)S(1)}, f32[64,768]{1,0:T(8,128)S(1)}, u32[]{:S(2)}, u32[]{:S(2)}) %collective-permute-start.3) | collective-permute-done | bytes 196640 | tf_op jit(solution)/shard_map/ppermute | solution.py:420
  23.6 2.7 %collective-permute-start.1 = (f32[64,768]{1,0:T(8,128)S(1)}, f32[64,768]{1,0:T(8,128)S(1)}, u32[]{:S(2)}, u32[]{:S(2)}) collective-permute-start(f32[64,768]{1,0:T(8,128)S(1)} %collective-permute-done.refs_1_), channel_id=1, source_target_pairs={{0,50},{16,0},{32,16},{48,32},{2,48},{18,2},{34,18},{50,34},{1,51}... | collective-permute-start | bytes 589832 | tf_op jit(solution)/shard_map/ppermute | solution.py:420
  26.3 3.6 %collective-permute-done.4.refs_6_ = f32[64,768]{1,0:T(8,128)S(1)} collective-permute-done((f32[64,768]{1,0:T(8,128)S(1)}, f32[64,768]{1,0:T(8,128)S(1)}, u32[]{:S(2)}, u32[]{:S(2)}) %collective-permute-start.4) | collective-permute-done | bytes 196640 | tf_op jit(solution)/shard_map/ppermute | solution.py:420
  29.8 2.7 %collective-permute-start.2 = (f32[64,768]{1,0:T(8,128)S(1)}, f32[64,768]{1,0:T(8,128)S(1)}, u32[]{:S(2)}, u32[]{:S(2)}) collective-permute-start(f32[64,768]{1,0:T(8,128)S(1)} %collective-permute-done.1.refs_2_), channel_id=1, source_target_pairs={{0,50},{16,0},{32,16},{48,32},{2,48},{18,2},{34,18},{50,34},{1,51}... | collective-permute-start | bytes 589832 | tf_op jit(solution)/shard_map/ppermute | solution.py:420
  32.5 3.5 %collective-permute-done.5.refs_5_ = f32[64,768]{1,0:T(8,128)S(1)} collective-permute-done((f32[64,768]{1,0:T(8,128)S(1)}, f32[64,768]{1,0:T(8,128)S(1)}, u32[]{:S(2)}, u32[]{:S(2)}) %collective-permute-start.5) | collective-permute-done | bytes 196640 | tf_op jit(solution)/shard_map/ppermute | solution.py:420
  36.0 6.1 %collective-permute-done.6.refs_4_ = f32[64,768]{1,0:T(8,128)S(1)} collective-permute-done((f32[64,768]{1,0:T(8,128)S(1)}, f32[64,768]{1,0:T(8,128)S(1)}, u32[]{:S(2)}, u32[]{:S(2)}) %collective-permute-start.6) | collective-permute-done | bytes 196640 | tf_op jit(solution)/shard_map/ppermute | solution.py:420
  42.2 3.8 %collective-permute-start.7 = (f32[256,768]{1,0:T(8,128)S(1)}, f32[256,768]{1,0:T(8,128)S(1)}, u32[]{:S(2)}, u32[]{:S(2)}) collective-permute-start(f32[256,768]{1,0:T(8,128)S(1)} %get-tuple-element.13.own_ref), channel_id=1, source_target_pairs={{0,1},{1,0},{2,3},{3,2},{4,5},{5,4},{6,7},{7,6},{8,9},{9,8},{10,11... | collective-permute-start | bytes 2359304 | tf_op jit(solution)/shard_map/ppermute | solution.py:432
  46.1 1.9 %collective-permute-done.7.other_ref = f32[256,768]{1,0:T(8,128)S(1)} collective-permute-done((f32[256,768]{1,0:T(8,128)S(1)}, f32[256,768]{1,0:T(8,128)S(1)}, u32[]{:S(2)}, u32[]{:S(2)}) %collective-permute-start.7) | collective-permute-done | bytes 786464 | tf_op jit(solution)/shard_map/ppermute | solution.py:432
  48.9 10.3 %shard_map.61 = (f32[512,512]{1,0:T(8,128)}, f32[512,256]{1,0:T(8,128)}, f32[512,256]{1,0:T(8,128)}) custom-call(f32[256,768]{1,0:T(8,128)} %copy-done.8, f32[256,768]{1,0:T(8,128)} %copy-done.13, f32[16,32,1280]{2,1,0:T(8,128)} %all-to-all-done.packed_ref), custom_call_target="tpu_custom_call" | custom-call | flops 2415919104 | bytes 6291456 | tf_op jit(solution)/shard_map/pallas_call | solution.py:162
  63.6 6.7 %all-to-all-start.1 = ((f32[8,64,256]{2,1,0:T(8,128)}), f32[8,64,256]{2,1,0:T(8,128)S(1)}, u32[]{:S(2)}, u32[]{:S(2)}) async-start(f32[8,64,256]{2,1,0:T(8,128)} %shard_map.62), calls=%async_computation.1 | async-start | bytes 1048576 | tf_op jit(solution)/shard_map/all_to_all | solution.py:472
  72.0 9.0 %shard_map.64.own_ref = f32[512,512]{1,0:T(8,128)} custom-call(f32[256,768]{1,0:T(8,128)} %copy-done.7, f32[256,768]{1,0:T(8,128)} %copy-done.12, f32[16,32,1280]{2,1,0:T(8,128)} %all-to-all-done.packed_ref), custom_call_target="tpu_custom_call" | custom-call | flops 2415919104 | bytes 6291456 | tf_op jit(solution)/shard_map/pallas_call | solution.py:162
  83.7 9.0 %all-to-all-start.2 = ((f32[8,64,256]{2,1,0:T(8,128)}), f32[8,64,256]{2,1,0:T(8,128)S(1)}, u32[]{:S(2)}, u32[]{:S(2)}) async-start(f32[8,64,256]{2,1,0:T(8,128)} %shard_map.63), calls=%async_computation.2 | async-start | bytes 1048576 | tf_op jit(solution)/shard_map/all_to_all | solution.py:404
  95.0 8.2 %all-to-all-done.2.residual_ref = f32[8,64,256]{2,1,0:T(8,128)S(1)} async-done(((f32[8,64,256]{2,1,0:T(8,128)}), f32[8,64,256]{2,1,0:T(8,128)S(1)}, u32[]{:S(2)}, u32[]{:S(2)}) %all-to-all-start.2) | async-done | bytes 524320 | tf_op jit(solution)/shard_map/all_to_all | solution.py:404
  104.5 2.3 %shard_map.66 = f32[16,72,256]{2,1,0:T(8,128)S(1)} custom-call(s32[1]{0:T(128)} %bitcast.place_ref, f32[512,512]{1,0:T(8,128)S(1)} %copy-done.1, f32[512,512]{1,0:T(8,128)} %collective-permute-done.12.other_ref, f32[8,64,256]{2,1,0:T(8,128)S(1)} %all-to-all-done.2.residual_ref, f32[8,256]{1,0:T(8,128)S(1)} %get-tuple-element.20.sums_ref), custom_call_target="tpu_custom_call" | custom-call | flops 805306368 | bytes 4194304 | tf_op jit(solution)/shard_map/pallas_call | solution.py:271
  106.8 19.3 %all_to_all.30.parts_ref = f32[16,72,256]{2,1,0:T(8,128)S(1)} all-to-all(f32[16,72,256]{2,1,0:T(8,128)S(1)} %shard_map.66), channel_id=1, replica_groups=mesh['x'=4,'z_lo'=4,'y'=4,'z_hi'=2,'core'=2] {'x','y'}, dimensions={0} | all-to-all | bytes 2359296 | tf_op jit(solution)/shard_map/all_to_all | solution.py:478
  126.2 14.2 %all_to_all.31.grad_ref = f32[16,64,256]{2,1,0:T(8,128)S(1)} all-to-all(f32[16,64,256]{2,1,0:T(8,128)S(1)} %get-tuple-element.21), channel_id=1, replica_groups={{204,200,196,192,140,136,132,128,76,72,68,64,12,8,4,0},{205,201,197,193..., dimensions={0} | all-to-all | bytes 2097152 | tf_op jit(solution)/shard_map/all_to_all | solution.py:404
  140.4 1.8 %shard_map.68 = f32[8,72,256]{2,1,0:T(8,128)} custom-call(s32[1]{0:T(128)} %bitcast.place_ref, bf16[512,1024]{1,0:T(8,128)(2,1)S(1)} %copy-done.3, bf16[512,1024]{1,0:T(8,128)(2,1)S(1)} %copy-done.5, f32[16,64,256]{2,1,0:T(8,128)S(1)} %all_to_all.31.grad_ref, f32[8,256]{1,0:T(8,128)S(1)} %get-tuple-element.22.largest_ref), custom_call_target="tpu_custom_call" | custom-call | flops 805306368 | bytes 4194304 | tf_op jit(solution)/shard_map/pallas_call | solution.py:320
  142.3 14.4 %all-to-all-start.5 = ((f32[8,72,256]{2,1,0:T(8,128)}), f32[8,72,256]{2,1,0:T(8,128)S(1)}, u32[]{:S(2)}, u32[]{:S(2)}) async-start(f32[8,72,256]{2,1,0:T(8,128)} %shard_map.68), calls=%async_computation.5 | async-start | bytes 1179648 | tf_op jit(solution)/shard_map/all_to_all | solution.py:404
  157.4 9.7 %all-to-all-done.5.refs_0_ = f32[8,72,256]{2,1,0:T(8,128)S(1)} async-done(((f32[8,72,256]{2,1,0:T(8,128)}), f32[8,72,256]{2,1,0:T(8,128)S(1)}, u32[]{:S(2)}, u32[]{:S(2)}) %all-to-all-start.5) | async-done | bytes 589856 | tf_op jit(solution)/shard_map/all_to_all | solution.py:404
  167.2 4.8 %collective-permute-start.13 = (f32[64,256]{1,0:T(8,128)S(1)}, f32[64,256]{1,0:T(8,128)S(1)}, u32[]{:S(2)}, u32[]{:S(2)}) collective-permute-start(f32[64,256]{1,0:T(8,128)S(1)} %pad_maximum_fusion.3), channel_id=1, source_target_pairs={{0,1},{1,0},{2,3},{3,2},{4,5},{5,4},{6,7},{7,6},{8,9},{9,8},{10,11... | collective-permute-start | bytes 196616 | tf_op jit(solution)/shard_map/ppermute | solution.py:432
  (62 shorter events, 15.9 us)
Async XLA Ops:
  3.2 10.2 %copy-start.9 = (f32[32,768]{1,0:T(8,128)S(1)}, f32[32,768]{1,0:T(8,128)}, u32[]{:S(2)}) copy-start(f32[32,768]{1,0:T(8,128)} %centre_ref.1) | copy-start | bytes 294916
  3.3 44.7 %all-to-all-start = ((f32[16,32,1280]{2,1,0:T(8,128)}), f32[16,32,1280]{2,1,0:T(8,128)}, u32[]{:S(2)}, u32[]{:S(2)}) async-start(f32[16,32,1280]{2,1,0:T(8,128)} %shard_map.60), calls=%async_computation | async-start | bytes 5242880 | tf_op jit(solution)/shard_map/all_to_all | solution.py:404
  13.5 10.1 %collective-permute-start.3 = (f32[64,768]{1,0:T(8,128)S(1)}, f32[64,768]{1,0:T(8,128)S(1)}, u32[]{:S(2)}, u32[]{:S(2)}) collective-permute-start(f32[64,768]{1,0:T(8,128)S(1)} %constant_dynamic-update-slice_fusion.refs_0_), channel_id=1, source_target_pairs={{0,16},{16,32},{32,48},{48,2},{2,18},{18,34},{34,50},{50,0},{1,17}... | collective-permute-start | bytes 589832 | tf_op jit(solution)/shard_map/ppermute | solution.py:420
  15.2 8.4 %collective-permute-start = (f32[64,768]{1,0:T(8,128)S(1)}, f32[64,768]{1,0:T(8,128)S(1)}, u32[]{:S(2)}, u32[]{:S(2)}) collective-permute-start(f32[64,768]{1,0:T(8,128)S(1)} %constant_dynamic-update-slice_fusion.refs_0_), channel_id=1, source_target_pairs={{0,50},{16,0},{32,16},{48,32},{2,48},{18,2},{34,18},{50,34},{1,51}... | collective-permute-start | bytes 589832 | tf_op jit(solution)/shard_map/ppermute | solution.py:420
  23.6 6.3 %collective-permute-start.4 = (f32[64,768]{1,0:T(8,128)S(1)}, f32[64,768]{1,0:T(8,128)S(1)}, u32[]{:S(2)}, u32[]{:S(2)}) collective-permute-start(f32[64,768]{1,0:T(8,128)S(1)} %collective-permute-done.3.refs_7_), channel_id=1, source_target_pairs={{0,16},{16,32},{32,48},{48,2},{2,18},{18,34},{34,50},{50,0},{1,17}... | collective-permute-start | bytes 589832 | tf_op jit(solution)/shard_map/ppermute | solution.py:420
  23.6 6.3 %collective-permute-start.1 = (f32[64,768]{1,0:T(8,128)S(1)}, f32[64,768]{1,0:T(8,128)S(1)}, u32[]{:S(2)}, u32[]{:S(2)}) collective-permute-start(f32[64,768]{1,0:T(8,128)S(1)} %collective-permute-done.refs_1_), channel_id=1, source_target_pairs={{0,50},{16,0},{32,16},{48,32},{2,48},{18,2},{34,18},{50,34},{1,51}... | collective-permute-start | bytes 589832 | tf_op jit(solution)/shard_map/ppermute | solution.py:420
  29.8 6.1 %collective-permute-start.5 = (f32[64,768]{1,0:T(8,128)S(1)}, f32[64,768]{1,0:T(8,128)S(1)}, u32[]{:S(2)}, u32[]{:S(2)}) collective-permute-start(f32[64,768]{1,0:T(8,128)S(1)} %collective-permute-done.4.refs_6_), channel_id=1, source_target_pairs={{0,16},{16,32},{32,48},{48,2},{2,18},{18,34},{34,50},{50,0},{1,17}... | collective-permute-start | bytes 589832 | tf_op jit(solution)/shard_map/ppermute | solution.py:420
  29.8 6.1 %collective-permute-start.2 = (f32[64,768]{1,0:T(8,128)S(1)}, f32[64,768]{1,0:T(8,128)S(1)}, u32[]{:S(2)}, u32[]{:S(2)}) collective-permute-start(f32[64,768]{1,0:T(8,128)S(1)} %collective-permute-done.1.refs_2_), channel_id=1, source_target_pairs={{0,50},{16,0},{32,16},{48,32},{2,48},{18,2},{34,18},{50,34},{1,51}... | collective-permute-start | bytes 589832 | tf_op jit(solution)/shard_map/ppermute | solution.py:420
  36.0 6.1 %collective-permute-start.6 = (f32[64,768]{1,0:T(8,128)S(1)}, f32[64,768]{1,0:T(8,128)S(1)}, u32[]{:S(2)}, u32[]{:S(2)}) collective-permute-start(f32[64,768]{1,0:T(8,128)S(1)} %collective-permute-done.5.refs_5_), channel_id=1, source_target_pairs={{0,16},{16,32},{32,48},{48,2},{2,18},{18,34},{34,50},{50,0},{1,17}... | collective-permute-start | bytes 589832 | tf_op jit(solution)/shard_map/ppermute | solution.py:420
  42.2 17.7 %copy-start.7 = (f32[256,768]{1,0:T(8,128)}, f32[256,768]{1,0:T(8,128)S(1)}, u32[]{:S(2)}) copy-start(f32[256,768]{1,0:T(8,128)S(1)} %get-tuple-element.16.own_ref) | copy-start | bytes 2359300
  42.2 5.8 %collective-permute-start.7 = (f32[256,768]{1,0:T(8,128)S(1)}, f32[256,768]{1,0:T(8,128)S(1)}, u32[]{:S(2)}, u32[]{:S(2)}) collective-permute-start(f32[256,768]{1,0:T(8,128)S(1)} %get-tuple-element.13.own_ref), channel_id=1, source_target_pairs={{0,1},{1,0},{2,3},{3,2},{4,5},{5,4},{6,7},{7,6},{8,9},{9,8},{10,11... | collective-permute-start | bytes 2359304 | tf_op jit(solution)/shard_map/ppermute | solution.py:432
  48.9 21.4 %copy-start.11 = (f32[32,512]{1,0:T(8,128)S(1)}, f32[32,512]{1,0:T(8,128)}, u32[]{:S(2)}) copy-start(f32[32,512]{1,0:T(8,128)} %param.6) | copy-start | bytes 196612
  59.2 2.4 %collective-permute-start.8 = (f32[512,256]{1,0:T(8,128)}, f32[512,256]{1,0:T(8,128)S(1)}, u32[]{:S(2)}, u32[]{:S(2)}) collective-permute-start(f32[512,256]{1,0:T(8,128)} %get-tuple-element.15), channel_id=1, source_target_pairs={{0,1},{1,0},{2,3},{3,2},{4,5},{5,4},{6,7},{7,6},{8,9},{9,8},{10,11... | collective-permute-start | bytes 1572872 | tf_op jit(solution)/shard_map/ppermute | solution.py:432
  59.9 11.2 %collective-permute-start.10 = (f32[256,768]{1,0:T(8,128)S(1)}, f32[256,768]{1,0:T(8,128)S(1)}, u32[]{:S(2)}, u32[]{:S(2)}) collective-permute-start(f32[256,768]{1,0:T(8,128)S(1)} %get-tuple-element.16.own_ref), channel_id=1, source_target_pairs={{0,1},{1,0},{2,3},{3,2},{4,5},{5,4},{6,7},{7,6},{8,9},{9,8},{10,11... | collective-permute-start | bytes 2359304 | tf_op jit(solution)/shard_map/ppermute | solution.py:432
  63.6 19.2 %all-to-all-start.1 = ((f32[8,64,256]{2,1,0:T(8,128)}), f32[8,64,256]{2,1,0:T(8,128)S(1)}, u32[]{:S(2)}, u32[]{:S(2)}) async-start(f32[8,64,256]{2,1,0:T(8,128)} %shard_map.62), calls=%async_computation.1 | async-start | bytes 1048576 | tf_op jit(solution)/shard_map/all_to_all | solution.py:472
  70.3 11.2 %collective-permute-start.9 = (f32[32,256]{1,0:T(8,128)S(1)}, f32[32,256]{1,0:T(8,128)S(1)}, u32[]{:S(2)}, u32[]{:S(2)}) collective-permute-start(f32[32,256]{1,0:T(8,128)S(1)} %get-tuple-element.33), channel_id=1, source_target_pairs={{0,1},{1,0},{2,3},{3,2},{4,5},{5,4},{6,7},{7,6},{8,9},{9,8},{10,11... | collective-permute-start | bytes 98312 | tf_op jit(solution)/shard_map/ppermute | solution.py:432
  81.0 11.7 %copy-start = (f32[512,512]{1,0:T(8,128)S(1)}, f32[512,512]{1,0:T(8,128)}, u32[]{:S(2)}) copy-start(f32[512,512]{1,0:T(8,128)} %shard_map.64.own_ref) | copy-start | bytes 3145732
  81.0 11.7 %collective-permute-start.11 = (f32[512,512]{1,0:T(8,128)}, f32[512,512]{1,0:T(8,128)S(1)}, u32[]{:S(2)}, u32[]{:S(2)}) collective-permute-start(f32[512,512]{1,0:T(8,128)} %shard_map.64.own_ref), channel_id=1, source_target_pairs={{0,1},{1,0},{2,3},{3,2},{4,5},{5,4},{6,7},{7,6},{8,9},{9,8},{10,11... | collective-permute-start | bytes 3145736 | tf_op jit(solution)/shard_map/ppermute | solution.py:432
  81.1 14.0 %collective-permute-start.12 = (f32[512,512]{1,0:T(8,128)}, f32[512,512]{1,0:T(8,128)}, u32[]{:S(2)}, u32[]{:S(2)}) collective-permute-start(f32[512,512]{1,0:T(8,128)} %get-tuple-element.19.own_ref), channel_id=1, source_target_pairs={{0,1},{1,0},{2,3},{3,2},{4,5},{5,4},{6,7},{7,6},{8,9},{9,8},{10,11... | collective-permute-start | bytes 3145736 | tf_op jit(solution)/shard_map/ppermute | solution.py:432
  83.7 19.6 %all-to-all-start.2 = ((f32[8,64,256]{2,1,0:T(8,128)}), f32[8,64,256]{2,1,0:T(8,128)S(1)}, u32[]{:S(2)}, u32[]{:S(2)}) async-start(f32[8,64,256]{2,1,0:T(8,128)} %shard_map.63), calls=%async_computation.2 | async-start | bytes 1048576 | tf_op jit(solution)/shard_map/all_to_all | solution.py:404
  106.8 33.6 %copy-start.3 = (bf16[512,1024]{1,0:T(8,128)(2,1)S(1)}, bf16[512,1024]{1,0:T(8,128)(2,1)}, u32[]{:S(2)}) copy-start(bf16[512,1024]{1,0:T(8,128)(2,1)} %copy-done.2) | copy-start | bytes 3145732
  106.8 33.6 %copy-start.5 = (bf16[512,1024]{1,0:T(8,128)(2,1)S(1)}, bf16[512,1024]{1,0:T(8,128)(2,1)}, u32[]{:S(2)}) copy-start(bf16[512,1024]{1,0:T(8,128)(2,1)} %copy-done.4) | copy-start | bytes 3145732
  142.3 24.8 %all-to-all-start.5 = ((f32[8,72,256]{2,1,0:T(8,128)}), f32[8,72,256]{2,1,0:T(8,128)S(1)}, u32[]{:S(2)}, u32[]{:S(2)}) async-start(f32[8,72,256]{2,1,0:T(8,128)} %shard_map.68), calls=%async_computation.5 | async-start | bytes 1179648 | tf_op jit(solution)/shard_map/all_to_all | solution.py:404
  167.2 5.7 %collective-permute-start.13 = (f32[64,256]{1,0:T(8,128)S(1)}, f32[64,256]{1,0:T(8,128)S(1)}, u32[]{:S(2)}, u32[]{:S(2)}) collective-permute-start(f32[64,256]{1,0:T(8,128)S(1)} %pad_maximum_fusion.3), channel_id=1, source_target_pairs={{0,1},{1,0},{2,3},{3,2},{4,5},{5,4},{6,7},{7,6},{8,9},{9,8},{10,11... | collective-permute-start | bytes 196616 | tf_op jit(solution)/shard_map/ppermute | solution.py:432
  (8 other events, 22.0 us)

commit v7 on v6

--- a/solution.py
+++ b/solution.py
@@ -399,8 +399,20 @@
     )(*pieces)
 
 
+def served(axis):
+    count = lax.axis_size(axis)
+    if axis != plane:
+        return list(range(count))
+    side = lax.axis_size("y")
+    return [(place // side + place) % side * side + place % side for place in range(count)]
+
+
+def forward(parts, axis):
+    return lax.all_to_all(parts, axis, 0, 0, axis_index_groups=[served(axis)])
+
+
 def backward(copies, axis):
-    order = [list(range(lax.axis_size(axis)))[::-1]]
+    order = [served(axis)[::-1]]
     return lax.all_to_all(copies, axis, 0, 0, axis_index_groups=order)
 
 
@@ -475,7 +487,7 @@
 
     (far_tile,) = tile_of(far, far_other, centres, half)
     *fars, sums = far_terms(far_tile, from_other(far_tile), half)
-    parts = lax.all_to_all(gradient(place, tiles, residual_full, sums), plane, 0, 0)
+    parts = forward(gradient(place, tiles, residual_full, sums), plane)
     grad, copies, largest = collect(parts)
     grad_full = backward(copies, plane)
     parts = backward(product(place, fars, grad_full, largest), ring_order)

time: 174 us -> 181 us (1.040)
  blocking collectives: 33.5 us -> 38.5 us
  waiting for transfers between devices: 41.1 us -> 43 us
    all_to_all x1, blocking collectives: 19.3 us -> 23.6 us  [forward(): return lax.all_to_all(parts, axis, 0, 0, axis_index_groups=[served(axis)])]
    all_to_all x3, waiting for transfers between devices: 17.9 us -> 19.9 us  [backward(): return lax.all_to_all(copies, axis, 0, 0, axis_index_groups=order)]
where the time goes in v7:
time: 181 us; the launch traced here: 180 us
  starting transfers between devices  61.9 us (34%)
  waiting for transfers between devices  43 us (24%)
  blocking collectives  38.5 us (21%)
  Pallas kernels  28.5 us (16%)
  local copies, waits for them, and re-layouts  6.84 us (4%)
    all_to_all x3, starting transfers between devices, backward(): return lax.all_to_all(copies, axis, 0, 0, axis_index_groups=order)  34.4 us
    all_to_all x1, blocking collectives, forward(): return lax.all_to_all(parts, axis, 0, 0, axis_index_groups=[served(axis)])  23.6 us
    all_to_all x3, waiting for transfers between devices, backward(): return lax.all_to_all(copies, axis, 0, 0, axis_index_groups=order)  19.9 us
    pallas_call x2, Pallas kernels, tile_of(): pl.pallas_call(functools.partial(tile_kernel, half, shared), in_specs=[wh...  19.3 us
    ppermute x7, waiting for transfers between devices, hop(): return lax.ppermute(held, ('z_lo', 'z_hi'), pairs)  17.5 us
    all_to_all x1, blocking collectives, backward(): return lax.all_to_all(copies, axis, 0, 0, axis_index_groups=order)  14.9 us
    ppermute x7, starting transfers between devices, hop(): return lax.ppermute(held, ('z_lo', 'z_hi'), pairs)  11.1 us
    ppermute x7, starting transfers between devices, from_other(): return lax.ppermute(value, 'core', swap)  9.54 us
  transfers between devices with their start and end apart: 18, of which 10 were waited for; matrix products, arithmetic and copies ran while one was open for 0% of the time, Pallas kernels for 6%

profile of v7, /device:TPU:1, one launch (start us, length us, event | category | flops | bytes accessed | tf_op | source)
XLA Modules:
  0.0 180.3 jit_solution(10159861681134674408)
XLA Ops:
  0.6 2.6 %shard_map.60 = f32[16,32,1280]{2,1,0:T(8,128)} custom-call(s32[1]{0:T(128)} %bitcast.1.core_ref, f32[32,512]{1,0:T(8,128)} %weight_ref.1, f32[32,768]{1,0:T(8,128)} %centre_ref.1), custom_call_target="tpu_custom_call" | custom-call | bytes 2621440 | tf_op jit(solution)/shard_map/pallas_call | solution.py:371
  3.3 10.5 %all-to-all-start = ((f32[16,32,1280]{2,1,0:T(8,128)}), f32[16,32,1280]{2,1,0:T(8,128)}, u32[]{:S(2)}, u32[]{:S(2)}) async-start(f32[16,32,1280]{2,1,0:T(8,128)} %shard_map.60), calls=%async_computation | async-start | bytes 5242880 | tf_op jit(solution)/shard_map/all_to_all | solution.py:416
  13.8 1.7 collective-permute-start.3
  15.5 4.0 %collective-permute-start = (f32[64,768]{1,0:T(8,128)S(1)}, f32[64,768]{1,0:T(8,128)S(1)}, u32[]{:S(2)}, u32[]{:S(2)}) collective-permute-start(f32[64,768]{1,0:T(8,128)S(1)} %constant_dynamic-update-slice_fusion.refs_0_), channel_id=1, source_target_pairs={{0,50},{16,0},{32,16},{48,32},{2,48},{18,2},{34,18},{50,34},{1,51}... | collective-permute-start | bytes 589832 | tf_op jit(solution)/shard_map/ppermute | solution.py:432
  19.5 4.3 %collective-permute-done.3.refs_7_ = f32[64,768]{1,0:T(8,128)S(1)} collective-permute-done((f32[64,768]{1,0:T(8,128)S(1)}, f32[64,768]{1,0:T(8,128)S(1)}, u32[]{:S(2)}, u32[]{:S(2)}) %collective-permute-start.3) | collective-permute-done | bytes 196640 | tf_op jit(solution)/shard_map/ppermute | solution.py:432
  23.8 2.7 %collective-permute-start.1 = (f32[64,768]{1,0:T(8,128)S(1)}, f32[64,768]{1,0:T(8,128)S(1)}, u32[]{:S(2)}, u32[]{:S(2)}) collective-permute-start(f32[64,768]{1,0:T(8,128)S(1)} %collective-permute-done.refs_1_), channel_id=1, source_target_pairs={{0,50},{16,0},{32,16},{48,32},{2,48},{18,2},{34,18},{50,34},{1,51}... | collective-permute-start | bytes 589832 | tf_op jit(solution)/shard_map/ppermute | solution.py:432
  26.5 3.6 %collective-permute-done.4.refs_6_ = f32[64,768]{1,0:T(8,128)S(1)} collective-permute-done((f32[64,768]{1,0:T(8,128)S(1)}, f32[64,768]{1,0:T(8,128)S(1)}, u32[]{:S(2)}, u32[]{:S(2)}) %collective-permute-start.4) | collective-permute-done | bytes 196640 | tf_op jit(solution)/shard_map/ppermute | solution.py:432
  30.1 2.7 %collective-permute-start.2 = (f32[64,768]{1,0:T(8,128)S(1)}, f32[64,768]{1,0:T(8,128)S(1)}, u32[]{:S(2)}, u32[]{:S(2)}) collective-permute-start(f32[64,768]{1,0:T(8,128)S(1)} %collective-permute-done.1.refs_2_), channel_id=1, source_target_pairs={{0,50},{16,0},{32,16},{48,32},{2,48},{18,2},{34,18},{50,34},{1,51}... | collective-permute-start | bytes 589832 | tf_op jit(solution)/shard_map/ppermute | solution.py:432
  32.8 3.5 %collective-permute-done.5.refs_5_ = f32[64,768]{1,0:T(8,128)S(1)} collective-permute-done((f32[64,768]{1,0:T(8,128)S(1)}, f32[64,768]{1,0:T(8,128)S(1)}, u32[]{:S(2)}, u32[]{:S(2)}) %collective-permute-start.5) | collective-permute-done | bytes 196640 | tf_op jit(solution)/shard_map/ppermute | solution.py:432
  36.2 6.1 %collective-permute-done.6.refs_4_ = f32[64,768]{1,0:T(8,128)S(1)} collective-permute-done((f32[64,768]{1,0:T(8,128)S(1)}, f32[64,768]{1,0:T(8,128)S(1)}, u32[]{:S(2)}, u32[]{:S(2)}) %collective-permute-start.6) | collective-permute-done | bytes 196640 | tf_op jit(solution)/shard_map/ppermute | solution.py:432
  42.5 3.8 %collective-permute-start.7 = (f32[256,768]{1,0:T(8,128)S(1)}, f32[256,768]{1,0:T(8,128)S(1)}, u32[]{:S(2)}, u32[]{:S(2)}) collective-permute-start(f32[256,768]{1,0:T(8,128)S(1)} %get-tuple-element.13.own_ref), channel_id=1, source_target_pairs={{0,1},{1,0},{2,3},{3,2},{4,5},{5,4},{6,7},{7,6},{8,9},{9,8},{10,11... | collective-permute-start | bytes 2359304 | tf_op jit(solution)/shard_map/ppermute | solution.py:444
  46.3 1.9 %collective-permute-done.7.other_ref = f32[256,768]{1,0:T(8,128)S(1)} collective-permute-done((f32[256,768]{1,0:T(8,128)S(1)}, f32[256,768]{1,0:T(8,128)S(1)}, u32[]{:S(2)}, u32[]{:S(2)}) %collective-permute-start.7) | collective-permute-done | bytes 786464 | tf_op jit(solution)/shard_map/ppermute | solution.py:444
  49.2 10.3 %shard_map.61 = (f32[512,512]{1,0:T(8,128)}, f32[512,256]{1,0:T(8,128)}, f32[512,256]{1,0:T(8,128)}) custom-call(f32[256,768]{1,0:T(8,128)} %copy-done.8, f32[256,768]{1,0:T(8,128)} %copy-done.13, f32[16,32,1280]{2,1,0:T(8,128)} %all-to-all-done.packed_ref), custom_call_target="tpu_custom_call" | custom-call | flops 2415919104 | bytes 6291456 | tf_op jit(solution)/shard_map/pallas_call | solution.py:162
  63.8 6.9 %all-to-all-start.1 = ((f32[8,64,256]{2,1,0:T(8,128)}), f32[8,64,256]{2,1,0:T(8,128)S(1)}, u32[]{:S(2)}, u32[]{:S(2)}) async-start(f32[8,64,256]{2,1,0:T(8,128)} %shard_map.62), calls=%async_computation.1 | async-start | bytes 1048576 | tf_op jit(solution)/shard_map/all_to_all | solution.py:484
  72.4 9.0 %shard_map.64.own_ref = f32[512,512]{1,0:T(8,128)} custom-call(f32[256,768]{1,0:T(8,128)} %copy-done.7, f32[256,768]{1,0:T(8,128)} %copy-done.12, f32[16,32,1280]{2,1,0:T(8,128)} %all-to-all-done.packed_ref), custom_call_target="tpu_custom_call" | custom-call | flops 2415919104 | bytes 6291456 | tf_op jit(solution)/shard_map/pallas_call | solution.py:162
  84.1 9.0 %all-to-all-start.2 = ((f32[8,64,256]{2,1,0:T(8,128)}), f32[8,64,256]{2,1,0:T(8,128)S(1)}, u32[]{:S(2)}, u32[]{:S(2)}) async-start(f32[8,64,256]{2,1,0:T(8,128)} %shard_map.63), calls=%async_computation.2 | async-start | bytes 1048576 | tf_op jit(solution)/shard_map/all_to_all | solution.py:416
  95.4 8.2 %all-to-all-done.2.residual_ref = f32[8,64,256]{2,1,0:T(8,128)S(1)} async-done(((f32[8,64,256]{2,1,0:T(8,128)}), f32[8,64,256]{2,1,0:T(8,128)S(1)}, u32[]{:S(2)}, u32[]{:S(2)}) %all-to-all-start.2) | async-done | bytes 524320 | tf_op jit(solution)/shard_map/all_to_all | solution.py:416
  104.9 2.3 %shard_map.66 = f32[16,72,256]{2,1,0:T(8,128)S(1)} custom-call(s32[1]{0:T(128)} %bitcast.place_ref, f32[512,512]{1,0:T(8,128)S(1)} %copy-done.1, f32[512,512]{1,0:T(8,128)} %collective-permute-done.12.other_ref, f32[8,64,256]{2,1,0:T(8,128)S(1)} %all-to-all-done.2.residual_ref, f32[8,256]{1,0:T(8,128)S(1)} %get-tuple-element.20.sums_ref), custom_call_target="tpu_custom_call" | custom-call | flops 805306368 | bytes 4194304 | tf_op jit(solution)/shard_map/pallas_call | solution.py:271
  107.2 23.6 %all_to_all.30.parts_ref = f32[16,72,256]{2,1,0:T(8,128)S(1)} all-to-all(f32[16,72,256]{2,1,0:T(8,128)S(1)} %shard_map.66), channel_id=1, replica_groups={{0,68,136,204,64,132,200,12,128,196,8,76,192,4,72,140},{1,69,137,205,65..., dimensions={0} | all-to-all | bytes 2359296 | tf_op jit(solution)/shard_map/all_to_all | solution.py:411
  130.9 14.9 %all_to_all.31.grad_ref = f32[16,64,256]{2,1,0:T(8,128)S(1)} all-to-all(f32[16,64,256]{2,1,0:T(8,128)S(1)} %get-tuple-element.21), channel_id=1, replica_groups={{140,72,4,192,76,8,196,128,12,200,132,64,204,136,68,0},{141,73,5,193,77..., dimensions={0} | all-to-all | bytes 2097152 | tf_op jit(solution)/shard_map/all_to_all | solution.py:416
  145.8 1.8 %shard_map.68 = f32[8,72,256]{2,1,0:T(8,128)} custom-call(s32[1]{0:T(128)} %bitcast.place_ref, bf16[512,1024]{1,0:T(8,128)(2,1)S(1)} %copy-done.3, bf16[512,1024]{1,0:T(8,128)(2,1)S(1)} %copy-done.5, f32[16,64,256]{2,1,0:T(8,128)S(1)} %all_to_all.31.grad_ref, f32[8,256]{1,0:T(8,128)S(1)} %get-tuple-element.22.largest_ref), custom_call_target="tpu_custom_call" | custom-call | flops 805306368 | bytes 4194304 | tf_op jit(solution)/shard_map/pallas_call | solution.py:320
  147.6 14.9 %all-to-all-start.5 = ((f32[8,72,256]{2,1,0:T(8,128)}), f32[8,72,256]{2,1,0:T(8,128)S(1)}, u32[]{:S(2)}, u32[]{:S(2)}) async-start(f32[8,72,256]{2,1,0:T(8,128)} %shard_map.68), calls=%async_computation.5 | async-start | bytes 1179648 | tf_op jit(solution)/shard_map/all_to_all | solution.py:416
  163.3 11.6 %all-to-all-done.5.refs_0_ = f32[8,72,256]{2,1,0:T(8,128)S(1)} async-done(((f32[8,72,256]{2,1,0:T(8,128)}), f32[8,72,256]{2,1,0:T(8,128)S(1)}, u32[]{:S(2)}, u32[]{:S(2)}) %all-to-all-start.5) | async-done | bytes 589856 | tf_op jit(solution)/shard_map/all_to_all | solution.py:416
  175.1 3.6 %collective-permute-start.13 = (f32[64,256]{1,0:T(8,128)S(1)}, f32[64,256]{1,0:T(8,128)S(1)}, u32[]{:S(2)}, u32[]{:S(2)}) collective-permute-start(f32[64,256]{1,0:T(8,128)S(1)} %pad_maximum_fusion.3), channel_id=1, source_target_pairs={{0,1},{1,0},{2,3},{3,2},{4,5},{5,4},{6,7},{7,6},{8,9},{9,8},{10,11... | collective-permute-start | bytes 196616 | tf_op jit(solution)/shard_map/ppermute | solution.py:444
  (62 shorter events, 15.9 us)
Async XLA Ops:
  3.2 10.5 %copy-start.9 = (f32[32,768]{1,0:T(8,128)S(1)}, f32[32,768]{1,0:T(8,128)}, u32[]{:S(2)}) copy-start(f32[32,768]{1,0:T(8,128)} %centre_ref.1) | copy-start | bytes 294916
  3.3 45.0 %all-to-all-start = ((f32[16,32,1280]{2,1,0:T(8,128)}), f32[16,32,1280]{2,1,0:T(8,128)}, u32[]{:S(2)}, u32[]{:S(2)}) async-start(f32[16,32,1280]{2,1,0:T(8,128)} %shard_map.60), calls=%async_computation | async-start | bytes 5242880 | tf_op jit(solution)/shard_map/all_to_all | solution.py:416
  13.8 10.1 %collective-permute-start.3 = (f32[64,768]{1,0:T(8,128)S(1)}, f32[64,768]{1,0:T(8,128)S(1)}, u32[]{:S(2)}, u32[]{:S(2)}) collective-permute-start(f32[64,768]{1,0:T(8,128)S(1)} %constant_dynamic-update-slice_fusion.refs_0_), channel_id=1, source_target_pairs={{0,16},{16,32},{32,48},{48,2},{2,18},{18,34},{34,50},{50,0},{1,17}... | collective-permute-start | bytes 589832 | tf_op jit(solution)/shard_map/ppermute | solution.py:432
  15.5 8.4 %collective-permute-start = (f32[64,768]{1,0:T(8,128)S(1)}, f32[64,768]{1,0:T(8,128)S(1)}, u32[]{:S(2)}, u32[]{:S(2)}) collective-permute-start(f32[64,768]{1,0:T(8,128)S(1)} %constant_dynamic-update-slice_fusion.refs_0_), channel_id=1, source_target_pairs={{0,50},{16,0},{32,16},{48,32},{2,48},{18,2},{34,18},{50,34},{1,51}... | collective-permute-start | bytes 589832 | tf_op jit(solution)/shard_map/ppermute | solution.py:432
  23.8 6.3 %collective-permute-start.4 = (f32[64,768]{1,0:T(8,128)S(1)}, f32[64,768]{1,0:T(8,128)S(1)}, u32[]{:S(2)}, u32[]{:S(2)}) collective-permute-start(f32[64,768]{1,0:T(8,128)S(1)} %collective-permute-done.3.refs_7_), channel_id=1, source_target_pairs={{0,16},{16,32},{32,48},{48,2},{2,18},{18,34},{34,50},{50,0},{1,17}... | collective-permute-start | bytes 589832 | tf_op jit(solution)/shard_map/ppermute | solution.py:432
  23.8 6.3 %collective-permute-start.1 = (f32[64,768]{1,0:T(8,128)S(1)}, f32[64,768]{1,0:T(8,128)S(1)}, u32[]{:S(2)}, u32[]{:S(2)}) collective-permute-start(f32[64,768]{1,0:T(8,128)S(1)} %collective-permute-done.refs_1_), channel_id=1, source_target_pairs={{0,50},{16,0},{32,16},{48,32},{2,48},{18,2},{34,18},{50,34},{1,51}... | collective-permute-start | bytes 589832 | tf_op jit(solution)/shard_map/ppermute | solution.py:432
  30.1 6.1 %collective-permute-start.5 = (f32[64,768]{1,0:T(8,128)S(1)}, f32[64,768]{1,0:T(8,128)S(1)}, u32[]{:S(2)}, u32[]{:S(2)}) collective-permute-start(f32[64,768]{1,0:T(8,128)S(1)} %collective-permute-done.4.refs_6_), channel_id=1, source_target_pairs={{0,16},{16,32},{32,48},{48,2},{2,18},{18,34},{34,50},{50,0},{1,17}... | collective-permute-start | bytes 589832 | tf_op jit(solution)/shard_map/ppermute | solution.py:432
  30.1 6.1 %collective-permute-start.2 = (f32[64,768]{1,0:T(8,128)S(1)}, f32[64,768]{1,0:T(8,128)S(1)}, u32[]{:S(2)}, u32[]{:S(2)}) collective-permute-start(f32[64,768]{1,0:T(8,128)S(1)} %collective-permute-done.1.refs_2_), channel_id=1, source_target_pairs={{0,50},{16,0},{32,16},{48,32},{2,48},{18,2},{34,18},{50,34},{1,51}... | collective-permute-start | bytes 589832 | tf_op jit(solution)/shard_map/ppermute | solution.py:432
  36.2 6.1 %collective-permute-start.6 = (f32[64,768]{1,0:T(8,128)S(1)}, f32[64,768]{1,0:T(8,128)S(1)}, u32[]{:S(2)}, u32[]{:S(2)}) collective-permute-start(f32[64,768]{1,0:T(8,128)S(1)} %collective-permute-done.5.refs_5_), channel_id=1, source_target_pairs={{0,16},{16,32},{32,48},{48,2},{2,18},{18,34},{34,50},{50,0},{1,17}... | collective-permute-start | bytes 589832 | tf_op jit(solution)/shard_map/ppermute | solution.py:432
  42.5 17.7 %copy-start.7 = (f32[256,768]{1,0:T(8,128)}, f32[256,768]{1,0:T(8,128)S(1)}, u32[]{:S(2)}) copy-start(f32[256,768]{1,0:T(8,128)S(1)} %get-tuple-element.16.own_ref) | copy-start | bytes 2359300
  42.5 5.8 %collective-permute-start.7 = (f32[256,768]{1,0:T(8,128)S(1)}, f32[256,768]{1,0:T(8,128)S(1)}, u32[]{:S(2)}, u32[]{:S(2)}) collective-permute-start(f32[256,768]{1,0:T(8,128)S(1)} %get-tuple-element.13.own_ref), channel_id=1, source_target_pairs={{0,1},{1,0},{2,3},{3,2},{4,5},{5,4},{6,7},{7,6},{8,9},{9,8},{10,11... | collective-permute-start | bytes 2359304 | tf_op jit(solution)/shard_map/ppermute | solution.py:444
  49.2 21.6 %copy-start.11 = (f32[32,512]{1,0:T(8,128)S(1)}, f32[32,512]{1,0:T(8,128)}, u32[]{:S(2)}) copy-start(f32[32,512]{1,0:T(8,128)} %param.6) | copy-start | bytes 196612
  59.5 2.4 %collective-permute-start.8 = (f32[512,256]{1,0:T(8,128)}, f32[512,256]{1,0:T(8,128)S(1)}, u32[]{:S(2)}, u32[]{:S(2)}) collective-permute-start(f32[512,256]{1,0:T(8,128)} %get-tuple-element.15), channel_id=1, source_target_pairs={{0,1},{1,0},{2,3},{3,2},{4,5},{5,4},{6,7},{7,6},{8,9},{9,8},{10,11... | collective-permute-start | bytes 1572872 | tf_op jit(solution)/shard_map/ppermute | solution.py:444
  60.2 11.3 %collective-permute-start.10 = (f32[256,768]{1,0:T(8,128)S(1)}, f32[256,768]{1,0:T(8,128)S(1)}, u32[]{:S(2)}, u32[]{:S(2)}) collective-permute-start(f32[256,768]{1,0:T(8,128)S(1)} %get-tuple-element.16.own_ref), channel_id=1, source_target_pairs={{0,1},{1,0},{2,3},{3,2},{4,5},{5,4},{6,7},{7,6},{8,9},{9,8},{10,11... | collective-permute-start | bytes 2359304 | tf_op jit(solution)/shard_map/ppermute | solution.py:444
  63.8 19.4 %all-to-all-start.1 = ((f32[8,64,256]{2,1,0:T(8,128)}), f32[8,64,256]{2,1,0:T(8,128)S(1)}, u32[]{:S(2)}, u32[]{:S(2)}) async-start(f32[8,64,256]{2,1,0:T(8,128)} %shard_map.62), calls=%async_computation.1 | async-start | bytes 1048576 | tf_op jit(solution)/shard_map/all_to_all | solution.py:484
  70.7 11.2 %collective-permute-start.9 = (f32[32,256]{1,0:T(8,128)S(1)}, f32[32,256]{1,0:T(8,128)S(1)}, u32[]{:S(2)}, u32[]{:S(2)}) collective-permute-start(f32[32,256]{1,0:T(8,128)S(1)} %get-tuple-element.33), channel_id=1, source_target_pairs={{0,1},{1,0},{2,3},{3,2},{4,5},{5,4},{6,7},{7,6},{8,9},{9,8},{10,11... | collective-permute-start | bytes 98312 | tf_op jit(solution)/shard_map/ppermute | solution.py:444
  81.4 11.7 %copy-start = (f32[512,512]{1,0:T(8,128)S(1)}, f32[512,512]{1,0:T(8,128)}, u32[]{:S(2)}) copy-start(f32[512,512]{1,0:T(8,128)} %shard_map.64.own_ref) | copy-start | bytes 3145732
  81.4 11.7 %collective-permute-start.11 = (f32[512,512]{1,0:T(8,128)}, f32[512,512]{1,0:T(8,128)S(1)}, u32[]{:S(2)}, u32[]{:S(2)}) collective-permute-start(f32[512,512]{1,0:T(8,128)} %shard_map.64.own_ref), channel_id=1, source_target_pairs={{0,1},{1,0},{2,3},{3,2},{4,5},{5,4},{6,7},{7,6},{8,9},{9,8},{10,11... | collective-permute-start | bytes 3145736 | tf_op jit(solution)/shard_map/ppermute | solution.py:444
  81.5 14.0 %collective-permute-start.12 = (f32[512,512]{1,0:T(8,128)}, f32[512,512]{1,0:T(8,128)}, u32[]{:S(2)}, u32[]{:S(2)}) collective-permute-start(f32[512,512]{1,0:T(8,128)} %get-tuple-element.19.own_ref), channel_id=1, source_target_pairs={{0,1},{1,0},{2,3},{3,2},{4,5},{5,4},{6,7},{7,6},{8,9},{9,8},{10,11... | collective-permute-start | bytes 3145736 | tf_op jit(solution)/shard_map/ppermute | solution.py:444
  84.1 19.6 %all-to-all-start.2 = ((f32[8,64,256]{2,1,0:T(8,128)}), f32[8,64,256]{2,1,0:T(8,128)S(1)}, u32[]{:S(2)}, u32[]{:S(2)}) async-start(f32[8,64,256]{2,1,0:T(8,128)} %shard_map.63), calls=%async_computation.2 | async-start | bytes 1048576 | tf_op jit(solution)/shard_map/all_to_all | solution.py:416
  107.2 38.6 %copy-start.3 = (bf16[512,1024]{1,0:T(8,128)(2,1)S(1)}, bf16[512,1024]{1,0:T(8,128)(2,1)}, u32[]{:S(2)}) copy-start(bf16[512,1024]{1,0:T(8,128)(2,1)} %copy-done.2) | copy-start | bytes 3145732
  107.2 38.6 %copy-start.5 = (bf16[512,1024]{1,0:T(8,128)(2,1)S(1)}, bf16[512,1024]{1,0:T(8,128)(2,1)}, u32[]{:S(2)}) copy-start(bf16[512,1024]{1,0:T(8,128)(2,1)} %copy-done.4) | copy-start | bytes 3145732
  147.6 27.3 %all-to-all-start.5 = ((f32[8,72,256]{2,1,0:T(8,128)}), f32[8,72,256]{2,1,0:T(8,128)S(1)}, u32[]{:S(2)}, u32[]{:S(2)}) async-start(f32[8,72,256]{2,1,0:T(8,128)} %shard_map.68), calls=%async_computation.5 | async-start | bytes 1179648 | tf_op jit(solution)/shard_map/all_to_all | solution.py:416
  175.1 4.5 %collective-permute-start.13 = (f32[64,256]{1,0:T(8,128)S(1)}, f32[64,256]{1,0:T(8,128)S(1)}, u32[]{:S(2)}, u32[]{:S(2)}) collective-permute-start(f32[64,256]{1,0:T(8,128)S(1)} %pad_maximum_fusion.3), channel_id=1, source_target_pairs={{0,1},{1,0},{2,3},{3,2},{4,5},{5,4},{6,7},{7,6},{8,9},{9,8},{10,11... | collective-permute-start | bytes 196616 | tf_op jit(solution)/shard_map/ppermute | solution.py:444
  (8 other events, 22.3 us)
